TPU v7x, 256 devices: a whole 4x4x8 slice. The times are simulated.
256 devices in a mesh: ta: 4 (over x), ha: 8 (over z), wa: 8 (over y, core).
Axes of the slice: x: 4, y: 4, z: 8, core: 2. Of those that a mesh axis runs over, the one named last changes fastest.
Arguments:
- latents: float32 [8, 32, 32, 384], P('ta', 'ha', 'wa'), may hold values from -6 to 6
- first_gain: float32 [384], replicated, may hold values from 0.1 to 1.9
- first_kernel: float32 [384, 3, 3, 3, 384], P('wa'), may hold values from -0.0625 to 0.0625
- first_bias: float32 [384], replicated, may hold values from -3 to 3
- second_gain: float32 [384], replicated, may hold values from 0.1 to 1.9
- second_kernel: float32 [384, 3, 3, 3, 384], P('wa'), may hold values from -0.0625 to 0.0625
- second_bias: float32 [384], replicated, may hold values from -3 to 3
- attn_gain: float32 [384], replicated, may hold values from 0.1 to 1.9
- w_query: float32 [384, 384], replicated, may hold values from -2 to 2, as said below
- w_key: float32 [384, 384], replicated, may hold values from -2 to 2, as said below
- w_value: float32 [384, 384], replicated, may hold values from -0.3125 to 0.3125
- w_out: float32 [384, 384], replicated, may hold values from -0.3125 to 0.3125
- out_bias: float32 [384], replicated, may hold values from -3 to 3
Outputs:
- decoded: float32 [8, 32, 32, 384], P('ta', 'ha', 'wa')
Inputs may be any that keep to these rules, and one draw needn't show every extreme that they name: `w_query`: a dense matrix. `w_key`: a dense matrix.
All inputs are finite; a program needn't handle non-finite values.
Results may differ from a plain program's by a relative error of at most 0.00017.
Values sent between devices are 32-bit elements; how exact they have to be, the bound alone decides.
No kernel may reach another device: no remote copies, remote signals or barrier semaphores. Data moves between devices by JAX's collectives and lax.ppermute only.
A program may use at most 64 MiB of HBM per device.

v0:
```python
import math

import jax
import jax.numpy as jnp
from jax import lax
from jax.sharding import PartitionSpec as P


def from_behind(shard, axis, by):
    peers = lax.axis_size(axis)
    pairs = [(i, i + by) for i in range(peers) if 0 <= i + by < peers]
    return lax.ppermute(shard, axis, pairs)


def padded_2(cells, sides, width):
    for axis, dim in sides:
        count = lax.axis_size(axis)
        ends = count - 1
        head = lax.slice_in_dim(cells, 0, width, axis=dim)
        tail = lax.slice_in_dim(cells, cells.shape[dim] - width, cells.shape[dim], axis=dim)
        cells = jnp.concatenate(
            [
                lax.ppermute(tail, axis, [(i, (i + 1) % count) for i in range(ends)]),
                cells,
                lax.ppermute(head, axis, [((i + 1) % count, i) for i in range(ends)]),
            ],
            axis=dim,
        )
    return cells


def channel_norm(values, gain):
    return values * lax.rsqrt(jnp.mean(values * values, axis=-1, keepdims=True) + 1e-06) * gain


def causal_conv(activated, kernel, bias):
    frames = activated.shape[0]
    channels = activated.shape[3]
    out_count = kernel.shape[0]
    widened = lax.all_gather(activated, "wa", axis=2, tiled=True)
    earlier = from_behind(widened, "ta", 1)
    extended = jnp.concatenate([earlier, widened], axis=0)
    padded = padded_2(extended, (("ha", 1),), 1)
    padded = jnp.pad(padded, ((0, 0), (0, 0), (1, 1), (0, 0)))
    heights = activated.shape[1]
    widths = padded.shape[2] - 2
    row_count = frames * heights * widths
    summed = jnp.zeros((row_count, out_count), jnp.float32)
    for time_tap in range(3):
        patches = jnp.concatenate(
            [
                padded[
                    time_tap : time_tap + frames,
                    row_tap : row_tap + heights,
                    col_tap : col_tap + widths,
                ].reshape(row_count, channels)
                for row_tap in range(3)
                for col_tap in range(3)
            ],
            axis=1,
        )
        tap_kernel = kernel[:, time_tap].reshape(out_count, 9 * channels)
        summed = summed + lax.dot_general(
            patches,
            tap_kernel,
            (((1,), (1,)), ((), ())),
            precision=lax.Precision.HIGHEST,
            preferred_element_type=jnp.float32,
        )
    strip = summed.reshape(frames, heights, widths, out_count)
    owned = lax.all_to_all(strip, "wa", split_axis=2, concat_axis=3, tiled=True)
    return owned + bias


def absorb_keys(carry, queries, key_piece, value_piece, scale):
    top, denom, accum = carry
    scores = jnp.einsum("fqc,fkc->fqk", queries, key_piece, precision=lax.Precision.HIGHEST) * scale
    new_top = jnp.maximum(top, jnp.max(scores, axis=-1))
    weights = jnp.exp(scores - new_top[..., None])
    denom = jnp.sum(weights, axis=-1)
    accum = jnp.einsum("fqk,fkc->fqc", weights, value_piece, precision=lax.Precision.HIGHEST)
    return (new_top, denom, accum)


def per_device(
    latents,
    first_gain,
    first_kernel,
    first_bias,
    second_gain,
    second_kernel,
    second_bias,
    attn_gain,
    w_query,
    w_key,
    w_value,
    w_out,
    out_bias,
):
    inner = causal_conv(jax.nn.silu(channel_norm(latents, first_gain)), first_kernel, first_bias)
    blocked = latents + causal_conv(
        jax.nn.silu(channel_norm(inner, second_gain)), second_kernel, second_bias
    )
    frames, heights, widths, channels = blocked.shape
    cell_count = heights * widths
    normed_rows = channel_norm(blocked, attn_gain).reshape(frames * cell_count, channels)
    queries = jnp.dot(
        normed_rows, w_query, precision=lax.Precision.HIGHEST, preferred_element_type=jnp.float32
    ).reshape(frames, cell_count, channels)
    scale = 1.0 / math.sqrt(channels)
    start_state = (
        jnp.full((frames, cell_count), -1e30, jnp.float32),
        jnp.zeros((frames, cell_count), jnp.float32),
        jnp.zeros((frames, cell_count, channels), jnp.float32),
    )
    keys = jnp.dot(
        normed_rows, w_key, precision=lax.Precision.HIGHEST, preferred_element_type=jnp.float32
    ).reshape(frames, cell_count, channels)
    values = jnp.dot(
        normed_rows, w_value, precision=lax.Precision.HIGHEST, preferred_element_type=jnp.float32
    ).reshape(frames, cell_count, channels)
    top, denom, accum = absorb_keys(
        start_state,
        queries,
        lax.all_gather(keys, ("ha", "wa"), axis=1, tiled=True),
        lax.all_gather(values, ("ha", "wa"), axis=1, tiled=True),
        scale,
    )
    mixed = accum / denom[..., None]
    projected = (
        jnp.dot(
            mixed.reshape(frames * cell_count, channels),
            w_out,
            precision=lax.Precision.HIGHEST,
            preferred_element_type=jnp.float32,
        )
        + out_bias
    )
    return blocked + projected.reshape(frames, heights, widths, channels)


def solution(mesh):
    in_specs = (
        P("ta", "ha", "wa", None),
        P(),
        P("wa", None, None, None, None),
        P(),
        P(),
        P("wa", None, None, None, None),
        P(),
        P(),
        P(),
        P(),
        P(),
        P(),
        P(),
    )
    out_specs = P("ta", "ha", "wa", None)
    return jax.shard_map(
        per_device, mesh=mesh, in_specs=in_specs, out_specs=out_specs, check_vma=False
    )
```

profile of v0, /device:TPU:1, one launch (start us, length us, event | category | flops | bytes accessed | tf_op | source)
XLA Modules:
  0.0 315.1 jit_solution(18345777338632848029)
XLA Ops:
  6.5 1.0 multiply_reduce_fusion.2
  7.6 0.9 divide_multiply_fusion.1
  8.5 16.1 %all_gather.12 = f32[2,4,32,384]{3,1,0,2:T(4,128)S(1)} all-gather(f32[2,4,4,384]{3,1,0,2:T(4,128)S(1)} %copy.50), channel_id=1, replica_groups=mesh['ta'=4,'ha'=8,'wa'=8] {'wa'}, dimensions={2}, use_global_device_ids=true | all-gather | bytes 442368 | tf_op jit(solution)/shard_map/all_gather | solution.py:40
  24.7 1.9 collective-permute-start
  26.6 8.3 %collective-permute-done = f32[2,4,32,384]{3,2,1,0:T(8,128)S(1)} collective-permute-done((f32[2,4,32,384]{3,2,1,0:T(8,128)S(1)}, f32[2,4,32,384]{3,2,1,0:T(8,128)S(1)}, u32[]{:S(2)}, u32[]{:S(2)}) %collective-permute-start) | collective-permute-done | bytes 393248 | tf_op jit(solution)/shard_map/ppermute | solution.py:12
  35.0 0.8 fusion.22
  35.8 3.5 %collective-permute-start.1 = (f32[4,1,32,384]{3,2,1,0:T(8,128)}, f32[4,1,32,384]{3,2,1,0:T(8,128)S(1)}, u32[]{:S(2)}, u32[]{:S(2)}) collective-permute-start(f32[4,1,32,384]{3,2,1,0:T(8,128)} %get-tuple-element.71), channel_id=1, source_target_pairs={{0,8},{8,16},{16,24},{24,32},{32,40},{40,48},{48,56},{1,9},{9,17},... | collective-permute-start | bytes 589832 | tf_op jit(solution)/shard_map/ppermute | solution.py:23
  39.4 1.3 collective-permute-start.2
  40.7 1.2 fusion.18
  42.6 1.4 copy.53
  44.1 1.2 reshape_squeeze.18
  45.3 1.4 copy.56
  46.7 1.2 reshape_squeeze.20
  47.9 1.1 select_maximum_fusion.2
  49.0 0.8 fusion.20
  50.0 1.4 pad_maximum_fusion.2
  52.2 3.1 fusion.24
  55.4 3.1 convolution_add_fusion.4
  58.6 3.1 convolution_add_fusion.3
  61.9 0.8 reshape.280
  62.7 5.0 %all-to-all-start = ((f32[8,1,1536]{2,1,0:T(1,128)}), f32[8,1,1536]{2,1,0:T(1,128)S(1)}, u32[]{:S(2)}, u32[]{:S(2)}) async-start(f32[8,1,1536]{2,1,0:T(1,128)} %reshape.280), calls=%async_computation | async-start | bytes 98304 | tf_op jit(solution)/shard_map/all_to_all | solution.py:71
  67.8 4.7 %all-to-all-done = f32[8,1,1536]{2,1,0:T(1,128)S(1)} async-done(((f32[8,1,1536]{2,1,0:T(1,128)}), f32[8,1,1536]{2,1,0:T(1,128)S(1)}, u32[]{:S(2)}, u32[]{:S(2)}) %all-to-all-start) | async-done | bytes 49184 | tf_op jit(solution)/shard_map/all_to_all | solution.py:71
  73.0 0.8 reduce.1
  74.4 13.6 %all_gather.13 = f32[2,4,32,384]{3,1,0,2:T(4,128)S(1)} all-gather(f32[2,4,4,384]{3,1,0,2:T(4,128)S(1)} %copy.61), channel_id=1, replica_groups=mesh['ta'=4,'ha'=8,'wa'=8] {'wa'}, dimensions={2}, use_global_device_ids=true | all-gather | bytes 442368 | tf_op jit(solution)/shard_map/all_gather | solution.py:40
  88.1 4.1 %collective-permute-start.3 = (f32[2,4,32,384]{3,2,1,0:T(8,128)S(1)}, f32[2,4,32,384]{3,2,1,0:T(8,128)S(1)}, u32[]{:S(2)}, u32[]{:S(2)}) collective-permute-start(f32[2,4,32,384]{3,2,1,0:T(8,128)S(1)} %copy.62), channel_id=1, source_target_pairs={{0,64},{64,128},{128,192},{1,65},{65,129},{129,193},{2,66},{66,130... | collective-permute-start | bytes 1179656 | tf_op jit(solution)/shard_map/ppermute | solution.py:12
  92.2 8.3 %collective-permute-done.3 = f32[2,4,32,384]{3,2,1,0:T(8,128)S(1)} collective-permute-done((f32[2,4,32,384]{3,2,1,0:T(8,128)S(1)}, f32[2,4,32,384]{3,2,1,0:T(8,128)S(1)}, u32[]{:S(2)}, u32[]{:S(2)}) %collective-permute-start.3) | collective-permute-done | bytes 393248 | tf_op jit(solution)/shard_map/ppermute | solution.py:12
  100.6 0.8 fusion.21
  101.4 4.3 %collective-permute-start.4 = (f32[4,1,32,384]{3,2,1,0:T(8,128)}, f32[4,1,32,384]{3,2,1,0:T(8,128)S(1)}, u32[]{:S(2)}, u32[]{:S(2)}) collective-permute-start(f32[4,1,32,384]{3,2,1,0:T(8,128)} %get-tuple-element.65), channel_id=1, source_target_pairs={{0,8},{8,16},{16,24},{24,32},{32,40},{40,48},{48,56},{1,9},{9,17},... | collective-permute-start | bytes 589832 | tf_op jit(solution)/shard_map/ppermute | solution.py:23
  105.7 1.3 collective-permute-start.5
  107.0 2.7 fusion.17
  110.4 1.4 copy.64
  111.9 1.2 reshape_squeeze.21
  113.1 1.4 copy.67
  114.5 1.2 reshape_squeeze.23
  115.8 1.1 select_maximum_fusion
  116.8 0.8 fusion.19
  117.8 1.4 pad_maximum_fusion
  120.1 3.1 fusion.25
  123.2 3.1 convolution_add_fusion.2
  126.4 3.1 convolution_add_fusion.1
  130.0 8.6 %all_to_all.36 = f32[8,1,1536]{2,1,0:T(1,128)S(1)} all-to-all(f32[8,1,1536]{2,1,0:T(1,128)S(1)} %reshape.282), channel_id=1, replica_groups=mesh['ta'=4,'ha'=8,'wa'=8] {'wa'}, dimensions={0} | all-to-all | bytes 98304 | tf_op jit(solution)/shard_map/all_to_all | solution.py:71
  138.6 0.8 reduce.2
  139.9 1.0 fusion.3
  141.1 1.0 fusion.1
  142.6 82.5 %all-gather.3.cloned.1.call-done = f32[2,1024,384]{2,1,0:T(8,128)} async-done(((f32[2,16,384]{2,1,0:T(8,128)}), f32[2,1024,384]{2,1,0:T(8,128)}) %all-gather.3.cloned.1.call-update) | async-done | bytes 3145744 | tf_op jit(solution)/shard_map/all_gather | solution.py:125
  225.1 4.6 %fusion.23 = (f32[2,16]{1,0:T(2,128)S(1)}, f32[2,16,1024]{2,1,0:T(8,128)S(1)}) fusion(f32[2,16,384]{2,1,0:T(8,128)S(1)} %fusion.5, f32[2,1024,384]{2,1,0:T(8,128)} %all-gather.3.cloned.1.call-done), kind=kOutput, calls=%fused_computation.126 | convolution fusion | flops 151060448 | bytes 3326080 | tf_op jit(solution)/shard_map/fqc,fkc->fqk/dot_general | solution.py:77
  229.9 73.7 %all-gather.5.cloned.1.call-done = f32[2,1024,384]{2,1,0:T(8,128)} async-done(((f32[2,16,384]{2,1,0:T(8,128)}), f32[2,1024,384]{2,1,0:T(8,128)}) %all-gather.5.cloned.1.call-update) | async-done | bytes 3145744 | tf_op jit(solution)/shard_map/all_gather | solution.py:126
  303.6 3.5 %convolution_divide_fusion = f32[2,16,384]{2,1,0:T(8,128)S(1)} fusion(f32[2,1024,384]{2,1,0:T(8,128)} %all-gather.5.cloned.1.call-done, f32[2,16,1024]{2,1,0:T(8,128)S(1)} %get-tuple-element.74, f32[2,16]{1,0:T(2,128)S(1)} %broadcast_maximum_fusion, f32[2,16]{1,0:T(2,128)S(1)} %fusion.15), kind=kOutput, calls=%fused_computation.17 | convolution fusion | flops 151040000 | bytes 3326208 | tf_op jit(solution)/shard_map/fqk,fkc->fqc/dot_general | solution.py:81
  (141 shorter events, 7.4 us)
Async XLA Ops:
  6.5 133.4 %copy-start = (f32[384,384]{1,0:T(8,128)S(1)}, f32[384,384]{1,0:T(8,128)}, u32[]{:S(2)}) copy-start(f32[384,384]{1,0:T(8,128)} %param.22) | copy-start | bytes 1769476
  6.5 34.1 %copy-start.5 = (f32[48,3,3,3,384]{4,0,3,2,1:T(8,128)S(1)}, f32[48,3,3,3,384]{4,0,3,2,1:T(8,128)}, u32[]{:S(2)}) copy-start(f32[48,3,3,3,384]{4,0,3,2,1:T(8,128)} %param.15) | copy-start | bytes 5971972
  24.7 14.7 %copy-start.6 = (f32[2,4,32,384]{3,2,1,0:T(8,128)}, f32[2,4,32,384]{3,2,1,0:T(8,128)S(1)}, u32[]{:S(2)}) copy-start(f32[2,4,32,384]{3,2,1,0:T(8,128)S(1)} %copy.51) | copy-start | bytes 1179652
  24.7 10.3 %collective-permute-start = (f32[2,4,32,384]{3,2,1,0:T(8,128)S(1)}, f32[2,4,32,384]{3,2,1,0:T(8,128)S(1)}, u32[]{:S(2)}, u32[]{:S(2)}) collective-permute-start(f32[2,4,32,384]{3,2,1,0:T(8,128)S(1)} %copy.51), channel_id=1, source_target_pairs={{0,64},{64,128},{128,192},{1,65},{65,129},{129,193},{2,66},{66,130... | collective-permute-start | bytes 1179656 | tf_op jit(solution)/shard_map/ppermute | solution.py:12
  35.8 12.1 %collective-permute-start.1 = (f32[4,1,32,384]{3,2,1,0:T(8,128)}, f32[4,1,32,384]{3,2,1,0:T(8,128)S(1)}, u32[]{:S(2)}, u32[]{:S(2)}) collective-permute-start(f32[4,1,32,384]{3,2,1,0:T(8,128)} %get-tuple-element.71), channel_id=1, source_target_pairs={{0,8},{8,16},{16,24},{24,32},{32,40},{40,48},{48,56},{1,9},{9,17},... | collective-permute-start | bytes 589832 | tf_op jit(solution)/shard_map/ppermute | solution.py:23
  39.4 8.6 %collective-permute-start.2 = (f32[4,1,32,384]{3,2,1,0:T(8,128)}, f32[4,1,32,384]{3,2,1,0:T(8,128)}, u32[]{:S(2)}, u32[]{:S(2)}) collective-permute-start(f32[4,1,32,384]{3,2,1,0:T(8,128)} %get-tuple-element.72), channel_id=1, source_target_pairs={{8,0},{16,8},{24,16},{32,24},{40,32},{48,40},{56,48},{9,1},{17,9},... | collective-permute-start | bytes 589832 | tf_op jit(solution)/shard_map/ppermute | solution.py:25
  50.0 1.5 copy-start.7
  52.1 3.3 %copy-start.1 = (f32[48,3456]{1,0:T(8,128)S(1)}, f32[48,3456]{1,0:T(8,128)}, u32[]{:S(2)}) copy-start(f32[48,3456]{1,0:T(8,128)} %reshape_squeeze.18) | copy-start | bytes 1990660
  52.2 6.3 %copy-start.3 = (f32[48,3456]{1,0:T(8,128)S(1)}, f32[48,3456]{1,0:T(8,128)}, u32[]{:S(2)}) copy-start(f32[48,3456]{1,0:T(8,128)} %reshape_squeeze.20) | copy-start | bytes 1990660
  58.6 9.2 %copy-start.14 = (f32[384]{0:T(512)S(1)}, f32[384]{0:T(512)}, u32[]{:S(2)}) copy-start(f32[384]{0:T(512)} %param.16) | copy-start | bytes 4612
  58.6 15.7 %copy-start.18 = (f32[384]{0:T(512)S(1)}, f32[384]{0:T(512)}, u32[]{:S(2)}) copy-start(f32[384]{0:T(512)} %param.17) | copy-start | bytes 4612
  62.7 9.8 %all-to-all-start = ((f32[8,1,1536]{2,1,0:T(1,128)}), f32[8,1,1536]{2,1,0:T(1,128)S(1)}, u32[]{:S(2)}, u32[]{:S(2)}) async-start(f32[8,1,1536]{2,1,0:T(1,128)} %reshape.280), calls=%async_computation | async-start | bytes 98304 | tf_op jit(solution)/shard_map/all_to_all | solution.py:71
  67.7 157.4 %all-gather.3.cloned.1.call-start = ((), (), s32[]{:S(2)}) async-start(), calls=%async_computation.2 | async-start | bytes 3194880 | tf_op jit(solution)/shard_map/all_gather | solution.py:125
  88.1 17.6 %copy-start.8 = (f32[2,4,32,384]{3,2,1,0:T(8,128)}, f32[2,4,32,384]{3,2,1,0:T(8,128)S(1)}, u32[]{:S(2)}) copy-start(f32[2,4,32,384]{3,2,1,0:T(8,128)S(1)} %copy.62) | copy-start | bytes 1179652
  88.1 12.5 %collective-permute-start.3 = (f32[2,4,32,384]{3,2,1,0:T(8,128)S(1)}, f32[2,4,32,384]{3,2,1,0:T(8,128)S(1)}, u32[]{:S(2)}, u32[]{:S(2)}) collective-permute-start(f32[2,4,32,384]{3,2,1,0:T(8,128)S(1)} %copy.62), channel_id=1, source_target_pairs={{0,64},{64,128},{128,192},{1,65},{65,129},{129,193},{2,66},{66,130... | collective-permute-start | bytes 1179656 | tf_op jit(solution)/shard_map/ppermute | solution.py:12
  101.4 14.3 %collective-permute-start.4 = (f32[4,1,32,384]{3,2,1,0:T(8,128)}, f32[4,1,32,384]{3,2,1,0:T(8,128)S(1)}, u32[]{:S(2)}, u32[]{:S(2)}) collective-permute-start(f32[4,1,32,384]{3,2,1,0:T(8,128)} %get-tuple-element.65), channel_id=1, source_target_pairs={{0,8},{8,16},{16,24},{24,32},{32,40},{40,48},{48,56},{1,9},{9,17},... | collective-permute-start | bytes 589832 | tf_op jit(solution)/shard_map/ppermute | solution.py:23
  105.7 10.0 %collective-permute-start.5 = (f32[4,1,32,384]{3,2,1,0:T(8,128)}, f32[4,1,32,384]{3,2,1,0:T(8,128)}, u32[]{:S(2)}, u32[]{:S(2)}) collective-permute-start(f32[4,1,32,384]{3,2,1,0:T(8,128)} %get-tuple-element.66), channel_id=1, source_target_pairs={{8,0},{16,8},{24,16},{32,24},{40,32},{48,40},{56,48},{9,1},{17,9},... | collective-permute-start | bytes 589832 | tf_op jit(solution)/shard_map/ppermute | solution.py:25
  117.8 1.5 copy-start.9
  119.9 3.3 %copy-start.2 = (f32[48,3456]{1,0:T(8,128)S(1)}, f32[48,3456]{1,0:T(8,128)}, u32[]{:S(2)}) copy-start(f32[48,3456]{1,0:T(8,128)} %reshape_squeeze.21) | copy-start | bytes 1990660
  120.1 6.3 %copy-start.4 = (f32[48,3456]{1,0:T(8,128)S(1)}, f32[48,3456]{1,0:T(8,128)}, u32[]{:S(2)}) copy-start(f32[48,3456]{1,0:T(8,128)} %reshape_squeeze.23) | copy-start | bytes 1990660
  126.4 13.3 %copy-start.13 = (f32[2,4,4,384]{3,2,1,0:T(4,128)S(1)}, f32[2,4,4,384]{3,2,1,0:T(4,128)}, u32[]{:S(2)}) copy-start(f32[2,4,4,384]{3,2,1,0:T(4,128)} %param.13) | copy-start | bytes 147460
  126.4 13.3 %copy-start.15 = (f32[384]{0:T(512)S(1)}, f32[384]{0:T(512)}, u32[]{:S(2)}) copy-start(f32[384]{0:T(512)} %param.19) | copy-start | bytes 4612
  126.4 13.4 %copy-start.17 = (f32[384]{0:T(512)S(1)}, f32[384]{0:T(512)}, u32[]{:S(2)}) copy-start(f32[384]{0:T(512)} %param.20) | copy-start | bytes 4612
  126.4 14.6 %copy-start.10 = (f32[384,384]{1,0:T(8,128)S(1)}, f32[384,384]{1,0:T(8,128)}, u32[]{:S(2)}) copy-start(f32[384,384]{1,0:T(8,128)} %param.23) | copy-start | bytes 1769476
  126.4 15.7 %copy-start.11 = (f32[384,384]{1,0:T(8,128)S(1)}, f32[384,384]{1,0:T(8,128)}, u32[]{:S(2)}) copy-start(f32[384,384]{1,0:T(8,128)} %param.21) | copy-start | bytes 1769476
  141.0 162.6 %all-gather.5.cloned.1.call-start = ((), (), s32[]{:S(2)}) async-start(), calls=%async_computation.3 | async-start | bytes 3194880 | tf_op jit(solution)/shard_map/all_gather | solution.py:126
  142.6 164.6 %copy-start.12 = (f32[384,384]{1,0:T(8,128)S(1)}, f32[384,384]{1,0:T(8,128)}, u32[]{:S(2)}) copy-start(f32[384,384]{1,0:T(8,128)} %param.24) | copy-start | bytes 1769476
  142.6 164.5 %copy-start.16 = (f32[384]{0:T(512)S(1)}, f32[384]{0:T(512)}, u32[]{:S(2)}) copy-start(f32[384]{0:T(512)} %param.25) | copy-start | bytes 4612
Sparse Core Ops, SparseCore 0:
  141.1 83.9 all-gather.2
  227.8 75.7 all-gather.4
where the time goes:
time: 316 us; the launch traced here: 315 us
  waiting for transfers between devices  178 us (56%)
  blocking collectives  38.2 us (12%)
  matrix products  29.9 us (9%)
  local copies, waits for them, and re-layouts  23.7 us (8%)
  starting transfers between devices  21.5 us (7%)
  between operations  14.5 us (5%)
  other arithmetic  9.67 us (3%)
    all_gather x1, waiting for transfers between devices, per_device(): lax.all_gather(keys, ('ha', 'wa'), axis=1, tiled=True)  82.5 us
    all_gather x1, waiting for transfers between devices, per_device(): lax.all_gather(values, ('ha', 'wa'), axis=1, tiled=True)  73.7 us
    all_gather x2, blocking collectives, causal_conv(): widened = lax.all_gather(activated, 'wa', axis=2, tiled=True)  29.6 us
    dot_general x6, matrix products, causal_conv(): lax.dot_general(patches, tap_kernel, (((1,), (1,)), ((), ())), precision=...  18.8 us
    ppermute x2, waiting for transfers between devices, from_behind(): return lax.ppermute(shard, axis, pairs)  16.6 us
    slice x8, local copies, waits for them, and re-layouts, causal_conv(): tap_kernel = kernel[:, time_tap].reshape(out_count, 9 * channels)  10.4 us
    all_to_all x1, blocking collectives, causal_conv(): owned = lax.all_to_all(strip, 'wa', split_axis=2, concat_axis=3, tiled=True)  8.61 us
    ppermute x2, starting transfers between devices, padded_2(): lax.ppermute(tail, axis, [(i, (i + 1) % count) for i in range(ends)])  7.81 us
  transfers between devices with their start and end apart: 9, of which 5 were waited for; matrix products, arithmetic and copies ran while one was open for 7% of the time, Pallas kernels for 0%

commit v1 on v0

v1 whole, which is shorter than its diff:
```python
import math

import jax
import jax.numpy as jnp
from jax import lax
from jax.experimental import pallas as pl
from jax.experimental.pallas import tpu as pltpu
from jax.sharding import PartitionSpec as P

C = 384
OUT = 48
CHIPS = 4
F32 = jnp.float32
BF16 = jnp.bfloat16


Z_OFFSETS = ((0, 4), (1, -3), (2, -2), (-1, 3))


def sibling(x):
    return lax.ppermute(x, "wa", [(i, i ^ 1) for i in range(2 * CHIPS)])


def across_chips(xs):
    n = 2 * CHIPS
    return [
        lax.ppermute(x, "wa", [(i, (i + 2 * k) % n) for i in range(n)])
        for k, x in enumerate(xs, 1)
    ]


def gathered(x):
    same = [x] + across_chips([x] * (CHIPS - 1))
    return same + [sibling(piece) for piece in same]


def shifted(x, axis, by):
    n = lax.axis_size(axis)
    return lax.ppermute(x, axis, [(i, (i + by) % n) for i in range(n)])


def call(kernel, outs, *args, scratch=(), scalars=None):
    in_specs = [pl.BlockSpec(memory_space=pltpu.VMEM)] * len(args)
    if scalars is not None:
        in_specs = [pl.BlockSpec(memory_space=pltpu.SMEM)] + in_specs
        args = (scalars,) + args
    return pl.pallas_call(
        kernel,
        out_shape=[jax.ShapeDtypeStruct(s, F32) for s in outs],
        in_specs=in_specs,
        out_specs=[pl.BlockSpec(memory_space=pltpu.VMEM)] * len(outs),
        scratch_shapes=list(scratch),
        compiler_params=pltpu.CompilerParams(vmem_limit_bytes=40 * 1024 * 1024),
    )(*args)


def halves(x):
    high = x.astype(BF16)
    return high, (x - high.astype(F32)).astype(BF16)


def product(wh, wl, xh, xl):
    def dot(a, b):
        return lax.dot_general(a, b, (((1,), (0,)), ((), ())), preferred_element_type=F32)

    return dot(wh, xh) + (dot(wh, xl) + dot(wl, xh))


def activated(x, gain):
    mean = jnp.mean(x * x, axis=0, keepdims=True)
    v = x * lax.rsqrt(mean + 1e-6) * gain
    return v / (1.0 + jnp.exp(-v))


def lane_of(shape):
    return lax.broadcasted_iota(jnp.int32, shape, 1)


def columns_joined(left, mid, right):
    col = lane_of(mid.shape) & 31
    return (
        mid
        + jnp.where(col != 0, pltpu.roll(left, 1, 1), 0.0)
        + jnp.where(col != 31, pltpu.roll(right, 127, 1), 0.0)
    )


def frames_joined(first, second, third):
    late = (lane_of(second.shape) & 127) >= 64
    moved = pltpu.roll(second, 64, 1)
    own = third + jnp.where(late, moved, 0.0)
    following = first + jnp.where(late, 0.0, moved)
    return own, following


def first_conv_kernel(at, *refs):
    pieces, (gain, wh, wl) = refs[:8], refs[8:11]
    own_out, next_out, strip_out, cells, prod = refs[11:]
    y, c = at[2], at[3]
    for k in range(CHIPS):
        mine, other = pieces[k][...], pieces[CHIPS + k][...]
        both = jnp.concatenate(
            [jnp.where(c == 0, mine, other), jnp.where(c == 0, other, mine)], axis=2
        )
        chip = lax.rem(y - k + CHIPS, CHIPS)
        for f in range(2):
            for r in range(4):
                base = (r // 2) * 128 + f * 64 + (r % 2) * 32
                cells[pl.ds(pl.multiple_of(base + 8 * chip, 8), 8), :] = both[f, r]
    strip = cells[...].T
    strip_out[...] = strip
    xh, xl = halves(activated(strip, gain[...]))
    prod[...] = product(wh[...], wl[...], xh, xl)
    second_row = (lane_of((OUT, 128)) & 63) >= 32
    tiles = []
    for a in range(3):
        rows = []
        for i in range(3):
            t = 9 * a + 3 * i
            rows.append(
                [
                    columns_joined(
                        *(
                            prod[(t + j) * OUT : (t + j + 1) * OUT, p * 128 : p * 128 + 128]
                            for j in range(3)
                        )
                    )
                    for p in range(2)
                ]
            )
        down, level, up = rows
        upper = [jnp.where(second_row, pltpu.roll(v, 32, 1), 0.0) for v in level]
        lower = [jnp.where(second_row, 0.0, pltpu.roll(v, 96, 1)) for v in level]
        tiles.append(
            [
                up[0] + upper[0],
                up[1] + down[0] + lower[0] + upper[1],
                down[1] + lower[1],
            ]
        )
    for n in range(3):
        own, following = frames_joined(tiles[0][n], tiles[1][n], tiles[2][n])
        own_out[:, n * 128 : n * 128 + 128] = own
        next_out[:, n * 128 : n * 128 + 128] = following


def add_frames_kernel(at, own, arrived, top, mid, bottom):
    total = own[...] + jnp.where(at[0] > 0, arrived[...], 0.0)
    top[...] = total[:, :128]
    mid[...] = total[:, 128:256]
    bottom[...] = total[:, 256:]


def add_rows_kernel(at, top, mid, bottom, above, below, bias, out):
    h, w = at[1], 2 * at[2] + at[3]
    b = bias[pl.ds(pl.multiple_of(w * OUT, 8), OUT), :]
    second = (lane_of((OUT, 128)) & 63) >= 32
    whole_top = top[...] + above[...] + b
    whole_bottom = bottom[...] + below[...] + b
    edge_top = jnp.where(second, top[...] + b, 0.0)
    edge_bottom = jnp.where(second, 0.0, bottom[...] + b)
    out[:, :128] = jnp.where(h > 0, whole_top, edge_top)
    out[:, 128:256] = mid[...] + b
    out[:, 256:] = jnp.where(h < 7, whole_bottom, edge_bottom)


def put_channels(at, pieces, scratch):
    y, c = at[2], at[3]
    for k in range(CHIPS):
        chip = lax.rem(y - k + CHIPS, CHIPS)
        for core, piece in ((c, pieces[k]), (1 - c, pieces[CHIPS + k])):
            start = pl.multiple_of((2 * chip + core) * OUT, 8)
            scratch[pl.ds(start, OUT), :] = piece[...]


def second_conv_kernel(at, *refs):
    pieces, (gain, wh, wl) = refs[:8], refs[8:11]
    own_out, next_out, inner, prod = refs[11:]
    put_channels(at, pieces, inner)
    act = activated(inner[...], gain[...])
    top, mid, bottom = act[:, :128], act[:, 128:256], act[:, 256:]
    second_row = (lane_of((C, 128)) & 63) >= 32
    level = jnp.concatenate(
        [
            jnp.where(second_row, pltpu.roll(mid, 32, 1), pltpu.roll(top, 96, 1)),
            jnp.where(second_row, pltpu.roll(bottom, 32, 1), pltpu.roll(mid, 96, 1)),
        ],
        axis=1,
    )
    stacked = jnp.concatenate([act[:, :256], level, act[:, 128:]], axis=0)
    xh, xl = halves(stacked)
    prod[...] = product(wh[...], wl[...], xh, xl)
    for p in range(2):
        lanes = slice(p * 128, p * 128 + 128)
        joined = [
            columns_joined(
                *(prod[(3 * a + j) * OUT : (3 * a + j + 1) * OUT, lanes] for j in range(3))
            )
            for a in range(3)
        ]
        own, following = frames_joined(*joined)
        own_out[:, lanes] = own
        next_out[:, lanes] = following


def add_last_kernel(at, own, arrived, bias, out):
    w = 2 * at[2] + at[3]
    b = bias[pl.ds(pl.multiple_of(w * OUT, 8), OUT), :]
    out[...] = own[...] + jnp.where(at[0] > 0, arrived[...], 0.0) + b


def norm_kernel(at, *refs):
    pieces, (strip, gain) = refs[:8], refs[8:10]
    blocked_out, normed_out, total = refs[10:]
    put_channels(at, pieces, total)
    whole = total[...] + strip[...]
    early, late = whole[:, :128], whole[:, 128:]
    first = lane_of((C, 128)) < 64
    frame = jnp.where(
        at[3] == 0,
        jnp.where(first, early, pltpu.roll(late, 64, 1)),
        jnp.where(first, pltpu.roll(early, 64, 1), late),
    )
    blocked_out[...] = frame
    mean = jnp.mean(frame * frame, axis=0, keepdims=True)
    normed_out[...] = frame * lax.rsqrt(mean + 1e-6) * gain[...]


def query_kernel(at, blocked, normed, w_score, queries_out, rest_out, cells):
    y = at[2]
    cells[...] = blocked[...].T
    for r in range(4):
        start = pl.multiple_of(32 * r + 8 * y, 8)
        rest_out[8 * r : 8 * r + 8, :] = cells[pl.ds(start, 8), :]
    queries_out[...] = jnp.dot(
        normed[...].T, w_score[...], precision=lax.Precision.HIGHEST, preferred_element_type=F32
    )


def mix_kernel(at, queries, keys_a, keys_b, *refs):
    outs, state = refs[:CHIPS], refs[CHIPS]
    y = at[2]
    q = queries[...]
    scores = [
        jnp.dot(q, k[...], precision=lax.Precision.HIGHEST, preferred_element_type=F32)
        for k in (keys_a, keys_b)
    ]
    top = jnp.max(jnp.maximum(*scores), axis=1, keepdims=True)
    weights = [jnp.exp(s - top) for s in scores]
    denom = jnp.sum(weights[0] + weights[1], axis=1, keepdims=True)
    accum = [
        lax.dot_general(
            p,
            k[...],
            (((1,), (1,)), ((), ())),
            precision=lax.Precision.HIGHEST,
            preferred_element_type=F32,
        )
        for p, k in zip(weights, (keys_a, keys_b))
    ]
    state[:, :C] = accum[0] + accum[1]
    state[:, C:] = jnp.where(lane_of((128, 128)) < 64, top, denom)
    for k in range(CHIPS):
        chip = lax.rem(y + k, CHIPS)
        for r in range(4):
            start = pl.multiple_of(32 * r + 8 * chip, 8)
            outs[k][8 * r : 8 * r + 8, :] = state[pl.ds(start, 8), :]


def project_kernel(at, a, b, c, d, w_mixed, bias, rest, mine_out, other_out):
    parts = [x[...] for x in (a, b, c, d)]
    tops = [x[:, C : C + 1] for x in parts]
    top = jnp.maximum(jnp.maximum(tops[0], tops[1]), jnp.maximum(tops[2], tops[3]))
    factors = [jnp.exp(t - top) for t in tops]
    denom = sum(f * x[:, C + 64 : C + 65] for f, x in zip(factors, parts))
    mixed = sum(f * x[:, :C] for f, x in zip(factors, parts)) / denom
    done = rest[...] + (
        jnp.dot(mixed, w_mixed[...], precision=lax.Precision.HIGHEST, preferred_element_type=F32)
        + bias[...]
    )
    done = done.reshape(4, 8, C)
    left, right = done[:, :4], done[:, 4:]
    mine_out[...] = jnp.where(at[3] == 0, left, right)
    other_out[...] = jnp.where(at[3] == 0, right, left)


def split_weights(kernel, order):
    w = jnp.transpose(kernel, order)
    w = w.reshape(-1, math.prod(w.shape[order.index(0) + 1 :]))
    high = lax.reduce_precision(w, 8, 7)
    return high.astype(BF16), (w - high).astype(BF16)


def per_device(
    latents,
    first_gain,
    first_kernel,
    first_bias,
    second_gain,
    second_kernel,
    second_bias,
    attn_gain,
    w_query,
    w_key,
    w_value,
    w_out,
    out_bias,
):
    wa = lax.axis_index("wa")
    at = jnp.stack([lax.axis_index("ta"), lax.axis_index("ha"), wa // 2, wa % 2]).astype(jnp.int32)
    column = lambda v: v.reshape(C, 1)

    first_w = split_weights(first_kernel, (1, 2, 3, 0, 4))
    second_w = split_weights(second_kernel, (1, 3, 0, 2, 4))
    w_score = lax.dot_general(
        w_query,
        w_key,
        (((1,), (1,)), ((), ())),
        precision=lax.Precision.HIGHEST,
        preferred_element_type=F32,
    ) * (1.0 / math.sqrt(C))
    w_mixed = jnp.dot(w_value, w_out, precision=lax.Precision.HIGHEST, preferred_element_type=F32)

    own, following, strip = call(
        first_conv_kernel,
        [(OUT, 384), (OUT, 384), (C, 256)],
        *gathered(latents),
        column(first_gain),
        *first_w,
        scratch=[pltpu.VMEM((256, C), F32), pltpu.VMEM((27 * OUT, 256), F32)],
        scalars=at,
    )
    top, mid, bottom = call(
        add_frames_kernel, [(OUT, 128)] * 3, own, shifted(following, "ta", 1), scalars=at
    )
    above, below = shifted(bottom, "ha", 1), shifted(top, "ha", -1)
    (inner,) = call(
        add_rows_kernel,
        [(OUT, 384)],
        top,
        mid,
        bottom,
        above,
        below,
        column(first_bias),
        scalars=at,
    )
    own, following = call(
        second_conv_kernel,
        [(OUT, 256), (OUT, 256)],
        *gathered(inner),
        column(second_gain),
        *second_w,
        scratch=[pltpu.VMEM((C, 384), F32), pltpu.VMEM((9 * OUT, 256), F32)],
        scalars=at,
    )
    (change,) = call(
        add_last_kernel,
        [(OUT, 256)],
        own,
        shifted(following, "ta", 1),
        column(second_bias),
        scalars=at,
    )
    blocked, normed = call(
        norm_kernel,
        [(C, 128), (C, 128)],
        *gathered(change),
        strip,
        column(attn_gain),
        scratch=[pltpu.VMEM((C, 256), F32)],
        scalars=at,
    )
    keys = []
    for n in range(2):
        pairs = []
        for h in range(8):
            for w in range(8):
                offset = Z_OFFSETS[w // 2][n] * (1 if w % 2 == 0 else -1)
                pairs.append((((h + offset) % 8) * 8 + w, h * 8 + w))
        keys.append(lax.ppermute(normed, ("ha", "wa"), pairs))
    queries, rest = call(
        query_kernel,
        [(128, C), (32, C)],
        blocked,
        normed,
        w_score,
        scratch=[pltpu.VMEM((128, C), F32)],
        scalars=at,
    )
    states = call(
        mix_kernel,
        [(32, C + 128)] * CHIPS,
        queries,
        *keys,
        scratch=[pltpu.VMEM((128, C + 128), F32)],
        scalars=at,
    )
    mine, other = call(
        project_kernel,
        [(4, 4, C), (4, 4, C)],
        states[0],
        *across_chips(states[1:]),
        w_mixed,
        out_bias.reshape(1, C),
        rest,
        scalars=at,
    )
    other = sibling(other)
    even = wa % 2 == 0
    return jnp.stack([jnp.where(even, mine, other), jnp.where(even, other, mine)])


def solution(mesh):
    in_specs = (
        P("ta", "ha", "wa", None),
        P(),
        P("wa", None, None, None, None),
        P(),
        P(),
        P("wa", None, None, None, None),
        P(),
        P(),
        P(),
        P(),
        P(),
        P(),
        P(),
    )
    out_specs = P("ta", "ha", "wa", None)
    return jax.shard_map(
        per_device, mesh=mesh, in_specs=in_specs, out_specs=out_specs, check_vma=False
    )
```

time: 316 us -> 84.7 us (0.27)
  the two profiles are of different devices: /device:TPU:1 before, /device:TPU:33 now
where the time goes in v1:
time: 84.7 us; the launch traced here: 84.6 us
  starting transfers between devices  48.9 us (58%)
  waiting for transfers between devices  17.2 us (20%)
  Pallas kernels  10.7 us (13%)
  other arithmetic  2.84 us (3%)
  matrix products  2.54 us (3%)
  local copies, waits for them, and re-layouts  2.15 us (3%)
    ppermute x12, starting transfers between devices, across_chips(): lax.ppermute(x, 'wa', [(i, (i + 2 * k) % n) for i in range(n)])  22.6 us
    ppermute x13, starting transfers between devices, sibling(): return lax.ppermute(x, 'wa', [(i, i ^ 1) for i in range(2 * CHIPS)])  17.1 us
    pallas_call x9, Pallas kernels, call(): pl.pallas_call(kernel, out_shape=[jax.ShapeDtypeStruct(s, F32) for s in o...  10.7 us
    ppermute x4, waiting for transfers between devices, shifted(): return lax.ppermute(x, axis, [(i, (i + by) % n) for i in range(n)])  10.2 us
    ppermute x2, starting transfers between devices, per_device(): keys.append(lax.ppermute(normed, ('ha', 'wa'), pairs))  6.08 us
    ppermute x4, starting transfers between devices, shifted(): return lax.ppermute(x, axis, [(i, (i + by) % n) for i in range(n)])  3.09 us
    ppermute x2, waiting for transfers between devices, per_device(): keys.append(lax.ppermute(normed, ('ha', 'wa'), pairs))  2.49 us
    ppermute x13, waiting for transfers between devices, sibling(): return lax.ppermute(x, 'wa', [(i, i ^ 1) for i in range(2 * CHIPS)])  2.36 us
  transfers between devices with their start and end apart: 31, of which 13 were waited for; matrix products, arithmetic and copies ran while one was open for 8% of the time, Pallas kernels for 1%

profile of v1, /device:TPU:33, one launch (start us, length us, event | category | flops | bytes accessed | tf_op | source)
XLA Modules:
  0.0 84.6 jit_solution(11757120790570755389)
XLA Ops:
  0.0 1.4 %collective-permute-start = (f32[2,4,4,384]{3,2,1,0:T(4,128)}, f32[2,4,4,384]{3,2,1,0:T(4,128)S(1)}, u32[]{:S(2)}, u32[]{:S(2)}) collective-permute-start(f32[2,4,4,384]{3,2,1,0:T(4,128)} %refs_0_.1), channel_id=1, source_target_pairs={{0,2},{1,3},{2,4},{3,5},{4,6},{5,7},{6,0},{7,1},{8,10},{9,11},{10,... | collective-permute-start | bytes 147464 | tf_op jit(solution)/shard_map/ppermute | solution.py:27
  1.4 2.6 %collective-permute-start.1 = (f32[2,4,4,384]{3,2,1,0:T(4,128)}, f32[2,4,4,384]{3,2,1,0:T(4,128)S(1)}, u32[]{:S(2)}, u32[]{:S(2)}) collective-permute-start(f32[2,4,4,384]{3,2,1,0:T(4,128)} %refs_0_.1), channel_id=1, source_target_pairs={{0,4},{1,5},{2,6},{3,7},{4,0},{5,1},{6,2},{7,3},{8,12},{9,13},{10,... | collective-permute-start | bytes 147464 | tf_op jit(solution)/shard_map/ppermute | solution.py:27
  4.0 1.1 %collective-permute-start.2 = (f32[2,4,4,384]{3,2,1,0:T(4,128)}, f32[2,4,4,384]{3,2,1,0:T(4,128)S(1)}, u32[]{:S(2)}, u32[]{:S(2)}) collective-permute-start(f32[2,4,4,384]{3,2,1,0:T(4,128)} %refs_0_.1), channel_id=1, source_target_pairs={{0,6},{1,7},{2,0},{3,1},{4,2},{5,3},{6,4},{7,5},{8,14},{9,15},{10,... | collective-permute-start | bytes 147464 | tf_op jit(solution)/shard_map/ppermute | solution.py:27
  5.1 1.5 %collective-permute-start.3 = (f32[2,4,4,384]{3,2,1,0:T(4,128)}, f32[2,4,4,384]{3,2,1,0:T(4,128)S(1)}, u32[]{:S(2)}, u32[]{:S(2)}) collective-permute-start(f32[2,4,4,384]{3,2,1,0:T(4,128)} %refs_0_.1), channel_id=1, source_target_pairs={{0,1},{1,0},{2,3},{3,2},{4,5},{5,4},{6,7},{7,6},{8,9},{9,8},{10,11... | collective-permute-start | bytes 147464 | tf_op jit(solution)/shard_map/ppermute | solution.py:21
  6.6 1.9 %fusion = (bf16[1296,384]{1,0:T(8,128)(2,1)S(1)}, bf16[1296,384]{1,0:T(8,128)(2,1)S(1)}) fusion(f32[48,3,3,3,384]{4,0,3,2,1:T(8,128)} %param.15), kind=kLoop, calls=%fused_computation.4 | loop fusion | flops 1990656 | bytes 3981312 | tf_op jit(solution)/shard_map/convert_element_type | solution.py:291
  8.6 0.5 collective-permute-start.5
  9.1 0.4 collective-permute-start.6
  10.0 0.4 collective-permute-done.6.refs_7_
  10.4 2.2 %shard_map.127 = (f32[48,384]{1,0:T(8,128)S(1)}, f32[48,384]{1,0:T(8,128)S(1)}, f32[384,256]{1,0:T(8,128)S(1)}) custom-call(s32[4]{0:T(128)S(1)} %pad_add_fusion.at, f32[2,4,4,384]{3,2,1,0:T(4,128)S(1)} %copy-done.1, f32[2,4,4,384]{3,2,1,0:T(4,128)S(1)} %collective-permute-done.refs_1_, f32[2,4,4,384]{3,2,1,0:T(4,128)S(1)} %collective-permute-done.1.refs_2_, ...), custom_call_target="tpu_custom_call" | custom-call | tf_op jit(solution)/shard_map/pallas_call | solution.py:47
  12.7 1.3 %collective-permute-start.7 = (f32[48,384]{1,0:T(8,128)S(1)}, f32[48,384]{1,0:T(8,128)S(1)}, u32[]{:S(2)}, u32[]{:S(2)}) collective-permute-start(f32[48,384]{1,0:T(8,128)S(1)} %get-tuple-element.24), channel_id=1, source_target_pairs={{0,64},{64,128},{128,192},{192,0},{1,65},{65,129},{129,193},{193,1... | collective-permute-start | bytes 221192 | tf_op jit(solution)/shard_map/ppermute | solution.py:39
  14.0 3.2 %collective-permute-done.7.arrived = f32[48,384]{1,0:T(8,128)S(1)} collective-permute-done((f32[48,384]{1,0:T(8,128)S(1)}, f32[48,384]{1,0:T(8,128)S(1)}, u32[]{:S(2)}, u32[]{:S(2)}) %collective-permute-start.7) | collective-permute-done | bytes 73760 | tf_op jit(solution)/shard_map/ppermute | solution.py:39
  17.2 0.6 shard_map.128
  17.7 1.7 %collective-permute-start.8 = (f32[48,128]{1,0:T(8,128)S(1)}, f32[48,128]{1,0:T(8,128)S(1)}, u32[]{:S(2)}, u32[]{:S(2)}) collective-permute-start(f32[48,128]{1,0:T(8,128)S(1)} %get-tuple-element.27.bottom), channel_id=1, source_target_pairs={{0,8},{8,16},{16,24},{24,32},{32,40},{40,48},{48,56},{56,0},{1,9},... | collective-permute-start | bytes 73736 | tf_op jit(solution)/shard_map/ppermute | solution.py:39
  19.5 0.9 %collective-permute-done.8.above = f32[48,128]{1,0:T(8,128)S(1)} collective-permute-done((f32[48,128]{1,0:T(8,128)S(1)}, f32[48,128]{1,0:T(8,128)S(1)}, u32[]{:S(2)}, u32[]{:S(2)}) %collective-permute-start.8) | collective-permute-done | bytes 24608 | tf_op jit(solution)/shard_map/ppermute | solution.py:39
  20.5 2.1 %collective-permute-done.9.below = f32[48,128]{1,0:T(8,128)S(1)} collective-permute-done((f32[48,128]{1,0:T(8,128)S(1)}, f32[48,128]{1,0:T(8,128)S(1)}, u32[]{:S(2)}, u32[]{:S(2)}) %collective-permute-start.9) | collective-permute-done | bytes 24608 | tf_op jit(solution)/shard_map/ppermute | solution.py:39
  22.6 0.6 shard_map.129.refs_0_
  23.2 0.6 collective-permute-start.10
  23.8 2.9 %collective-permute-start.11 = (f32[48,384]{1,0:T(8,128)S(1)}, f32[48,384]{1,0:T(8,128)S(1)}, u32[]{:S(2)}, u32[]{:S(2)}) collective-permute-start(f32[48,384]{1,0:T(8,128)S(1)} %shard_map.129.refs_0_), channel_id=1, source_target_pairs={{0,4},{1,5},{2,6},{3,7},{4,0},{5,1},{6,2},{7,3},{8,12},{9,13},{10,... | collective-permute-start | bytes 221192 | tf_op jit(solution)/shard_map/ppermute | solution.py:27
  26.7 0.4 collective-permute-start.12
  27.2 1.0 %copy.17 = f32[3,3,48,3,384]{4,3,2,1,0:T(4,128)S(1)} copy(f32[3,3,48,3,384]{4,2,1,3,0:T(8,128)S(1)} %bitcast.23) | data formatting | bytes 3981312 | tf_op jit(solution)/shard_map/transpose | solution.py:288
  28.3 3.3 %collective-permute-start.13 = (f32[48,384]{1,0:T(8,128)S(1)}, f32[48,384]{1,0:T(8,128)S(1)}, u32[]{:S(2)}, u32[]{:S(2)}) collective-permute-start(f32[48,384]{1,0:T(8,128)S(1)} %shard_map.129.refs_0_), channel_id=1, source_target_pairs={{0,1},{1,0},{2,3},{3,2},{4,5},{5,4},{6,7},{7,6},{8,9},{9,8},{10,11... | collective-permute-start | bytes 221192 | tf_op jit(solution)/shard_map/ppermute | solution.py:21
  31.8 1.1 %collective-permute-start.15 = (f32[48,384]{1,0:T(8,128)S(1)}, f32[48,384]{1,0:T(8,128)S(1)}, u32[]{:S(2)}, u32[]{:S(2)}) collective-permute-start(f32[48,384]{1,0:T(8,128)S(1)} %collective-permute-done.11.refs_2_), channel_id=1, source_target_pairs={{0,1},{1,0},{2,3},{3,2},{4,5},{5,4},{6,7},{7,6},{8,9},{9,8},{10,11... | collective-permute-start | bytes 221192 | tf_op jit(solution)/shard_map/ppermute | solution.py:21
  32.9 1.2 %collective-permute-start.16 = (f32[48,384]{1,0:T(8,128)S(1)}, f32[48,384]{1,0:T(8,128)S(1)}, u32[]{:S(2)}, u32[]{:S(2)}) collective-permute-start(f32[48,384]{1,0:T(8,128)S(1)} %collective-permute-done.12.refs_3_), channel_id=1, source_target_pairs={{0,1},{1,0},{2,3},{3,2},{4,5},{5,4},{6,7},{7,6},{8,9},{9,8},{10,11... | collective-permute-start | bytes 221192 | tf_op jit(solution)/shard_map/ppermute | solution.py:21
  35.0 1.9 %shard_map.130 = (f32[48,256]{1,0:T(8,128)S(1)}, f32[48,256]{1,0:T(8,128)S(1)}) custom-call(s32[4]{0:T(128)S(1)} %pad_add_fusion.at, f32[48,384]{1,0:T(8,128)S(1)} %shard_map.129.refs_0_, f32[48,384]{1,0:T(8,128)S(1)} %collective-permute-done.10.refs_1_, f32[48,384]{1,0:T(8,128)S(1)} %collective-permute-done.11.refs_2_, ...), custom_call_target="tpu_custom_call" | custom-call | tf_op jit(solution)/shard_map/pallas_call | solution.py:47
  37.2 4.0 %collective-permute-done.17.arrived = f32[48,256]{1,0:T(8,128)S(1)} collective-permute-done((f32[48,256]{1,0:T(8,128)S(1)}, f32[48,256]{1,0:T(8,128)S(1)}, u32[]{:S(2)}, u32[]{:S(2)}) %collective-permute-start.17) | collective-permute-done | bytes 49184 | tf_op jit(solution)/shard_map/ppermute | solution.py:39
  41.2 0.6 shard_map.131.refs_0_
  41.9 2.5 %collective-permute-start.19 = (f32[48,256]{1,0:T(8,128)S(1)}, f32[48,256]{1,0:T(8,128)S(1)}, u32[]{:S(2)}, u32[]{:S(2)}) collective-permute-start(f32[48,256]{1,0:T(8,128)S(1)} %shard_map.131.refs_0_), channel_id=1, source_target_pairs={{0,4},{1,5},{2,6},{3,7},{4,0},{5,1},{6,2},{7,3},{8,12},{9,13},{10,... | collective-permute-start | bytes 147464 | tf_op jit(solution)/shard_map/ppermute | solution.py:27
  44.4 1.1 %collective-permute-start.20 = (f32[48,256]{1,0:T(8,128)S(1)}, f32[48,256]{1,0:T(8,128)S(1)}, u32[]{:S(2)}, u32[]{:S(2)}) collective-permute-start(f32[48,256]{1,0:T(8,128)S(1)} %shard_map.131.refs_0_), channel_id=1, source_target_pairs={{0,6},{1,7},{2,0},{3,1},{4,2},{5,3},{6,4},{7,5},{8,14},{9,15},{10,... | collective-permute-start | bytes 147464 | tf_op jit(solution)/shard_map/ppermute | solution.py:27
  45.5 2.1 %collective-permute-start.21 = (f32[48,256]{1,0:T(8,128)S(1)}, f32[48,256]{1,0:T(8,128)S(1)}, u32[]{:S(2)}, u32[]{:S(2)}) collective-permute-start(f32[48,256]{1,0:T(8,128)S(1)} %shard_map.131.refs_0_), channel_id=1, source_target_pairs={{0,1},{1,0},{2,3},{3,2},{4,5},{5,4},{6,7},{7,6},{8,9},{9,8},{10,11... | collective-permute-start | bytes 147464 | tf_op jit(solution)/shard_map/ppermute | solution.py:21
  47.6 1.5 %collective-permute-start.22 = (f32[48,256]{1,0:T(8,128)S(1)}, f32[48,256]{1,0:T(8,128)S(1)}, u32[]{:S(2)}, u32[]{:S(2)}) collective-permute-start(f32[48,256]{1,0:T(8,128)S(1)} %collective-permute-done.18.refs_1_), channel_id=1, source_target_pairs={{0,1},{1,0},{2,3},{3,2},{4,5},{5,4},{6,7},{7,6},{8,9},{9,8},{10,11... | collective-permute-start | bytes 147464 | tf_op jit(solution)/shard_map/ppermute | solution.py:21
  49.2 1.4 %collective-permute-start.24 = (f32[48,256]{1,0:T(8,128)S(1)}, f32[48,256]{1,0:T(8,128)S(1)}, u32[]{:S(2)}, u32[]{:S(2)}) collective-permute-start(f32[48,256]{1,0:T(8,128)S(1)} %collective-permute-done.20.refs_3_), channel_id=1, source_target_pairs={{0,1},{1,0},{2,3},{3,2},{4,5},{5,4},{6,7},{7,6},{8,9},{9,8},{10,11... | collective-permute-start | bytes 147464 | tf_op jit(solution)/shard_map/ppermute | solution.py:21
  50.7 0.7 collective-permute-done.24.refs_7_
  51.4 0.8 shard_map.132
  52.2 0.7 collective-permute-start.25
  52.9 5.4 %collective-permute-start.26 = (f32[384,128]{1,0:T(8,128)S(1)}, f32[384,128]{1,0:T(8,128)S(1)}, u32[]{:S(2)}, u32[]{:S(2)}) collective-permute-start(f32[384,128]{1,0:T(8,128)S(1)} %get-tuple-element.32.normed), channel_id=1, source_target_pairs={{32,0},{33,1},{42,2},{27,3},{52,4},{21,5},{30,6},{47,7},{40,8},{41... | collective-permute-start | bytes 589832 | tf_op jit(solution)/shard_map/ppermute | solution.py:381
  58.3 1.3 %convolution_multiply_fusion.w_score = f32[384,384]{1,0:T(8,128)S(1)} fusion(f32[384,384]{1,0:T(8,128)S(1)} %copy-done, f32[384,384]{1,0:T(8,128)S(1)} %copy-done.3), kind=kOutput, calls=%fused_computation.6 | convolution fusion | flops 679624704 | bytes 1769472 | tf_op jit(solution)/shard_map/dot_general | solution.py:315
  59.6 1.1 %shard_map.133 = (f32[128,384]{1,0:T(8,128)S(1)}, f32[32,384]{1,0:T(8,128)S(1)}) custom-call(s32[4]{0:T(128)S(1)} %pad_add_fusion.at, f32[384,128]{1,0:T(8,128)S(1)} %get-tuple-element.31.blocked, f32[384,128]{1,0:T(8,128)S(1)} %get-tuple-element.32.normed, f32[384,384]{1,0:T(8,128)S(1)} %convolution_multiply_fusion.w_score), custom_call_target="tpu_custom_call" | custom-call | tf_op jit(solution)/shard_map/pallas_call | solution.py:47
  60.8 2.5 %collective-permute-done.26.keys_b = f32[384,128]{1,0:T(8,128)S(1)} collective-permute-done((f32[384,128]{1,0:T(8,128)S(1)}, f32[384,128]{1,0:T(8,128)S(1)}, u32[]{:S(2)}, u32[]{:S(2)}) %collective-permute-start.26) | collective-permute-done | bytes 196640 | tf_op jit(solution)/shard_map/ppermute | solution.py:381
  63.3 1.7 %shard_map.134 = (f32[32,512]{1,0:T(8,128)S(1)}, f32[32,512]{1,0:T(8,128)S(1)}, f32[32,512]{1,0:T(8,128)S(1)}, f32[32,512]{1,0:T(8,128)S(1)}) custom-call(s32[4]{0:T(128)S(1)} %pad_add_fusion.at, f32[128,384]{1,0:T(8,128)S(1)} %get-tuple-element.33.queries, f32[384,128]{1,0:T(8,128)S(1)} %collective-permute-done.25.keys_a, ...), custom_call_target="tpu_custom_call" | custom-call | tf_op jit(solution)/shard_map/pallas_call | solution.py:47
  65.0 4.2 %collective-permute-start.27 = (f32[32,512]{1,0:T(8,128)S(1)}, f32[32,512]{1,0:T(8,128)S(1)}, u32[]{:S(2)}, u32[]{:S(2)}) collective-permute-start(f32[32,512]{1,0:T(8,128)S(1)} %get-tuple-element.35), channel_id=1, source_target_pairs={{0,2},{1,3},{2,4},{3,5},{4,6},{5,7},{6,0},{7,1},{8,10},{9,11},{10,... | collective-permute-start | bytes 196616 | tf_op jit(solution)/shard_map/ppermute | solution.py:27
  69.2 5.7 %collective-permute-start.28 = (f32[32,512]{1,0:T(8,128)S(1)}, f32[32,512]{1,0:T(8,128)S(1)}, u32[]{:S(2)}, u32[]{:S(2)}) collective-permute-start(f32[32,512]{1,0:T(8,128)S(1)} %get-tuple-element.36), channel_id=1, source_target_pairs={{0,4},{1,5},{2,6},{3,7},{4,0},{5,1},{6,2},{7,3},{8,12},{9,13},{10,... | collective-permute-start | bytes 196616 | tf_op jit(solution)/shard_map/ppermute | solution.py:27
  74.9 1.3 %fusion.2.w_mixed = f32[384,384]{1,0:T(8,128)S(1)} fusion(f32[384,384]{1,0:T(8,128)S(1)} %copy-done.4, f32[384,384]{1,0:T(8,128)S(1)} %copy-done.5), kind=kOutput, calls=%fused_computation.11 | convolution fusion | flops 679477248 | bytes 1769472 | tf_op jit(solution)/shard_map/dot_general | solution.py:322
  76.2 1.0 %collective-permute-done.28.c = f32[32,512]{1,0:T(8,128)S(1)} collective-permute-done((f32[32,512]{1,0:T(8,128)S(1)}, f32[32,512]{1,0:T(8,128)S(1)}, u32[]{:S(2)}, u32[]{:S(2)}) %collective-permute-start.28) | collective-permute-done | bytes 65568 | tf_op jit(solution)/shard_map/ppermute | solution.py:27
  77.3 1.0 %collective-permute-done.29.d = f32[32,512]{1,0:T(8,128)S(1)} collective-permute-done((f32[32,512]{1,0:T(8,128)S(1)}, f32[32,512]{1,0:T(8,128)S(1)}, u32[]{:S(2)}, u32[]{:S(2)}) %collective-permute-start.29) | collective-permute-done | bytes 65568 | tf_op jit(solution)/shard_map/ppermute | solution.py:27
  78.2 1.0 %shard_map.135 = (f32[4,4,384]{2,1,0:T(4,128)S(1)}, f32[4,4,384]{2,1,0:T(4,128)S(1)}) custom-call(s32[4]{0:T(128)S(1)} %pad_add_fusion.at, f32[32,512]{1,0:T(8,128)S(1)} %get-tuple-element.34.a, f32[32,512]{1,0:T(8,128)S(1)} %collective-permute-done.27.b, f32[32,512]{1,0:T(8,128)S(1)} %collective-permute-done.28.c, f32[32,512]{1,0:T(8,128)S(1)} %collective-permute-done.29.d, ...), custom_call_target="tpu_custom_call" | custom-call | tf_op jit(solution)/shard_map/pallas_call | solution.py:47
  79.3 3.8 %collective-permute-start.30 = (f32[4,4,384]{2,1,0:T(4,128)S(1)}, f32[4,4,384]{2,1,0:T(4,128)S(1)}, u32[]{:S(2)}, u32[]{:S(2)}) collective-permute-start(f32[4,4,384]{2,1,0:T(4,128)S(1)} %get-tuple-element.40), channel_id=1, source_target_pairs={{0,1},{1,0},{2,3},{3,2},{4,5},{5,4},{6,7},{7,6},{8,9},{9,8},{10,11... | collective-permute-start | bytes 73736 | tf_op jit(solution)/shard_map/ppermute | solution.py:21
  83.1 0.8 %collective-permute-done.30 = f32[4,4,384]{2,1,0:T(4,128)S(1)} collective-permute-done((f32[4,4,384]{2,1,0:T(4,128)S(1)}, f32[4,4,384]{2,1,0:T(4,128)S(1)}, u32[]{:S(2)}, u32[]{:S(2)}) %collective-permute-start.30) | collective-permute-done | bytes 24608 | tf_op jit(solution)/shard_map/ppermute | solution.py:21
  83.9 0.6 pad_maximum_fusion
  (62 shorter events, 2.2 us)
Async XLA Ops:
  0.0 58.3 %copy-start = (f32[384,384]{1,0:T(8,128)S(1)}, f32[384,384]{1,0:T(8,128)}, u32[]{:S(2)}) copy-start(f32[384,384]{1,0:T(8,128)} %param.21) | copy-start | bytes 1769476
  0.0 10.4 %copy-start.1 = (f32[2,4,4,384]{3,2,1,0:T(4,128)S(1)}, f32[2,4,4,384]{3,2,1,0:T(4,128)}, u32[]{:S(2)}) copy-start(f32[2,4,4,384]{3,2,1,0:T(4,128)} %refs_0_.1) | copy-start | bytes 147460
  0.0 9.6 %copy-start.6 = (f32[384]{0:T(512)S(1)}, f32[384]{0:T(512)}, u32[]{:S(2)}) copy-start(f32[384]{0:T(512)} %param.14) | copy-start | bytes 4612
  0.0 8.5 %collective-permute-start = (f32[2,4,4,384]{3,2,1,0:T(4,128)}, f32[2,4,4,384]{3,2,1,0:T(4,128)S(1)}, u32[]{:S(2)}, u32[]{:S(2)}) collective-permute-start(f32[2,4,4,384]{3,2,1,0:T(4,128)} %refs_0_.1), channel_id=1, source_target_pairs={{0,2},{1,3},{2,4},{3,5},{4,6},{5,7},{6,0},{7,1},{8,10},{9,11},{10,... | collective-permute-start | bytes 147464 | tf_op jit(solution)/shard_map/ppermute | solution.py:27
  1.4 7.2 %collective-permute-start.1 = (f32[2,4,4,384]{3,2,1,0:T(4,128)}, f32[2,4,4,384]{3,2,1,0:T(4,128)S(1)}, u32[]{:S(2)}, u32[]{:S(2)}) collective-permute-start(f32[2,4,4,384]{3,2,1,0:T(4,128)} %refs_0_.1), channel_id=1, source_target_pairs={{0,4},{1,5},{2,6},{3,7},{4,0},{5,1},{6,2},{7,3},{8,12},{9,13},{10,... | collective-permute-start | bytes 147464 | tf_op jit(solution)/shard_map/ppermute | solution.py:27
  4.0 5.1 %collective-permute-start.2 = (f32[2,4,4,384]{3,2,1,0:T(4,128)}, f32[2,4,4,384]{3,2,1,0:T(4,128)S(1)}, u32[]{:S(2)}, u32[]{:S(2)}) collective-permute-start(f32[2,4,4,384]{3,2,1,0:T(4,128)} %refs_0_.1), channel_id=1, source_target_pairs={{0,6},{1,7},{2,0},{3,1},{4,2},{5,3},{6,4},{7,5},{8,14},{9,15},{10,... | collective-permute-start | bytes 147464 | tf_op jit(solution)/shard_map/ppermute | solution.py:27
  5.1 4.7 %collective-permute-start.3 = (f32[2,4,4,384]{3,2,1,0:T(4,128)}, f32[2,4,4,384]{3,2,1,0:T(4,128)S(1)}, u32[]{:S(2)}, u32[]{:S(2)}) collective-permute-start(f32[2,4,4,384]{3,2,1,0:T(4,128)} %refs_0_.1), channel_id=1, source_target_pairs={{0,1},{1,0},{2,3},{3,2},{4,5},{5,4},{6,7},{7,6},{8,9},{9,8},{10,11... | collective-permute-start | bytes 147464 | tf_op jit(solution)/shard_map/ppermute | solution.py:21
  8.4 11.0 %copy-start.7 = (f32[384]{0:T(512)S(1)}, f32[384]{0:T(512)}, u32[]{:S(2)}) copy-start(f32[384]{0:T(512)} %param.16) | copy-start | bytes 4612
  8.5 18.7 %copy-start.2 = (f32[48,3,3,3,384]{4,0,3,2,1:T(8,128)S(1)}, f32[48,3,3,3,384]{4,0,3,2,1:T(8,128)}, u32[]{:S(2)}) copy-start(f32[48,3,3,3,384]{4,0,3,2,1:T(8,128)} %param.18) | copy-start | bytes 5971972
  8.5 1.3 %collective-permute-start.4 = (f32[2,4,4,384]{3,2,1,0:T(4,128)S(1)}, f32[2,4,4,384]{3,2,1,0:T(4,128)S(1)}, u32[]{:S(2)}, u32[]{:S(2)}) collective-permute-start(f32[2,4,4,384]{3,2,1,0:T(4,128)S(1)} %collective-permute-done.refs_1_), channel_id=1, source_target_pairs={{0,1},{1,0},{2,3},{3,2},{4,5},{5,4},{6,7},{7,6},{8,9},{9,8},{10,11... | collective-permute-start | bytes 147464 | tf_op jit(solution)/shard_map/ppermute | solution.py:21
  8.6 1.4 %collective-permute-start.5 = (f32[2,4,4,384]{3,2,1,0:T(4,128)S(1)}, f32[2,4,4,384]{3,2,1,0:T(4,128)S(1)}, u32[]{:S(2)}, u32[]{:S(2)}) collective-permute-start(f32[2,4,4,384]{3,2,1,0:T(4,128)S(1)} %collective-permute-done.1.refs_2_), channel_id=1, source_target_pairs={{0,1},{1,0},{2,3},{3,2},{4,5},{5,4},{6,7},{7,6},{8,9},{9,8},{10,11... | collective-permute-start | bytes 147464 | tf_op jit(solution)/shard_map/ppermute | solution.py:21
  9.1 1.3 %collective-permute-start.6 = (f32[2,4,4,384]{3,2,1,0:T(4,128)S(1)}, f32[2,4,4,384]{3,2,1,0:T(4,128)S(1)}, u32[]{:S(2)}, u32[]{:S(2)}) collective-permute-start(f32[2,4,4,384]{3,2,1,0:T(4,128)S(1)} %collective-permute-done.2.refs_3_), channel_id=1, source_target_pairs={{0,1},{1,0},{2,3},{3,2},{4,5},{5,4},{6,7},{7,6},{8,9},{9,8},{10,11... | collective-permute-start | bytes 147464 | tf_op jit(solution)/shard_map/ppermute | solution.py:21
  12.7 4.5 %collective-permute-start.7 = (f32[48,384]{1,0:T(8,128)S(1)}, f32[48,384]{1,0:T(8,128)S(1)}, u32[]{:S(2)}, u32[]{:S(2)}) collective-permute-start(f32[48,384]{1,0:T(8,128)S(1)} %get-tuple-element.24), channel_id=1, source_target_pairs={{0,64},{64,128},{128,192},{192,0},{1,65},{65,129},{129,193},{193,1... | collective-permute-start | bytes 221192 | tf_op jit(solution)/shard_map/ppermute | solution.py:39
  17.7 2.8 %collective-permute-start.8 = (f32[48,128]{1,0:T(8,128)S(1)}, f32[48,128]{1,0:T(8,128)S(1)}, u32[]{:S(2)}, u32[]{:S(2)}) collective-permute-start(f32[48,128]{1,0:T(8,128)S(1)} %get-tuple-element.27.bottom), channel_id=1, source_target_pairs={{0,8},{8,16},{16,24},{24,32},{32,40},{40,48},{48,56},{56,0},{1,9},... | collective-permute-start | bytes 73736 | tf_op jit(solution)/shard_map/ppermute | solution.py:39
  19.4 3.1 %collective-permute-start.9 = (f32[48,128]{1,0:T(8,128)S(1)}, f32[48,128]{1,0:T(8,128)S(1)}, u32[]{:S(2)}, u32[]{:S(2)}) collective-permute-start(f32[48,128]{1,0:T(8,128)S(1)} %get-tuple-element.25.top), channel_id=1, source_target_pairs={{0,56},{8,0},{16,8},{24,16},{32,24},{40,32},{48,40},{56,48},{1,57}... | collective-permute-start | bytes 73736 | tf_op jit(solution)/shard_map/ppermute | solution.py:39
  23.2 8.5 %collective-permute-start.10 = (f32[48,384]{1,0:T(8,128)S(1)}, f32[48,384]{1,0:T(8,128)S(1)}, u32[]{:S(2)}, u32[]{:S(2)}) collective-permute-start(f32[48,384]{1,0:T(8,128)S(1)} %shard_map.129.refs_0_), channel_id=1, source_target_pairs={{0,2},{1,3},{2,4},{3,5},{4,6},{5,7},{6,0},{7,1},{8,10},{9,11},{10,... | collective-permute-start | bytes 221192 | tf_op jit(solution)/shard_map/ppermute | solution.py:27
  23.8 8.0 %collective-permute-start.11 = (f32[48,384]{1,0:T(8,128)S(1)}, f32[48,384]{1,0:T(8,128)S(1)}, u32[]{:S(2)}, u32[]{:S(2)}) collective-permute-start(f32[48,384]{1,0:T(8,128)S(1)} %shard_map.129.refs_0_), channel_id=1, source_target_pairs={{0,4},{1,5},{2,6},{3,7},{4,0},{5,1},{6,2},{7,3},{8,12},{9,13},{10,... | collective-permute-start | bytes 221192 | tf_op jit(solution)/shard_map/ppermute | solution.py:27
  26.7 6.1 %collective-permute-start.12 = (f32[48,384]{1,0:T(8,128)S(1)}, f32[48,384]{1,0:T(8,128)S(1)}, u32[]{:S(2)}, u32[]{:S(2)}) collective-permute-start(f32[48,384]{1,0:T(8,128)S(1)} %shard_map.129.refs_0_), channel_id=1, source_target_pairs={{0,6},{1,7},{2,0},{3,1},{4,2},{5,3},{6,4},{7,5},{8,14},{9,15},{10,... | collective-permute-start | bytes 221192 | tf_op jit(solution)/shard_map/ppermute | solution.py:27
  28.3 6.6 %collective-permute-start.13 = (f32[48,384]{1,0:T(8,128)S(1)}, f32[48,384]{1,0:T(8,128)S(1)}, u32[]{:S(2)}, u32[]{:S(2)}) collective-permute-start(f32[48,384]{1,0:T(8,128)S(1)} %shard_map.129.refs_0_), channel_id=1, source_target_pairs={{0,1},{1,0},{2,3},{3,2},{4,5},{5,4},{6,7},{7,6},{8,9},{9,8},{10,11... | collective-permute-start | bytes 221192 | tf_op jit(solution)/shard_map/ppermute | solution.py:21
  31.7 3.3 %collective-permute-start.14 = (f32[48,384]{1,0:T(8,128)S(1)}, f32[48,384]{1,0:T(8,128)S(1)}, u32[]{:S(2)}, u32[]{:S(2)}) collective-permute-start(f32[48,384]{1,0:T(8,128)S(1)} %collective-permute-done.10.refs_1_), channel_id=1, source_target_pairs={{0,1},{1,0},{2,3},{3,2},{4,5},{5,4},{6,7},{7,6},{8,9},{9,8},{10,11... | collective-permute-start | bytes 221192 | tf_op jit(solution)/shard_map/ppermute | solution.py:21
  31.8 3.2 %collective-permute-start.15 = (f32[48,384]{1,0:T(8,128)S(1)}, f32[48,384]{1,0:T(8,128)S(1)}, u32[]{:S(2)}, u32[]{:S(2)}) collective-permute-start(f32[48,384]{1,0:T(8,128)S(1)} %collective-permute-done.11.refs_2_), channel_id=1, source_target_pairs={{0,1},{1,0},{2,3},{3,2},{4,5},{5,4},{6,7},{7,6},{8,9},{9,8},{10,11... | collective-permute-start | bytes 221192 | tf_op jit(solution)/shard_map/ppermute | solution.py:21
  32.9 2.1 %collective-permute-start.16 = (f32[48,384]{1,0:T(8,128)S(1)}, f32[48,384]{1,0:T(8,128)S(1)}, u32[]{:S(2)}, u32[]{:S(2)}) collective-permute-start(f32[48,384]{1,0:T(8,128)S(1)} %collective-permute-done.12.refs_3_), channel_id=1, source_target_pairs={{0,1},{1,0},{2,3},{3,2},{4,5},{5,4},{6,7},{7,6},{8,9},{9,8},{10,11... | collective-permute-start | bytes 221192 | tf_op jit(solution)/shard_map/ppermute | solution.py:21
  34.1 0.7 copy-start.8
  34.8 2.3 %copy-start.9 = (f32[384]{0:T(512)S(1)}, f32[384]{0:T(512)}, u32[]{:S(2)}) copy-start(f32[384]{0:T(512)} %param.19) | copy-start | bytes 4612
  34.8 15.8 %copy-start.10 = (f32[384]{0:T(512)S(1)}, f32[384]{0:T(512)}, u32[]{:S(2)}) copy-start(f32[384]{0:T(512)} %param.20) | copy-start | bytes 4612
  35.0 23.3 %copy-start.3 = (f32[384,384]{1,0:T(8,128)S(1)}, f32[384,384]{1,0:T(8,128)}, u32[]{:S(2)}) copy-start(f32[384,384]{1,0:T(8,128)} %param.22) | copy-start | bytes 1769476
  37.0 4.2 %collective-permute-start.17 = (f32[48,256]{1,0:T(8,128)S(1)}, f32[48,256]{1,0:T(8,128)S(1)}, u32[]{:S(2)}, u32[]{:S(2)}) collective-permute-start(f32[48,256]{1,0:T(8,128)S(1)} %get-tuple-element.29), channel_id=1, source_target_pairs={{0,64},{64,128},{128,192},{192,0},{1,65},{65,129},{129,193},{193,1... | collective-permute-start | bytes 147464 | tf_op jit(solution)/shard_map/ppermute | solution.py:39
  41.8 5.8 %collective-permute-start.18 = (f32[48,256]{1,0:T(8,128)S(1)}, f32[48,256]{1,0:T(8,128)S(1)}, u32[]{:S(2)}, u32[]{:S(2)}) collective-permute-start(f32[48,256]{1,0:T(8,128)S(1)} %shard_map.131.refs_0_), channel_id=1, source_target_pairs={{0,2},{1,3},{2,4},{3,5},{4,6},{5,7},{6,0},{7,1},{8,10},{9,11},{10,... | collective-permute-start | bytes 147464 | tf_op jit(solution)/shard_map/ppermute | solution.py:27
  41.9 7.3 %collective-permute-start.19 = (f32[48,256]{1,0:T(8,128)S(1)}, f32[48,256]{1,0:T(8,128)S(1)}, u32[]{:S(2)}, u32[]{:S(2)}) collective-permute-start(f32[48,256]{1,0:T(8,128)S(1)} %shard_map.131.refs_0_), channel_id=1, source_target_pairs={{0,4},{1,5},{2,6},{3,7},{4,0},{5,1},{6,2},{7,3},{8,12},{9,13},{10,... | collective-permute-start | bytes 147464 | tf_op jit(solution)/shard_map/ppermute | solution.py:27
  44.4 4.8 %collective-permute-start.20 = (f32[48,256]{1,0:T(8,128)S(1)}, f32[48,256]{1,0:T(8,128)S(1)}, u32[]{:S(2)}, u32[]{:S(2)}) collective-permute-start(f32[48,256]{1,0:T(8,128)S(1)} %shard_map.131.refs_0_), channel_id=1, source_target_pairs={{0,6},{1,7},{2,0},{3,1},{4,2},{5,3},{6,4},{7,5},{8,14},{9,15},{10,... | collective-permute-start | bytes 147464 | tf_op jit(solution)/shard_map/ppermute | solution.py:27
  45.5 5.2 %collective-permute-start.21 = (f32[48,256]{1,0:T(8,128)S(1)}, f32[48,256]{1,0:T(8,128)S(1)}, u32[]{:S(2)}, u32[]{:S(2)}) collective-permute-start(f32[48,256]{1,0:T(8,128)S(1)} %shard_map.131.refs_0_), channel_id=1, source_target_pairs={{0,1},{1,0},{2,3},{3,2},{4,5},{5,4},{6,7},{7,6},{8,9},{9,8},{10,11... | collective-permute-start | bytes 147464 | tf_op jit(solution)/shard_map/ppermute | solution.py:21
  47.6 3.0 %collective-permute-start.22 = (f32[48,256]{1,0:T(8,128)S(1)}, f32[48,256]{1,0:T(8,128)S(1)}, u32[]{:S(2)}, u32[]{:S(2)}) collective-permute-start(f32[48,256]{1,0:T(8,128)S(1)} %collective-permute-done.18.refs_1_), channel_id=1, source_target_pairs={{0,1},{1,0},{2,3},{3,2},{4,5},{5,4},{6,7},{7,6},{8,9},{9,8},{10,11... | collective-permute-start | bytes 147464 | tf_op jit(solution)/shard_map/ppermute | solution.py:21
  49.2 1.5 %collective-permute-start.23 = (f32[48,256]{1,0:T(8,128)S(1)}, f32[48,256]{1,0:T(8,128)S(1)}, u32[]{:S(2)}, u32[]{:S(2)}) collective-permute-start(f32[48,256]{1,0:T(8,128)S(1)} %collective-permute-done.19.refs_2_), channel_id=1, source_target_pairs={{0,1},{1,0},{2,3},{3,2},{4,5},{5,4},{6,7},{7,6},{8,9},{9,8},{10,11... | collective-permute-start | bytes 147464 | tf_op jit(solution)/shard_map/ppermute | solution.py:21
  49.2 2.3 %collective-permute-start.24 = (f32[48,256]{1,0:T(8,128)S(1)}, f32[48,256]{1,0:T(8,128)S(1)}, u32[]{:S(2)}, u32[]{:S(2)}) collective-permute-start(f32[48,256]{1,0:T(8,128)S(1)} %collective-permute-done.20.refs_3_), channel_id=1, source_target_pairs={{0,1},{1,0},{2,3},{3,2},{4,5},{5,4},{6,7},{7,6},{8,9},{9,8},{10,11... | collective-permute-start | bytes 147464 | tf_op jit(solution)/shard_map/ppermute | solution.py:21
  51.4 23.5 %copy-start.4 = (f32[384,384]{1,0:T(8,128)S(1)}, f32[384,384]{1,0:T(8,128)}, u32[]{:S(2)}) copy-start(f32[384,384]{1,0:T(8,128)} %param.23) | copy-start | bytes 1769476
  51.4 23.5 %copy-start.5 = (f32[384,384]{1,0:T(8,128)S(1)}, f32[384,384]{1,0:T(8,128)}, u32[]{:S(2)}) copy-start(f32[384,384]{1,0:T(8,128)} %param.24) | copy-start | bytes 1769476
  52.2 8.5 %collective-permute-start.25 = (f32[384,128]{1,0:T(8,128)S(1)}, f32[384,128]{1,0:T(8,128)S(1)}, u32[]{:S(2)}, u32[]{:S(2)}) collective-permute-start(f32[384,128]{1,0:T(8,128)S(1)} %get-tuple-element.32.normed), channel_id=1, source_target_pairs={{0,0},{1,1},{10,2},{59,3},{20,4},{53,5},{62,6},{15,7},{8,8},{9,9},... | collective-permute-start | bytes 589832 | tf_op jit(solution)/shard_map/ppermute | solution.py:381
  52.9 10.3 %collective-permute-start.26 = (f32[384,128]{1,0:T(8,128)S(1)}, f32[384,128]{1,0:T(8,128)S(1)}, u32[]{:S(2)}, u32[]{:S(2)}) collective-permute-start(f32[384,128]{1,0:T(8,128)S(1)} %get-tuple-element.32.normed), channel_id=1, source_target_pairs={{32,0},{33,1},{42,2},{27,3},{52,4},{21,5},{30,6},{47,7},{40,8},{41... | collective-permute-start | bytes 589832 | tf_op jit(solution)/shard_map/ppermute | solution.py:381
  59.6 16.6 %copy-start.11 = (f32[384]{0:T(512)S(1)}, f32[384]{0:T(512)}, u32[]{:S(2)}) copy-start(f32[384]{0:T(512)} %param.25) | copy-start | bytes 4612
  65.0 11.2 %collective-permute-start.27 = (f32[32,512]{1,0:T(8,128)S(1)}, f32[32,512]{1,0:T(8,128)S(1)}, u32[]{:S(2)}, u32[]{:S(2)}) collective-permute-start(f32[32,512]{1,0:T(8,128)S(1)} %get-tuple-element.35), channel_id=1, source_target_pairs={{0,2},{1,3},{2,4},{3,5},{4,6},{5,7},{6,0},{7,1},{8,10},{9,11},{10,... | collective-permute-start | bytes 196616 | tf_op jit(solution)/shard_map/ppermute | solution.py:27
  69.2 8.1 %collective-permute-start.28 = (f32[32,512]{1,0:T(8,128)S(1)}, f32[32,512]{1,0:T(8,128)S(1)}, u32[]{:S(2)}, u32[]{:S(2)}) collective-permute-start(f32[32,512]{1,0:T(8,128)S(1)} %get-tuple-element.36), channel_id=1, source_target_pairs={{0,4},{1,5},{2,6},{3,7},{4,0},{5,1},{6,2},{7,3},{8,12},{9,13},{10,... | collective-permute-start | bytes 196616 | tf_op jit(solution)/shard_map/ppermute | solution.py:27
  74.9 3.3 %collective-permute-start.29 = (f32[32,512]{1,0:T(8,128)S(1)}, f32[32,512]{1,0:T(8,128)S(1)}, u32[]{:S(2)}, u32[]{:S(2)}) collective-permute-start(f32[32,512]{1,0:T(8,128)S(1)} %get-tuple-element.37), channel_id=1, source_target_pairs={{0,6},{1,7},{2,0},{3,1},{4,2},{5,3},{6,4},{7,5},{8,14},{9,15},{10,... | collective-permute-start | bytes 196616 | tf_op jit(solution)/shard_map/ppermute | solution.py:27
  79.3 4.6 %collective-permute-start.30 = (f32[4,4,384]{2,1,0:T(4,128)S(1)}, f32[4,4,384]{2,1,0:T(4,128)S(1)}, u32[]{:S(2)}, u32[]{:S(2)}) collective-permute-start(f32[4,4,384]{2,1,0:T(4,128)S(1)} %get-tuple-element.40), channel_id=1, source_target_pairs={{0,1},{1,0},{2,3},{3,2},{4,5},{5,4},{6,7},{7,6},{8,9},{9,8},{10,11... | collective-permute-start | bytes 73736 | tf_op jit(solution)/shard_map/ppermute | solution.py:21

commit v2 on v1

v2 whole, which is shorter than its diff:
```python
import math

import jax
import jax.numpy as jnp
from jax import lax
from jax.experimental import pallas as pl
from jax.experimental.pallas import tpu as pltpu
from jax.sharding import PartitionSpec as P

C = 384
OUT = 48
CHIPS = 4
F32 = jnp.float32
BF16 = jnp.bfloat16


Z_OFFSETS = ((4, 0), (-3, 1), (-2, 2), (3, -1))


def sibling(x):
    return lax.ppermute(x, "wa", [(i, i ^ 1) for i in range(2 * CHIPS)])


def across_chips(xs):
    n = 2 * CHIPS
    return [
        lax.ppermute(x, "wa", [(i, (i + 2 * k) % n) for i in range(n)])
        for k, x in enumerate(xs, 1)
    ]


def gathered(x):
    same = [x] + across_chips([x] * (CHIPS - 1))
    return same + [sibling(piece) for piece in same]


def shifted(x, axis, by):
    n = lax.axis_size(axis)
    return lax.ppermute(x, axis, [(i, (i + by) % n) for i in range(n)])


def call(kernel, outs, *args, scratch=(), scalars=None, flops=1_000_000):
    in_specs = [pl.BlockSpec(memory_space=pltpu.VMEM)] * len(args)
    outs = [o if isinstance(o, jax.ShapeDtypeStruct) else jax.ShapeDtypeStruct(o, F32) for o in outs]
    moved = sum(x.size * x.dtype.itemsize for x in (*args, *outs))
    if scalars is not None:
        in_specs = [pl.BlockSpec(memory_space=pltpu.SMEM)] + in_specs
        args = (scalars,) + args
    return pl.pallas_call(
        kernel,
        out_shape=outs,
        in_specs=in_specs,
        out_specs=[pl.BlockSpec(memory_space=pltpu.VMEM)] * len(outs),
        scratch_shapes=list(scratch),
        compiler_params=pltpu.CompilerParams(vmem_limit_bytes=40 * 1024 * 1024),
        cost_estimate=pl.CostEstimate(flops=flops, bytes_accessed=moved, transcendentals=0),
    )(*args)


def halves(x):
    high = x.astype(BF16)
    return high, (x - high.astype(F32)).astype(BF16)


def product(wh, wl, xh, xl):
    def dot(a, b):
        return lax.dot_general(a, b, (((1,), (0,)), ((), ())), preferred_element_type=F32)

    return dot(wh, xh) + (dot(wh, xl) + dot(wl, xh))


def activated(x, gain):
    mean = jnp.mean(x * x, axis=0, keepdims=True)
    v = x * lax.rsqrt(mean + 1e-6) * gain
    return v / (1.0 + jnp.exp(-v))


def lane_of(shape):
    return lax.broadcasted_iota(jnp.int32, shape, 1)


def columns_joined(left, mid, right):
    col = lane_of(mid.shape) & 31
    return (
        mid
        + jnp.where(col != 0, pltpu.roll(left, 1, 1), 0.0)
        + jnp.where(col != 31, pltpu.roll(right, 127, 1), 0.0)
    )


def frames_moved(tap):
    late = (lane_of(tap.shape) & 127) >= 64
    moved = pltpu.roll(tap, 64, 1)
    return jnp.where(late, moved, 0.0), jnp.where(late, 0.0, moved)


def one_frame(early, late, second):
    first = lane_of(early.shape) < 64
    return jnp.where(
        second,
        jnp.where(first, pltpu.roll(early, 64, 1), late),
        jnp.where(first, early, pltpu.roll(late, 64, 1)),
    )


def rows_joined(prod, a):
    second_row = (lane_of((OUT, 128)) & 63) >= 32
    rows = []
    for i in range(3):
        t = 9 * a + 3 * i
        rows.append(
            [
                columns_joined(
                    *(
                        prod[(t + j) * OUT : (t + j + 1) * OUT, p * 128 : p * 128 + 128]
                        for j in range(3)
                    )
                )
                for p in range(2)
            ]
        )
    down, level, up = rows
    upper = [jnp.where(second_row, pltpu.roll(v, 32, 1), 0.0) for v in level]
    lower = [jnp.where(second_row, 0.0, pltpu.roll(v, 96, 1)) for v in level]
    return [
        up[0] + upper[0],
        up[1] + down[0] + lower[0] + upper[1],
        down[1] + lower[1],
    ]


def first_conv_kernel(at, *refs):
    pieces, (gain, wh, wl) = refs[:8], refs[8:11]
    next_out, own_out, strip_out, xh_out, xl_out, cells, prod = refs[11:]
    y, c = at[2], at[3]
    for k in range(CHIPS):
        mine, other = pieces[k][...], pieces[CHIPS + k][...]
        both = jnp.concatenate(
            [jnp.where(c == 0, mine, other), jnp.where(c == 0, other, mine)], axis=2
        )
        chip = lax.rem(y - k + CHIPS, CHIPS)
        for f in range(2):
            for r in range(4):
                base = (r // 2) * 128 + f * 64 + (r % 2) * 32
                cells[pl.ds(pl.multiple_of(base + 8 * chip, 8), 8), :] = both[f, r]
    strip = cells[...].T
    strip_out[...] = strip
    xh, xl = halves(activated(strip, gain[...]))
    xh_out[...] = xh
    xl_out[...] = xl
    prod[...] = product(wh[...], wl[...], xh, xl)
    first, second = rows_joined(prod, 0), rows_joined(prod, 1)
    for n in range(3):
        own, following = frames_moved(second[n])
        own_out[:, n * 128 : n * 128 + 128] = own
        next_out[:, n * 128 : n * 128 + 128] = first[n] + following


def first_conv_own_kernel(xh, xl, wh, wl, earlier, own_out, prod):
    prod[...] = product(wh[...], wl[...], xh[...], xl[...])
    for n, tile in enumerate(rows_joined(prod, 0)):
        lanes = slice(n * 128, n * 128 + 128)
        own_out[:, lanes] = tile + earlier[:, lanes]


def second_conv_kernel(at, *refs):
    pieces, (gain, wh, wl) = refs[:8], refs[8:11]
    next_mine, next_other, own_mine, own_other, inner, prod = refs[11:]
    y, c = at[2], at[3]
    for k in range(CHIPS):
        chip = lax.rem(y - k + CHIPS, CHIPS)
        for core, piece in ((c, pieces[k]), (1 - c, pieces[CHIPS + k])):
            start = pl.multiple_of((2 * chip + core) * OUT, 8)
            inner[pl.ds(start, OUT), :] = piece[...]
    act = activated(inner[...], gain[...])
    top, mid, bottom = act[:, :128], act[:, 128:256], act[:, 256:]
    second_row = (lane_of((C, 128)) & 63) >= 32
    level = jnp.concatenate(
        [
            jnp.where(second_row, pltpu.roll(mid, 32, 1), pltpu.roll(top, 96, 1)),
            jnp.where(second_row, pltpu.roll(bottom, 32, 1), pltpu.roll(mid, 96, 1)),
        ],
        axis=1,
    )
    stacked = jnp.concatenate([act[:, :256], level, act[:, 128:]], axis=0)
    xh, xl = halves(stacked)
    prod[...] = product(wh[...], wl[...], xh, xl)
    following, same = [], []
    for p in range(2):
        lanes = slice(p * 128, p * 128 + 128)
        first, second, third = [
            columns_joined(
                *(prod[(3 * a + j) * OUT : (3 * a + j + 1) * OUT, lanes] for j in range(3))
            )
            for a in range(3)
        ]
        own, moved = frames_moved(second)
        same.append(third + own)
        following.append(first + moved)
    next_mine[...] = one_frame(*following, c == 1)
    next_other[...] = one_frame(*following, c == 0)
    own_mine[...] = one_frame(*same, c == 1)
    own_other[...] = one_frame(*same, c == 0)


def norm_kernel(at, *refs):
    pieces, (strip, gain) = refs[:4], refs[4:6]
    blocked_out, normed_out, total = refs[6:]
    for k in range(CHIPS):
        chip = lax.rem(at[2] - k + CHIPS, CHIPS)
        start = pl.multiple_of(chip * (2 * OUT), 8)
        total[pl.ds(start, 2 * OUT), :] = pieces[k][...]
    frame = total[...] + one_frame(strip[:, :128], strip[:, 128:], at[3] == 1)
    blocked_out[...] = frame
    mean = jnp.mean(frame * frame, axis=0, keepdims=True)
    normed_out[...] = frame * lax.rsqrt(mean + 1e-6) * gain[...]


def query_kernel(at, blocked, normed, w_score, queries_out, rest_out, cells):
    y = at[2]
    cells[...] = blocked[...].T
    for r in range(4):
        start = pl.multiple_of(32 * r + 8 * y, 8)
        rest_out[8 * r : 8 * r + 8, :] = cells[pl.ds(start, 8), :]
    queries_out[...] = jnp.dot(
        normed[...].T, w_score[...], precision=lax.Precision.HIGHEST, preferred_element_type=F32
    )


def mix_kernel(at, queries, keys_a, keys_b, *refs):
    outs, state = refs[:CHIPS], refs[CHIPS]
    q = queries[...]
    scores = [
        jnp.dot(q, k[...], precision=lax.Precision.HIGHEST, preferred_element_type=F32)
        for k in (keys_a, keys_b)
    ]
    top = jnp.max(jnp.maximum(*scores), axis=1, keepdims=True)
    weights = [jnp.exp(s - top) for s in scores]
    denom = jnp.sum(weights[0] + weights[1], axis=1, keepdims=True)
    accum = [
        lax.dot_general(
            p,
            k[...],
            (((1,), (1,)), ((), ())),
            precision=lax.Precision.HIGHEST,
            preferred_element_type=F32,
        )
        for p, k in zip(weights, (keys_a, keys_b))
    ]
    state[:, :C] = accum[0] + accum[1]
    state[:, C:] = jnp.where(lane_of((128, 128)) < 64, top, denom)
    for k in range(CHIPS):
        chip = lax.rem(at[2] + k, CHIPS)
        for r in range(4):
            start = pl.multiple_of(32 * r + 8 * chip, 8)
            outs[k][8 * r : 8 * r + 8, :] = state[pl.ds(start, 8), :]


def merged(states):
    tops = [x[:, C : C + 1] for x in states]
    top = jnp.maximum(jnp.maximum(tops[0], tops[1]), jnp.maximum(tops[2], tops[3]))
    factors = [jnp.exp(t - top) for t in tops]
    denom = sum(f * x[:, C + 64 : C + 65] for f, x in zip(factors, states))
    return sum(f * x[:, :C] for f, x in zip(factors, states)) / denom


def project_kernel(at, a, b, c, d, w_mixed, bias, rest, mine_out, other_out):
    mixed = merged([x[...] for x in (a, b, c, d)])
    done = rest[...] + (
        jnp.dot(mixed, w_mixed[...], precision=lax.Precision.HIGHEST, preferred_element_type=F32)
        + bias[...]
    )
    done = done.reshape(4, 8, C)
    left, right = done[:, :4], done[:, 4:]
    mine_out[...] = jnp.where(at[3] == 0, left, right)
    other_out[...] = jnp.where(at[3] == 0, right, left)


def split_weights(kernel, order):
    w = jnp.transpose(kernel, order)
    w = w.reshape(-1, math.prod(w.shape[order.index(0) + 1 :]))
    high = lax.reduce_precision(w, 8, 7)
    return high.astype(BF16), (w - high).astype(BF16)


def per_device(
    latents,
    first_gain,
    first_kernel,
    first_bias,
    second_gain,
    second_kernel,
    second_bias,
    attn_gain,
    w_query,
    w_key,
    w_value,
    w_out,
    out_bias,
):
    wa = lax.axis_index("wa")
    at = jnp.stack([lax.axis_index("ta"), lax.axis_index("ha"), wa // 2, wa % 2]).astype(jnp.int32)
    column = lambda v: v.reshape(C, 1)

    first_w = split_weights(first_kernel[:, :2], (1, 2, 3, 0, 4))
    first_w_own = split_weights(first_kernel[:, 2:], (1, 2, 3, 0, 4))
    second_w = split_weights(second_kernel, (1, 3, 0, 2, 4))
    w_score = lax.dot_general(
        w_query,
        w_key,
        (((1,), (1,)), ((), ())),
        precision=lax.Precision.HIGHEST,
        preferred_element_type=F32,
    ) * (1.0 / math.sqrt(C))
    w_mixed = jnp.dot(w_value, w_out, precision=lax.Precision.HIGHEST, preferred_element_type=F32)

    operand = lambda *shape: jax.ShapeDtypeStruct(shape, BF16)
    following, earlier, strip, *x = call(
        first_conv_kernel,
        [(OUT, 384), (OUT, 384), (C, 256), operand(C, 256), operand(C, 256)],
        *gathered(latents),
        column(first_gain),
        *first_w,
        scratch=[pltpu.VMEM((256, C), F32), pltpu.VMEM((18 * OUT, 256), F32)],
        scalars=at,
        flops=1_000_000_000,
    )
    arrived = shifted(following, "ta", 1)
    (own,) = call(
        first_conv_own_kernel,
        [(OUT, 384)],
        *x,
        *first_w_own,
        earlier,
        scratch=[pltpu.VMEM((9 * OUT, 256), F32)],
        flops=500_000_000,
    )
    own = own + jnp.where(at[0] > 0, arrived, 0.0)
    top, mid, bottom = own[:, :128], own[:, 128:256], own[:, 256:]
    above, below = shifted(bottom, "ha", 1), shifted(top, "ha", -1)
    second_row = (lax.broadcasted_iota(jnp.int32, (1, 128), 1) & 63) >= 32
    b = lax.dynamic_slice_in_dim(column(first_bias), wa * OUT, OUT)
    inside = jnp.where(at[1] > 0, True, second_row)
    top = jnp.where(inside, top + b + jnp.where(at[1] > 0, above, 0.0), 0.0)
    inside = jnp.where(at[1] < 7, True, ~second_row)
    bottom = jnp.where(inside, bottom + b + jnp.where(at[1] < 7, below, 0.0), 0.0)
    inner = jnp.concatenate([top, mid + b, bottom], axis=1)
    next_mine, next_other, mine, other = call(
        second_conv_kernel,
        [(OUT, 128)] * 4,
        *gathered(inner),
        column(second_gain),
        *second_w,
        scratch=[pltpu.VMEM((C, 384), F32), pltpu.VMEM((9 * OUT, 256), F32)],
        scalars=at,
        flops=1_000_000_000,
    )
    arrived = shifted(next_mine, "ta", 1)
    n = 2 * CHIPS
    arrived_other = lax.ppermute(
        next_other,
        ("ta", "wa"),
        [(t * n + i, (t + 1) % 4 * n + (i ^ 1)) for t in range(4) for i in range(n)],
    )
    mine = mine + jnp.where(at[0] > 0, arrived, 0.0)
    other = sibling(other) + jnp.where(at[0] > 0, arrived_other, 0.0)
    even = wa % 2 == 0
    change = jnp.concatenate(
        [jnp.where(even, mine, other), jnp.where(even, other, mine)], axis=0
    ) + lax.dynamic_slice_in_dim(column(second_bias), at[2] * (2 * OUT), 2 * OUT)
    blocked, normed = call(
        norm_kernel,
        [(C, 128), (C, 128)],
        change,
        *across_chips([change] * (CHIPS - 1)),
        strip,
        column(attn_gain),
        scratch=[pltpu.VMEM((C, 128), F32)],
        scalars=at,
    )
    keys = []
    for n in range(2):
        pairs = []
        for h in range(8):
            for w in range(8):
                offset = Z_OFFSETS[w // 2][n] * (1 if w % 2 == 0 else -1)
                pairs.append((((h + offset) % 8) * 8 + w, h * 8 + w))
        keys.append(lax.ppermute(normed, ("ha", "wa"), pairs))
    queries, rest = call(
        query_kernel,
        [(128, C), (32, C)],
        blocked,
        normed,
        w_score,
        scratch=[pltpu.VMEM((128, C), F32)],
        scalars=at,
    )
    states = call(
        mix_kernel,
        [(32, C + 128)] * CHIPS,
        queries,
        *keys,
        scratch=[pltpu.VMEM((128, C + 128), F32)],
        scalars=at,
    )
    mine, other = call(
        project_kernel,
        [(4, 4, C), (4, 4, C)],
        states[0],
        *across_chips(states[1:]),
        w_mixed,
        out_bias.reshape(1, C),
        rest,
        scalars=at,
    )
    other = sibling(other)
    return jnp.stack([jnp.where(even, mine, other), jnp.where(even, other, mine)])


def solution(mesh):
    in_specs = (
        P("ta", "ha", "wa", None),
        P(),
        P("wa", None, None, None, None),
        P(),
        P(),
        P("wa", None, None, None, None),
        P(),
        P(),
        P(),
        P(),
        P(),
        P(),
        P(),
    )
    out_specs = P("ta", "ha", "wa", None)
    return jax.shard_map(
        per_device, mesh=mesh, in_specs=in_specs, out_specs=out_specs, check_vma=False
    )
```

time: 84.7 us -> 78.8 us (0.930)
  the two profiles are of different devices: /device:TPU:33 before, /device:TPU:1 now
where the time goes in v2:
time: 78.8 us; the launch traced here: 78.6 us
  starting transfers between devices  46.9 us (60%)
  waiting for transfers between devices  13.2 us (17%)
  Pallas kernels  9.22 us (12%)
  local copies, waits for them, and re-layouts  5 us (6%)
  matrix products  2.53 us (3%)
  other arithmetic  1.45 us (2%)
    ppermute x12, starting transfers between devices, across_chips(): lax.ppermute(x, 'wa', [(i, (i + 2 * k) % n) for i in range(n)])  24 us
    ppermute x10, starting transfers between devices, sibling(): return lax.ppermute(x, 'wa', [(i, i ^ 1) for i in range(2 * CHIPS)])  9.45 us
    pallas_call x7, Pallas kernels, call(): pl.pallas_call(kernel, out_shape=outs, in_specs=in_specs, out_specs=[pl.B...  9.22 us
    ppermute x4, starting transfers between devices, shifted(): return lax.ppermute(x, axis, [(i, (i + by) % n) for i in range(n)])  7.11 us
    ppermute x2, starting transfers between devices, per_device(): keys.append(lax.ppermute(normed, ('ha', 'wa'), pairs))  5.23 us
    ppermute x12, waiting for transfers between devices, across_chips(): lax.ppermute(x, 'wa', [(i, (i + 2 * k) % n) for i in range(n)])  4.98 us
    ppermute x4, waiting for transfers between devices, shifted(): return lax.ppermute(x, axis, [(i, (i + by) % n) for i in range(n)])  4.24 us
    transpose x1, local copies, waits for them, and re-layouts, split_weights(): w = jnp.transpose(kernel, order)  2.58 us
  transfers between devices with their start and end apart: 29, of which 12 were waited for; matrix products, arithmetic and copies ran while one was open for 10% of the time, Pallas kernels for 2%

profile of v2, /device:TPU:1, one launch (start us, length us, event | category | flops | bytes accessed | tf_op | source)
XLA Modules:
  0.0 78.6 jit_solution(8238753239896316082)
XLA Ops:
  0.0 2.1 %collective-permute-start = (f32[2,4,4,384]{3,2,1,0:T(4,128)}, f32[2,4,4,384]{3,2,1,0:T(4,128)S(1)}, u32[]{:S(2)}, u32[]{:S(2)}) collective-permute-start(f32[2,4,4,384]{3,2,1,0:T(4,128)} %refs_0_.1), channel_id=1, source_target_pairs={{0,2},{1,3},{2,4},{3,5},{4,6},{5,7},{6,0},{7,1},{8,10},{9,11},{10,... | collective-permute-start | bytes 147464 | tf_op jit(solution)/shard_map/ppermute | solution.py:27
  2.1 2.6 %collective-permute-start.1 = (f32[2,4,4,384]{3,2,1,0:T(4,128)}, f32[2,4,4,384]{3,2,1,0:T(4,128)S(1)}, u32[]{:S(2)}, u32[]{:S(2)}) collective-permute-start(f32[2,4,4,384]{3,2,1,0:T(4,128)} %refs_0_.1), channel_id=1, source_target_pairs={{0,4},{1,5},{2,6},{3,7},{4,0},{5,1},{6,2},{7,3},{8,12},{9,13},{10,... | collective-permute-start | bytes 147464 | tf_op jit(solution)/shard_map/ppermute | solution.py:27
  4.8 1.1 %collective-permute-start.2 = (f32[2,4,4,384]{3,2,1,0:T(4,128)}, f32[2,4,4,384]{3,2,1,0:T(4,128)S(1)}, u32[]{:S(2)}, u32[]{:S(2)}) collective-permute-start(f32[2,4,4,384]{3,2,1,0:T(4,128)} %refs_0_.1), channel_id=1, source_target_pairs={{0,6},{1,7},{2,0},{3,1},{4,2},{5,3},{6,4},{7,5},{8,14},{9,15},{10,... | collective-permute-start | bytes 147464 | tf_op jit(solution)/shard_map/ppermute | solution.py:27
  5.8 1.5 %collective-permute-start.3 = (f32[2,4,4,384]{3,2,1,0:T(4,128)}, f32[2,4,4,384]{3,2,1,0:T(4,128)S(1)}, u32[]{:S(2)}, u32[]{:S(2)}) collective-permute-start(f32[2,4,4,384]{3,2,1,0:T(4,128)} %refs_0_.1), channel_id=1, source_target_pairs={{0,1},{1,0},{2,3},{3,2},{4,5},{5,4},{6,7},{7,6},{8,9},{9,8},{10,11... | collective-permute-start | bytes 147464 | tf_op jit(solution)/shard_map/ppermute | solution.py:21
  7.6 1.7 %collective-permute-start.4 = (f32[2,4,4,384]{3,2,1,0:T(4,128)S(1)}, f32[2,4,4,384]{3,2,1,0:T(4,128)S(1)}, u32[]{:S(2)}, u32[]{:S(2)}) collective-permute-start(f32[2,4,4,384]{3,2,1,0:T(4,128)S(1)} %collective-permute-done.refs_1_), channel_id=1, source_target_pairs={{0,1},{1,0},{2,3},{3,2},{4,5},{5,4},{6,7},{7,6},{8,9},{9,8},{10,11... | collective-permute-start | bytes 147464 | tf_op jit(solution)/shard_map/ppermute | solution.py:21
  9.3 1.0 %collective-permute-start.6 = (f32[2,4,4,384]{3,2,1,0:T(4,128)S(1)}, f32[2,4,4,384]{3,2,1,0:T(4,128)S(1)}, u32[]{:S(2)}, u32[]{:S(2)}) collective-permute-start(f32[2,4,4,384]{3,2,1,0:T(4,128)S(1)} %collective-permute-done.2.refs_3_), channel_id=1, source_target_pairs={{0,1},{1,0},{2,3},{3,2},{4,5},{5,4},{6,7},{7,6},{8,9},{9,8},{10,11... | collective-permute-start | bytes 147464 | tf_op jit(solution)/shard_map/ppermute | solution.py:21
  10.5 0.7 collective-permute-done.6.refs_7_
  11.2 1.9 %shard_map.127 = (f32[48,384]{1,0:T(8,128)S(1)}, f32[48,384]{1,0:T(8,128)S(1)}, f32[384,256]{1,0:T(8,128)S(1)}, bf16[384,256]{1,0:T(8,128)(2,1)S(1)}, bf16[384,256]{1,0:T(8,128)(2,1)S(1)}) custom-call(s32[4]{0:T(128)S(1)} %pad_add_fusion.at, f32[2,4,4,384]{3,2,1,0:T(4,128)S(1)} %copy-done.1, f32[2,4,4,384]{3,2,1,0:T(4,128)S(1)} %collective-permute-done.refs_1_, ...), custom_call_target="tpu_custom_call" | custom-call | flops 1000000000 | bytes 2655744 | tf_op jit(solution)/shard_map/pallas_call | solution.py:49
  13.1 1.3 %collective-permute-start.7 = (f32[48,384]{1,0:T(8,128)S(1)}, f32[48,384]{1,0:T(8,128)S(1)}, u32[]{:S(2)}, u32[]{:S(2)}) collective-permute-start(f32[48,384]{1,0:T(8,128)S(1)} %get-tuple-element.27), channel_id=1, source_target_pairs={{0,64},{64,128},{128,192},{192,0},{1,65},{65,129},{129,193},{193,1... | collective-permute-start | bytes 221192 | tf_op jit(solution)/shard_map/ppermute | solution.py:39
  14.5 0.6 shard_map.128
  15.1 2.5 %collective-permute-done.7 = f32[48,384]{1,0:T(8,128)S(1)} collective-permute-done((f32[48,384]{1,0:T(8,128)S(1)}, f32[48,384]{1,0:T(8,128)S(1)}, u32[]{:S(2)}, u32[]{:S(2)}) %collective-permute-start.7) | collective-permute-done | bytes 73760 | tf_op jit(solution)/shard_map/ppermute | solution.py:39
  17.6 1.7 %collective-permute-start.8 = (f32[48,128]{1,0:T(8,128)S(1)}, f32[48,128]{1,0:T(8,128)S(1)}, u32[]{:S(2)}, u32[]{:S(2)}) collective-permute-start(f32[48,128]{1,0:T(8,128)S(1)} %get-tuple-element.54), channel_id=1, source_target_pairs={{0,8},{8,16},{16,24},{24,32},{32,40},{40,48},{48,56},{56,0},{1,9},... | collective-permute-start | bytes 73736 | tf_op jit(solution)/shard_map/ppermute | solution.py:39
  19.3 4.0 %collective-permute-start.9 = (f32[48,128]{1,0:T(8,128)S(1)}, f32[48,128]{1,0:T(8,128)S(1)}, u32[]{:S(2)}, u32[]{:S(2)}) collective-permute-start(f32[48,128]{1,0:T(8,128)S(1)} %get-tuple-element.55), channel_id=1, source_target_pairs={{0,56},{8,0},{16,8},{24,16},{32,24},{40,32},{48,40},{56,48},{1,57}... | collective-permute-start | bytes 73736 | tf_op jit(solution)/shard_map/ppermute | solution.py:39
  23.4 0.8 dynamic-slice.6
  24.6 0.8 %collective-permute-start.10 = (f32[48,384]{1,0:T(8,128)S(1)}, f32[48,384]{1,0:T(8,128)S(1)}, u32[]{:S(2)}, u32[]{:S(2)}) collective-permute-start(f32[48,384]{1,0:T(8,128)S(1)} %pad_maximum_fusion.refs_0_), channel_id=1, source_target_pairs={{0,2},{1,3},{2,4},{3,5},{4,6},{5,7},{6,0},{7,1},{8,10},{9,11},{10,... | collective-permute-start | bytes 221192 | tf_op jit(solution)/shard_map/ppermute | solution.py:27
  25.4 2.7 %collective-permute-start.11 = (f32[48,384]{1,0:T(8,128)S(1)}, f32[48,384]{1,0:T(8,128)S(1)}, u32[]{:S(2)}, u32[]{:S(2)}) collective-permute-start(f32[48,384]{1,0:T(8,128)S(1)} %pad_maximum_fusion.refs_0_), channel_id=1, source_target_pairs={{0,4},{1,5},{2,6},{3,7},{4,0},{5,1},{6,2},{7,3},{8,12},{9,13},{10,... | collective-permute-start | bytes 221192 | tf_op jit(solution)/shard_map/ppermute | solution.py:27
  28.1 0.7 collective-permute-start.12
  28.8 2.6 %copy.16 = f32[3,3,48,3,384]{4,3,2,1,0:T(4,128)S(1)} copy(f32[3,3,48,3,384]{4,2,1,3,0:T(8,128)} %bitcast.28) | data formatting | bytes 3981312 | tf_op jit(solution)/shard_map/transpose | solution.py:280
  31.6 2.8 %collective-permute-start.13 = (f32[48,384]{1,0:T(8,128)S(1)}, f32[48,384]{1,0:T(8,128)S(1)}, u32[]{:S(2)}, u32[]{:S(2)}) collective-permute-start(f32[48,384]{1,0:T(8,128)S(1)} %pad_maximum_fusion.refs_0_), channel_id=1, source_target_pairs={{0,1},{1,0},{2,3},{3,2},{4,5},{5,4},{6,7},{7,6},{8,9},{9,8},{10,11... | collective-permute-start | bytes 221192 | tf_op jit(solution)/shard_map/ppermute | solution.py:21
  34.4 0.4 collective-permute-start.15
  34.8 0.6 collective-permute-start.16
  36.3 2.0 %shard_map.129 = (f32[48,128]{1,0:T(8,128)S(1)}, f32[48,128]{1,0:T(8,128)S(1)}, f32[48,128]{1,0:T(8,128)S(1)}, f32[48,128]{1,0:T(8,128)S(1)}) custom-call(s32[4]{0:T(128)S(1)} %pad_add_fusion.at, f32[48,384]{1,0:T(8,128)S(1)} %pad_maximum_fusion.refs_0_, f32[48,384]{1,0:T(8,128)S(1)} %collective-permute-done.10.refs_1_, ...), custom_call_target="tpu_custom_call" | custom-call | flops 1000000000 | bytes 2680320 | tf_op jit(solution)/shard_map/pallas_call | solution.py:49
  38.4 0.6 collective-permute-start.18
  39.1 1.1 %collective-permute-start.19 = (f32[48,128]{1,0:T(8,128)S(1)}, f32[48,128]{1,0:T(8,128)S(1)}, u32[]{:S(2)}, u32[]{:S(2)}) collective-permute-start(f32[48,128]{1,0:T(8,128)S(1)} %get-tuple-element.31), channel_id=1, source_target_pairs={{0,65},{1,64},{2,67},{3,66},{4,69},{5,68},{6,71},{7,70},{64,129},{... | collective-permute-start | bytes 73736 | tf_op jit(solution)/shard_map/ppermute | solution.py:360
  40.2 0.8 dynamic-slice.7
  40.9 1.4 %collective-permute-done.17 = f32[48,128]{1,0:T(8,128)S(1)} collective-permute-done((f32[48,128]{1,0:T(8,128)S(1)}, f32[48,128]{1,0:T(8,128)S(1)}, u32[]{:S(2)}, u32[]{:S(2)}) %collective-permute-start.17) | collective-permute-done | bytes 24608 | tf_op jit(solution)/shard_map/ppermute | solution.py:39
  42.3 1.2 %collective-permute-done.19 = f32[48,128]{1,0:T(8,128)S(1)} collective-permute-done((f32[48,128]{1,0:T(8,128)S(1)}, f32[48,128]{1,0:T(8,128)S(1)}, u32[]{:S(2)}, u32[]{:S(2)}) %collective-permute-start.19) | collective-permute-done | bytes 24608 | tf_op jit(solution)/shard_map/ppermute | solution.py:360
  43.6 1.0 %collective-permute-start.20 = (f32[96,128]{1,0:T(8,128)S(1)}, f32[96,128]{1,0:T(8,128)S(1)}, u32[]{:S(2)}, u32[]{:S(2)}) collective-permute-start(f32[96,128]{1,0:T(8,128)S(1)} %maximum_add_fusion.refs_0_), channel_id=1, source_target_pairs={{0,2},{1,3},{2,4},{3,5},{4,6},{5,7},{6,0},{7,1},{8,10},{9,11},{10,... | collective-permute-start | bytes 147464 | tf_op jit(solution)/shard_map/ppermute | solution.py:27
  44.6 1.6 %collective-permute-start.21 = (f32[96,128]{1,0:T(8,128)S(1)}, f32[96,128]{1,0:T(8,128)S(1)}, u32[]{:S(2)}, u32[]{:S(2)}) collective-permute-start(f32[96,128]{1,0:T(8,128)S(1)} %maximum_add_fusion.refs_0_), channel_id=1, source_target_pairs={{0,4},{1,5},{2,6},{3,7},{4,0},{5,1},{6,2},{7,3},{8,12},{9,13},{10,... | collective-permute-start | bytes 147464 | tf_op jit(solution)/shard_map/ppermute | solution.py:27
  46.2 0.9 %collective-permute-start.22 = (f32[96,128]{1,0:T(8,128)S(1)}, f32[96,128]{1,0:T(8,128)S(1)}, u32[]{:S(2)}, u32[]{:S(2)}) collective-permute-start(f32[96,128]{1,0:T(8,128)S(1)} %maximum_add_fusion.refs_0_), channel_id=1, source_target_pairs={{0,6},{1,7},{2,0},{3,1},{4,2},{5,3},{6,4},{7,5},{8,14},{9,15},{10,... | collective-permute-start | bytes 147464 | tf_op jit(solution)/shard_map/ppermute | solution.py:27
  47.3 0.5 collective-permute-done.20.refs_1_
  47.8 1.3 %collective-permute-done.21.refs_2_ = f32[96,128]{1,0:T(8,128)S(1)} collective-permute-done((f32[96,128]{1,0:T(8,128)S(1)}, f32[96,128]{1,0:T(8,128)S(1)}, u32[]{:S(2)}, u32[]{:S(2)}) %collective-permute-start.21) | collective-permute-done | bytes 49184 | tf_op jit(solution)/shard_map/ppermute | solution.py:27
  49.2 0.6 collective-permute-done.22.refs_3_
  49.7 0.8 shard_map.130
  50.5 4.4 %collective-permute-start.23 = (f32[384,128]{1,0:T(8,128)S(1)}, f32[384,128]{1,0:T(8,128)S(1)}, u32[]{:S(2)}, u32[]{:S(2)}) collective-permute-start(f32[384,128]{1,0:T(8,128)S(1)} %get-tuple-element.34.normed), channel_id=1, source_target_pairs={{32,0},{33,1},{42,2},{27,3},{52,4},{21,5},{30,6},{47,7},{40,8},{41... | collective-permute-start | bytes 589832 | tf_op jit(solution)/shard_map/ppermute | solution.py:388
  54.9 0.9 %collective-permute-start.24 = (f32[384,128]{1,0:T(8,128)S(1)}, f32[384,128]{1,0:T(8,128)S(1)}, u32[]{:S(2)}, u32[]{:S(2)}) collective-permute-start(f32[384,128]{1,0:T(8,128)S(1)} %get-tuple-element.34.normed), channel_id=1, source_target_pairs={{0,0},{1,1},{10,2},{59,3},{20,4},{53,5},{62,6},{15,7},{8,8},{9,9},... | collective-permute-start | bytes 589832 | tf_op jit(solution)/shard_map/ppermute | solution.py:388
  55.8 1.3 %convolution_multiply_fusion.w_score = f32[384,384]{1,0:T(8,128)S(1)} fusion(f32[384,384]{1,0:T(8,128)S(1)} %copy-done, f32[384,384]{1,0:T(8,128)S(1)} %copy-done.2), kind=kOutput, calls=%fused_computation.6 | convolution fusion | flops 679624704 | bytes 1769472 | tf_op jit(solution)/shard_map/dot_general | solution.py:308
  57.1 1.1 %shard_map.131 = (f32[128,384]{1,0:T(8,128)S(1)}, f32[32,384]{1,0:T(8,128)S(1)}) custom-call(s32[4]{0:T(128)S(1)} %pad_add_fusion.at, f32[384,128]{1,0:T(8,128)S(1)} %get-tuple-element.33.blocked, f32[384,128]{1,0:T(8,128)S(1)} %get-tuple-element.34.normed, f32[384,384]{1,0:T(8,128)S(1)} %convolution_multiply_fusion.w_score), custom_call_target="tpu_custom_call" | custom-call | flops 1000000 | bytes 1228800 | tf_op jit(solution)/shard_map/pallas_call | solution.py:49
  58.2 1.2 %collective-permute-done.23.keys_a = f32[384,128]{1,0:T(8,128)S(1)} collective-permute-done((f32[384,128]{1,0:T(8,128)S(1)}, f32[384,128]{1,0:T(8,128)S(1)}, u32[]{:S(2)}, u32[]{:S(2)}) %collective-permute-start.23) | collective-permute-done | bytes 196640 | tf_op jit(solution)/shard_map/ppermute | solution.py:388
  59.4 1.7 %shard_map.132 = (f32[32,512]{1,0:T(8,128)S(1)}, f32[32,512]{1,0:T(8,128)S(1)}, f32[32,512]{1,0:T(8,128)S(1)}, f32[32,512]{1,0:T(8,128)S(1)}) custom-call(s32[4]{0:T(128)S(1)} %pad_add_fusion.at, f32[128,384]{1,0:T(8,128)S(1)} %get-tuple-element.35.queries, f32[384,128]{1,0:T(8,128)S(1)} %collective-permute-done.23.keys_a, ...), custom_call_target="tpu_custom_call" | custom-call | flops 1000000 | bytes 851968 | tf_op jit(solution)/shard_map/pallas_call | solution.py:49
  61.1 6.4 %collective-permute-start.25 = (f32[32,512]{1,0:T(8,128)S(1)}, f32[32,512]{1,0:T(8,128)S(1)}, u32[]{:S(2)}, u32[]{:S(2)}) collective-permute-start(f32[32,512]{1,0:T(8,128)S(1)} %get-tuple-element.37), channel_id=1, source_target_pairs={{0,2},{1,3},{2,4},{3,5},{4,6},{5,7},{6,0},{7,1},{8,10},{9,11},{10,... | collective-permute-start | bytes 196616 | tf_op jit(solution)/shard_map/ppermute | solution.py:27
  67.5 4.0 %collective-permute-start.26 = (f32[32,512]{1,0:T(8,128)S(1)}, f32[32,512]{1,0:T(8,128)S(1)}, u32[]{:S(2)}, u32[]{:S(2)}) collective-permute-start(f32[32,512]{1,0:T(8,128)S(1)} %get-tuple-element.38), channel_id=1, source_target_pairs={{0,4},{1,5},{2,6},{3,7},{4,0},{5,1},{6,2},{7,3},{8,12},{9,13},{10,... | collective-permute-start | bytes 196616 | tf_op jit(solution)/shard_map/ppermute | solution.py:27
  71.5 1.3 %fusion.4.w_mixed = f32[384,384]{1,0:T(8,128)S(1)} fusion(f32[384,384]{1,0:T(8,128)S(1)} %copy-done.3, f32[384,384]{1,0:T(8,128)S(1)} %copy-done.4), kind=kOutput, calls=%fused_computation.28 | convolution fusion | flops 679477248 | bytes 1769472 | tf_op jit(solution)/shard_map/dot_general | solution.py:315
  72.8 2.5 %collective-permute-done.26.c = f32[32,512]{1,0:T(8,128)S(1)} collective-permute-done((f32[32,512]{1,0:T(8,128)S(1)}, f32[32,512]{1,0:T(8,128)S(1)}, u32[]{:S(2)}, u32[]{:S(2)}) %collective-permute-start.26) | collective-permute-done | bytes 65568 | tf_op jit(solution)/shard_map/ppermute | solution.py:27
  75.3 1.0 %shard_map.133 = (f32[4,4,384]{2,1,0:T(4,128)S(1)}, f32[4,4,384]{2,1,0:T(4,128)S(1)}) custom-call(s32[4]{0:T(128)S(1)} %pad_add_fusion.at, f32[32,512]{1,0:T(8,128)S(1)} %get-tuple-element.36.a, f32[32,512]{1,0:T(8,128)S(1)} %collective-permute-done.25.b, f32[32,512]{1,0:T(8,128)S(1)} %collective-permute-done.26.c, f32[32,512]{1,0:T(8,128)S(1)} %collective-permute-done.27.d, ...), custom_call_target="tpu_custom_call" | custom-call | flops 1000000 | bytes 951808 | tf_op jit(solution)/shard_map/pallas_call | solution.py:49
  76.4 0.8 collective-permute-start.28
  77.2 0.8 %collective-permute-done.28 = f32[4,4,384]{2,1,0:T(4,128)S(1)} collective-permute-done((f32[4,4,384]{2,1,0:T(4,128)S(1)}, f32[4,4,384]{2,1,0:T(4,128)S(1)}, u32[]{:S(2)}, u32[]{:S(2)}) %collective-permute-start.28) | collective-permute-done | bytes 24608 | tf_op jit(solution)/shard_map/ppermute | solution.py:21
  78.0 0.6 pad_maximum_fusion.1
  (62 shorter events, 2.4 us)
Async XLA Ops:
  0.0 55.8 %copy-start = (f32[384,384]{1,0:T(8,128)S(1)}, f32[384,384]{1,0:T(8,128)}, u32[]{:S(2)}) copy-start(f32[384,384]{1,0:T(8,128)} %param.21) | copy-start | bytes 1769476
  0.0 7.3 %slice-start = ((f32[48,3,3,3,384]{4,0,3,2,1:T(8,128)}), f32[48,2,3,3,384]{4,0,3,2,1:T(8,128)S(1)}, s32[]{:S(2)}) async-start(f32[48,3,3,3,384]{4,0,3,2,1:T(8,128)} %param.15), calls=%async_computation | async-start | bytes 2654208 | tf_op jit(solution)/shard_map/slice | solution.py:305
  0.0 7.5 %collective-permute-start = (f32[2,4,4,384]{3,2,1,0:T(4,128)}, f32[2,4,4,384]{3,2,1,0:T(4,128)S(1)}, u32[]{:S(2)}, u32[]{:S(2)}) collective-permute-start(f32[2,4,4,384]{3,2,1,0:T(4,128)} %refs_0_.1), channel_id=1, source_target_pairs={{0,2},{1,3},{2,4},{3,5},{4,6},{5,7},{6,0},{7,1},{8,10},{9,11},{10,... | collective-permute-start | bytes 147464 | tf_op jit(solution)/shard_map/ppermute | solution.py:27
  2.1 7.2 %collective-permute-start.1 = (f32[2,4,4,384]{3,2,1,0:T(4,128)}, f32[2,4,4,384]{3,2,1,0:T(4,128)S(1)}, u32[]{:S(2)}, u32[]{:S(2)}) collective-permute-start(f32[2,4,4,384]{3,2,1,0:T(4,128)} %refs_0_.1), channel_id=1, source_target_pairs={{0,4},{1,5},{2,6},{3,7},{4,0},{5,1},{6,2},{7,3},{8,12},{9,13},{10,... | collective-permute-start | bytes 147464 | tf_op jit(solution)/shard_map/ppermute | solution.py:27
  4.8 4.5 %collective-permute-start.2 = (f32[2,4,4,384]{3,2,1,0:T(4,128)}, f32[2,4,4,384]{3,2,1,0:T(4,128)S(1)}, u32[]{:S(2)}, u32[]{:S(2)}) collective-permute-start(f32[2,4,4,384]{3,2,1,0:T(4,128)} %refs_0_.1), channel_id=1, source_target_pairs={{0,6},{1,7},{2,0},{3,1},{4,2},{5,3},{6,4},{7,5},{8,14},{9,15},{10,... | collective-permute-start | bytes 147464 | tf_op jit(solution)/shard_map/ppermute | solution.py:27
  5.8 4.7 %collective-permute-start.3 = (f32[2,4,4,384]{3,2,1,0:T(4,128)}, f32[2,4,4,384]{3,2,1,0:T(4,128)S(1)}, u32[]{:S(2)}, u32[]{:S(2)}) collective-permute-start(f32[2,4,4,384]{3,2,1,0:T(4,128)} %refs_0_.1), channel_id=1, source_target_pairs={{0,1},{1,0},{2,3},{3,2},{4,5},{5,4},{6,7},{7,6},{8,9},{9,8},{10,11... | collective-permute-start | bytes 147464 | tf_op jit(solution)/shard_map/ppermute | solution.py:21
  7.3 3.0 %copy-start.5 = (f32[384]{0:T(512)S(1)}, f32[384]{0:T(512)}, u32[]{:S(2)}) copy-start(f32[384]{0:T(512)} %param.14) | copy-start | bytes 4612
  7.3 3.8 %copy-start.1 = (f32[2,4,4,384]{3,2,1,0:T(4,128)S(1)}, f32[2,4,4,384]{3,2,1,0:T(4,128)}, u32[]{:S(2)}) copy-start(f32[2,4,4,384]{3,2,1,0:T(4,128)} %refs_0_.1) | copy-start | bytes 147460
  7.6 2.9 %collective-permute-start.4 = (f32[2,4,4,384]{3,2,1,0:T(4,128)S(1)}, f32[2,4,4,384]{3,2,1,0:T(4,128)S(1)}, u32[]{:S(2)}, u32[]{:S(2)}) collective-permute-start(f32[2,4,4,384]{3,2,1,0:T(4,128)S(1)} %collective-permute-done.refs_1_), channel_id=1, source_target_pairs={{0,1},{1,0},{2,3},{3,2},{4,5},{5,4},{6,7},{7,6},{8,9},{9,8},{10,11... | collective-permute-start | bytes 147464 | tf_op jit(solution)/shard_map/ppermute | solution.py:21
  9.3 1.2 %collective-permute-start.5 = (f32[2,4,4,384]{3,2,1,0:T(4,128)S(1)}, f32[2,4,4,384]{3,2,1,0:T(4,128)S(1)}, u32[]{:S(2)}, u32[]{:S(2)}) collective-permute-start(f32[2,4,4,384]{3,2,1,0:T(4,128)S(1)} %collective-permute-done.1.refs_2_), channel_id=1, source_target_pairs={{0,1},{1,0},{2,3},{3,2},{4,5},{5,4},{6,7},{7,6},{8,9},{9,8},{10,11... | collective-permute-start | bytes 147464 | tf_op jit(solution)/shard_map/ppermute | solution.py:21
  9.3 1.9 %collective-permute-start.6 = (f32[2,4,4,384]{3,2,1,0:T(4,128)S(1)}, f32[2,4,4,384]{3,2,1,0:T(4,128)S(1)}, u32[]{:S(2)}, u32[]{:S(2)}) collective-permute-start(f32[2,4,4,384]{3,2,1,0:T(4,128)S(1)} %collective-permute-done.2.refs_3_), channel_id=1, source_target_pairs={{0,1},{1,0},{2,3},{3,2},{4,5},{5,4},{6,7},{7,6},{8,9},{9,8},{10,11... | collective-permute-start | bytes 147464 | tf_op jit(solution)/shard_map/ppermute | solution.py:21
  10.4 4.0 %slice-start.1 = ((f32[48,3,3,3,384]{4,0,3,2,1:T(8,128)}), f32[48,1,3,3,384]{4,0,3,2,1:T(8,128)S(1)}, s32[]{:S(2)}) async-start(f32[48,3,3,3,384]{4,0,3,2,1:T(8,128)} %param.15), calls=%async_computation.1 | async-start | bytes 1327104 | tf_op jit(solution)/shard_map/slice | solution.py:306
  13.1 4.5 %collective-permute-start.7 = (f32[48,384]{1,0:T(8,128)S(1)}, f32[48,384]{1,0:T(8,128)S(1)}, u32[]{:S(2)}, u32[]{:S(2)}) collective-permute-start(f32[48,384]{1,0:T(8,128)S(1)} %get-tuple-element.27), channel_id=1, source_target_pairs={{0,64},{64,128},{128,192},{192,0},{1,65},{65,129},{129,193},{193,1... | collective-permute-start | bytes 221192 | tf_op jit(solution)/shard_map/ppermute | solution.py:39
  17.6 6.9 %collective-permute-start.8 = (f32[48,128]{1,0:T(8,128)S(1)}, f32[48,128]{1,0:T(8,128)S(1)}, u32[]{:S(2)}, u32[]{:S(2)}) collective-permute-start(f32[48,128]{1,0:T(8,128)S(1)} %get-tuple-element.54), channel_id=1, source_target_pairs={{0,8},{8,16},{16,24},{24,32},{32,40},{40,48},{48,56},{56,0},{1,9},... | collective-permute-start | bytes 73736 | tf_op jit(solution)/shard_map/ppermute | solution.py:39
  19.3 5.2 %collective-permute-start.9 = (f32[48,128]{1,0:T(8,128)S(1)}, f32[48,128]{1,0:T(8,128)S(1)}, u32[]{:S(2)}, u32[]{:S(2)}) collective-permute-start(f32[48,128]{1,0:T(8,128)S(1)} %get-tuple-element.55), channel_id=1, source_target_pairs={{0,56},{8,0},{16,8},{24,16},{32,24},{40,32},{48,40},{56,48},{1,57}... | collective-permute-start | bytes 73736 | tf_op jit(solution)/shard_map/ppermute | solution.py:39
  24.6 9.7 %collective-permute-start.10 = (f32[48,384]{1,0:T(8,128)S(1)}, f32[48,384]{1,0:T(8,128)S(1)}, u32[]{:S(2)}, u32[]{:S(2)}) collective-permute-start(f32[48,384]{1,0:T(8,128)S(1)} %pad_maximum_fusion.refs_0_), channel_id=1, source_target_pairs={{0,2},{1,3},{2,4},{3,5},{4,6},{5,7},{6,0},{7,1},{8,10},{9,11},{10,... | collective-permute-start | bytes 221192 | tf_op jit(solution)/shard_map/ppermute | solution.py:27
  25.4 9.0 %collective-permute-start.11 = (f32[48,384]{1,0:T(8,128)S(1)}, f32[48,384]{1,0:T(8,128)S(1)}, u32[]{:S(2)}, u32[]{:S(2)}) collective-permute-start(f32[48,384]{1,0:T(8,128)S(1)} %pad_maximum_fusion.refs_0_), channel_id=1, source_target_pairs={{0,4},{1,5},{2,6},{3,7},{4,0},{5,1},{6,2},{7,3},{8,12},{9,13},{10,... | collective-permute-start | bytes 221192 | tf_op jit(solution)/shard_map/ppermute | solution.py:27
  28.1 6.7 %collective-permute-start.12 = (f32[48,384]{1,0:T(8,128)S(1)}, f32[48,384]{1,0:T(8,128)S(1)}, u32[]{:S(2)}, u32[]{:S(2)}) collective-permute-start(f32[48,384]{1,0:T(8,128)S(1)} %pad_maximum_fusion.refs_0_), channel_id=1, source_target_pairs={{0,6},{1,7},{2,0},{3,1},{4,2},{5,3},{6,4},{7,5},{8,14},{9,15},{10,... | collective-permute-start | bytes 221192 | tf_op jit(solution)/shard_map/ppermute | solution.py:27
  31.6 4.7 %collective-permute-start.13 = (f32[48,384]{1,0:T(8,128)S(1)}, f32[48,384]{1,0:T(8,128)S(1)}, u32[]{:S(2)}, u32[]{:S(2)}) collective-permute-start(f32[48,384]{1,0:T(8,128)S(1)} %pad_maximum_fusion.refs_0_), channel_id=1, source_target_pairs={{0,1},{1,0},{2,3},{3,2},{4,5},{5,4},{6,7},{7,6},{8,9},{9,8},{10,11... | collective-permute-start | bytes 221192 | tf_op jit(solution)/shard_map/ppermute | solution.py:21
  34.3 1.9 %collective-permute-start.14 = (f32[48,384]{1,0:T(8,128)S(1)}, f32[48,384]{1,0:T(8,128)S(1)}, u32[]{:S(2)}, u32[]{:S(2)}) collective-permute-start(f32[48,384]{1,0:T(8,128)S(1)} %collective-permute-done.10.refs_1_), channel_id=1, source_target_pairs={{0,1},{1,0},{2,3},{3,2},{4,5},{5,4},{6,7},{7,6},{8,9},{9,8},{10,11... | collective-permute-start | bytes 221192 | tf_op jit(solution)/shard_map/ppermute | solution.py:21
  34.4 1.8 %collective-permute-start.15 = (f32[48,384]{1,0:T(8,128)S(1)}, f32[48,384]{1,0:T(8,128)S(1)}, u32[]{:S(2)}, u32[]{:S(2)}) collective-permute-start(f32[48,384]{1,0:T(8,128)S(1)} %collective-permute-done.11.refs_2_), channel_id=1, source_target_pairs={{0,1},{1,0},{2,3},{3,2},{4,5},{5,4},{6,7},{7,6},{8,9},{9,8},{10,11... | collective-permute-start | bytes 221192 | tf_op jit(solution)/shard_map/ppermute | solution.py:21
  34.8 1.5 %collective-permute-start.16 = (f32[48,384]{1,0:T(8,128)S(1)}, f32[48,384]{1,0:T(8,128)S(1)}, u32[]{:S(2)}, u32[]{:S(2)}) collective-permute-start(f32[48,384]{1,0:T(8,128)S(1)} %collective-permute-done.12.refs_3_), channel_id=1, source_target_pairs={{0,1},{1,0},{2,3},{3,2},{4,5},{5,4},{6,7},{7,6},{8,9},{9,8},{10,11... | collective-permute-start | bytes 221192 | tf_op jit(solution)/shard_map/ppermute | solution.py:21
  35.4 0.7 copy-start.6
  36.2 11.0 %copy-start.7 = (f32[384]{0:T(512)S(1)}, f32[384]{0:T(512)}, u32[]{:S(2)}) copy-start(f32[384]{0:T(512)} %param.20) | copy-start | bytes 4612
  36.3 19.5 %copy-start.2 = (f32[384,384]{1,0:T(8,128)S(1)}, f32[384,384]{1,0:T(8,128)}, u32[]{:S(2)}) copy-start(f32[384,384]{1,0:T(8,128)} %param.22) | copy-start | bytes 1769476
  38.3 4.0 %collective-permute-start.17 = (f32[48,128]{1,0:T(8,128)S(1)}, f32[48,128]{1,0:T(8,128)S(1)}, u32[]{:S(2)}, u32[]{:S(2)}) collective-permute-start(f32[48,128]{1,0:T(8,128)S(1)} %get-tuple-element.29), channel_id=1, source_target_pairs={{0,64},{64,128},{128,192},{192,0},{1,65},{65,129},{129,193},{193,1... | collective-permute-start | bytes 73736 | tf_op jit(solution)/shard_map/ppermute | solution.py:39
  38.4 3.9 %collective-permute-start.18 = (f32[48,128]{1,0:T(8,128)S(1)}, f32[48,128]{1,0:T(8,128)S(1)}, u32[]{:S(2)}, u32[]{:S(2)}) collective-permute-start(f32[48,128]{1,0:T(8,128)S(1)} %get-tuple-element.30), channel_id=1, source_target_pairs={{0,1},{1,0},{2,3},{3,2},{4,5},{5,4},{6,7},{7,6},{8,9},{9,8},{10,11... | collective-permute-start | bytes 73736 | tf_op jit(solution)/shard_map/ppermute | solution.py:21
  39.1 4.5 %collective-permute-start.19 = (f32[48,128]{1,0:T(8,128)S(1)}, f32[48,128]{1,0:T(8,128)S(1)}, u32[]{:S(2)}, u32[]{:S(2)}) collective-permute-start(f32[48,128]{1,0:T(8,128)S(1)} %get-tuple-element.31), channel_id=1, source_target_pairs={{0,65},{1,64},{2,67},{3,66},{4,69},{5,68},{6,71},{7,70},{64,129},{... | collective-permute-start | bytes 73736 | tf_op jit(solution)/shard_map/ppermute | solution.py:360
  43.6 4.2 %collective-permute-start.20 = (f32[96,128]{1,0:T(8,128)S(1)}, f32[96,128]{1,0:T(8,128)S(1)}, u32[]{:S(2)}, u32[]{:S(2)}) collective-permute-start(f32[96,128]{1,0:T(8,128)S(1)} %maximum_add_fusion.refs_0_), channel_id=1, source_target_pairs={{0,2},{1,3},{2,4},{3,5},{4,6},{5,7},{6,0},{7,1},{8,10},{9,11},{10,... | collective-permute-start | bytes 147464 | tf_op jit(solution)/shard_map/ppermute | solution.py:27
  44.6 4.6 %collective-permute-start.21 = (f32[96,128]{1,0:T(8,128)S(1)}, f32[96,128]{1,0:T(8,128)S(1)}, u32[]{:S(2)}, u32[]{:S(2)}) collective-permute-start(f32[96,128]{1,0:T(8,128)S(1)} %maximum_add_fusion.refs_0_), channel_id=1, source_target_pairs={{0,4},{1,5},{2,6},{3,7},{4,0},{5,1},{6,2},{7,3},{8,12},{9,13},{10,... | collective-permute-start | bytes 147464 | tf_op jit(solution)/shard_map/ppermute | solution.py:27
  46.2 3.5 %collective-permute-start.22 = (f32[96,128]{1,0:T(8,128)S(1)}, f32[96,128]{1,0:T(8,128)S(1)}, u32[]{:S(2)}, u32[]{:S(2)}) collective-permute-start(f32[96,128]{1,0:T(8,128)S(1)} %maximum_add_fusion.refs_0_), channel_id=1, source_target_pairs={{0,6},{1,7},{2,0},{3,1},{4,2},{5,3},{6,4},{7,5},{8,14},{9,15},{10,... | collective-permute-start | bytes 147464 | tf_op jit(solution)/shard_map/ppermute | solution.py:27
  49.7 21.8 %copy-start.3 = (f32[384,384]{1,0:T(8,128)S(1)}, f32[384,384]{1,0:T(8,128)}, u32[]{:S(2)}) copy-start(f32[384,384]{1,0:T(8,128)} %param.23) | copy-start | bytes 1769476
  49.7 21.8 %copy-start.4 = (f32[384,384]{1,0:T(8,128)S(1)}, f32[384,384]{1,0:T(8,128)}, u32[]{:S(2)}) copy-start(f32[384,384]{1,0:T(8,128)} %param.24) | copy-start | bytes 1769476
  50.5 8.8 %collective-permute-start.23 = (f32[384,128]{1,0:T(8,128)S(1)}, f32[384,128]{1,0:T(8,128)S(1)}, u32[]{:S(2)}, u32[]{:S(2)}) collective-permute-start(f32[384,128]{1,0:T(8,128)S(1)} %get-tuple-element.34.normed), channel_id=1, source_target_pairs={{32,0},{33,1},{42,2},{27,3},{52,4},{21,5},{30,6},{47,7},{40,8},{41... | collective-permute-start | bytes 589832 | tf_op jit(solution)/shard_map/ppermute | solution.py:388
  54.9 4.5 %collective-permute-start.24 = (f32[384,128]{1,0:T(8,128)S(1)}, f32[384,128]{1,0:T(8,128)S(1)}, u32[]{:S(2)}, u32[]{:S(2)}) collective-permute-start(f32[384,128]{1,0:T(8,128)S(1)} %get-tuple-element.34.normed), channel_id=1, source_target_pairs={{0,0},{1,1},{10,2},{59,3},{20,4},{53,5},{62,6},{15,7},{8,8},{9,9},... | collective-permute-start | bytes 589832 | tf_op jit(solution)/shard_map/ppermute | solution.py:388
  57.1 15.7 %copy-start.8 = (f32[384]{0:T(512)S(1)}, f32[384]{0:T(512)}, u32[]{:S(2)}) copy-start(f32[384]{0:T(512)} %param.25) | copy-start | bytes 4612
  61.1 11.7 %collective-permute-start.25 = (f32[32,512]{1,0:T(8,128)S(1)}, f32[32,512]{1,0:T(8,128)S(1)}, u32[]{:S(2)}, u32[]{:S(2)}) collective-permute-start(f32[32,512]{1,0:T(8,128)S(1)} %get-tuple-element.37), channel_id=1, source_target_pairs={{0,2},{1,3},{2,4},{3,5},{4,6},{5,7},{6,0},{7,1},{8,10},{9,11},{10,... | collective-permute-start | bytes 196616 | tf_op jit(solution)/shard_map/ppermute | solution.py:27
  67.5 7.9 %collective-permute-start.26 = (f32[32,512]{1,0:T(8,128)S(1)}, f32[32,512]{1,0:T(8,128)S(1)}, u32[]{:S(2)}, u32[]{:S(2)}) collective-permute-start(f32[32,512]{1,0:T(8,128)S(1)} %get-tuple-element.38), channel_id=1, source_target_pairs={{0,4},{1,5},{2,6},{3,7},{4,0},{5,1},{6,2},{7,3},{8,12},{9,13},{10,... | collective-permute-start | bytes 196616 | tf_op jit(solution)/shard_map/ppermute | solution.py:27
  71.5 3.8 %collective-permute-start.27 = (f32[32,512]{1,0:T(8,128)S(1)}, f32[32,512]{1,0:T(8,128)S(1)}, u32[]{:S(2)}, u32[]{:S(2)}) collective-permute-start(f32[32,512]{1,0:T(8,128)S(1)} %get-tuple-element.39), channel_id=1, source_target_pairs={{0,6},{1,7},{2,0},{3,1},{4,2},{5,3},{6,4},{7,5},{8,14},{9,15},{10,... | collective-permute-start | bytes 196616 | tf_op jit(solution)/shard_map/ppermute | solution.py:27
  76.4 1.6 %collective-permute-start.28 = (f32[4,4,384]{2,1,0:T(4,128)S(1)}, f32[4,4,384]{2,1,0:T(4,128)S(1)}, u32[]{:S(2)}, u32[]{:S(2)}) collective-permute-start(f32[4,4,384]{2,1,0:T(4,128)S(1)} %get-tuple-element.42), channel_id=1, source_target_pairs={{0,1},{1,0},{2,3},{3,2},{4,5},{5,4},{6,7},{7,6},{8,9},{9,8},{10,11... | collective-permute-start | bytes 73736 | tf_op jit(solution)/shard_map/ppermute | solution.py:21

commit v3 on v2

--- a/solution.py
+++ b/solution.py
@@ -63,10 +63,16 @@
 
 
 def product(wh, wl, xh, xl):
-    def dot(a, b):
-        return lax.dot_general(a, b, (((1,), (0,)), ((), ())), preferred_element_type=F32)
-
     return dot(wh, xh) + (dot(wh, xl) + dot(wl, xh))
+
+
+def dot(a, b, depth=0):
+    return lax.dot_general(a, b, (((1,), (depth,)), ((), ())), preferred_element_type=F32)
+
+
+def thrice(x, axis, left=False):
+    high, low = halves(x)
+    return jnp.concatenate([high, high, low] if left else [high, low, high], axis=axis)
 
 
 def activated(x, gain):
@@ -145,7 +151,7 @@
                 cells[pl.ds(pl.multiple_of(base + 8 * chip, 8), 8), :] = both[f, r]
     strip = cells[...].T
     strip_out[...] = strip
-    xh, xl = halves(activated(strip, gain[...]))
+    xh, xl = halves(activated(strip, gain[:, 0:1]))
     xh_out[...] = xh
     xl_out[...] = xl
     prod[...] = product(wh[...], wl[...], xh, xl)
@@ -172,7 +178,7 @@
         for core, piece in ((c, pieces[k]), (1 - c, pieces[CHIPS + k])):
             start = pl.multiple_of((2 * chip + core) * OUT, 8)
             inner[pl.ds(start, OUT), :] = piece[...]
-    act = activated(inner[...], gain[...])
+    act = activated(inner[...], gain[:, 1:2])
     top, mid, bottom = act[:, :128], act[:, 128:256], act[:, 256:]
     second_row = (lane_of((C, 128)) & 63) >= 32
     level = jnp.concatenate(
@@ -213,7 +219,7 @@
     frame = total[...] + one_frame(strip[:, :128], strip[:, 128:], at[3] == 1)
     blocked_out[...] = frame
     mean = jnp.mean(frame * frame, axis=0, keepdims=True)
-    normed_out[...] = frame * lax.rsqrt(mean + 1e-6) * gain[...]
+    normed_out[...] = frame * lax.rsqrt(mean + 1e-6) * gain[:, 2:3]
 
 
 def query_kernel(at, blocked, normed, w_score, queries_out, rest_out, cells):
@@ -237,17 +243,11 @@
     top = jnp.max(jnp.maximum(*scores), axis=1, keepdims=True)
     weights = [jnp.exp(s - top) for s in scores]
     denom = jnp.sum(weights[0] + weights[1], axis=1, keepdims=True)
-    accum = [
-        lax.dot_general(
-            p,
-            k[...],
-            (((1,), (1,)), ((), ())),
-            precision=lax.Precision.HIGHEST,
-            preferred_element_type=F32,
-        )
-        for p, k in zip(weights, (keys_a, keys_b))
-    ]
-    state[:, :C] = accum[0] + accum[1]
+    state[:, :C] = dot(
+        jnp.concatenate([thrice(p, 1, left=True) for p in weights], axis=1),
+        jnp.concatenate([thrice(k[...], 1) for k in (keys_a, keys_b)], axis=1),
+        depth=1,
+    )
     state[:, C:] = jnp.where(lane_of((128, 128)) < 64, top, denom)
     for k in range(CHIPS):
         chip = lax.rem(at[2] + k, CHIPS)
@@ -266,10 +266,8 @@
 
 def project_kernel(at, a, b, c, d, w_mixed, bias, rest, mine_out, other_out):
     mixed = merged([x[...] for x in (a, b, c, d)])
-    done = rest[...] + (
-        jnp.dot(mixed, w_mixed[...], precision=lax.Precision.HIGHEST, preferred_element_type=F32)
-        + bias[...]
-    )
+    projected = dot(thrice(mixed, 1, left=True), thrice(w_mixed[...], 0))
+    done = rest[...] + (projected + bias[...])
     done = done.reshape(4, 8, C)
     left, right = done[:, :4], done[:, 4:]
     mine_out[...] = jnp.where(at[3] == 0, left, right)
@@ -301,6 +299,7 @@
     wa = lax.axis_index("wa")
     at = jnp.stack([lax.axis_index("ta"), lax.axis_index("ha"), wa // 2, wa % 2]).astype(jnp.int32)
     column = lambda v: v.reshape(C, 1)
+    gains = jnp.stack([first_gain, second_gain, attn_gain], axis=1)
 
     first_w = split_weights(first_kernel[:, :2], (1, 2, 3, 0, 4))
     first_w_own = split_weights(first_kernel[:, 2:], (1, 2, 3, 0, 4))
@@ -319,7 +318,7 @@
         first_conv_kernel,
         [(OUT, 384), (OUT, 384), (C, 256), operand(C, 256), operand(C, 256)],
         *gathered(latents),
-        column(first_gain),
+        gains,
         *first_w,
         scratch=[pltpu.VMEM((256, C), F32), pltpu.VMEM((18 * OUT, 256), F32)],
         scalars=at,
@@ -349,7 +348,7 @@
         second_conv_kernel,
         [(OUT, 128)] * 4,
         *gathered(inner),
-        column(second_gain),
+        gains,
         *second_w,
         scratch=[pltpu.VMEM((C, 384), F32), pltpu.VMEM((9 * OUT, 256), F32)],
         scalars=at,
@@ -374,7 +373,7 @@
         change,
         *across_chips([change] * (CHIPS - 1)),
         strip,
-        column(attn_gain),
+        gains,
         scratch=[pltpu.VMEM((C, 128), F32)],
         scalars=at,
     )

time: 78.8 us -> 78.5 us (level)
  starting transfers between devices: 46.9 us -> 44 us
  waiting for transfers between devices: 13.2 us -> 14.7 us
  local copies, waits for them, and re-layouts: 5 us -> 6.46 us
    another operation x2 -> x6, local copies, waits for them, and re-layouts: 1.51 us -> 3.69 us  [the longest x4 2.18 us: per_device(): gains = jnp.stack([first_gain, second_gain, attn_gain], axis=1)]
    ppermute x10, starting transfers between devices: 9.45 us -> 7.43 us  [sibling(): return lax.ppermute(x, 'wa', [(i, i ^ 1) for i in range(2 * CHIPS)])]
    ppermute x12, starting transfers between devices: 24 us -> 23.1 us  [across_chips(): lax.ppermute(x, 'wa', [(i, (i + 2 * k) % n) for i in range(n)])]
  transfers between devices with their start and end apart: 29 -> 29, of which waited for: 12 -> 14; matrix products, arithmetic and copies ran while one was open for 10% -> 12% of each run, Pallas kernels for 2% -> 2%
where the time goes in v3:
time: 78.5 us; the launch traced here: 78.2 us
  starting transfers between devices  44 us (56%)
  waiting for transfers between devices  14.7 us (19%)
  Pallas kernels  8.8 us (11%)
  local copies, waits for them, and re-layouts  6.46 us (8%)
  matrix products  2.53 us (3%)
  other arithmetic  1.46 us (2%)
    ppermute x12, starting transfers between devices, across_chips(): lax.ppermute(x, 'wa', [(i, (i + 2 * k) % n) for i in range(n)])  23.1 us
    pallas_call x7, Pallas kernels, call(): pl.pallas_call(kernel, out_shape=outs, in_specs=in_specs, out_specs=[pl.B...  8.8 us
    ppermute x10, starting transfers between devices, sibling(): return lax.ppermute(x, 'wa', [(i, i ^ 1) for i in range(2 * CHIPS)])  7.43 us
    ppermute x4, starting transfers between devices, shifted(): return lax.ppermute(x, axis, [(i, (i + by) % n) for i in range(n)])  7.11 us
    ppermute x2, starting transfers between devices, per_device(): keys.append(lax.ppermute(normed, ('ha', 'wa'), pairs))  5.24 us
    ppermute x12, waiting for transfers between devices, across_chips(): lax.ppermute(x, 'wa', [(i, (i + 2 * k) % n) for i in range(n)])  5.23 us
    ppermute x4, waiting for transfers between devices, shifted(): return lax.ppermute(x, axis, [(i, (i + by) % n) for i in range(n)])  4.75 us
    transpose x1, local copies, waits for them, and re-layouts, split_weights(): w = jnp.transpose(kernel, order)  2.58 us
  transfers between devices with their start and end apart: 29, of which 14 were waited for; matrix products, arithmetic and copies ran while one was open for 12% of the time, Pallas kernels for 2%

profile of v3, /device:TPU:1, one launch (start us, length us, event | category | flops | bytes accessed | tf_op | source)
XLA Modules:
  0.0 78.2 jit_solution(5728552486495623602)
XLA Ops:
  0.0 2.1 %collective-permute-start = (f32[2,4,4,384]{3,2,1,0:T(4,128)}, f32[2,4,4,384]{3,2,1,0:T(4,128)S(1)}, u32[]{:S(2)}, u32[]{:S(2)}) collective-permute-start(f32[2,4,4,384]{3,2,1,0:T(4,128)} %refs_0_.1), channel_id=1, source_target_pairs={{0,2},{1,3},{2,4},{3,5},{4,6},{5,7},{6,0},{7,1},{8,10},{9,11},{10,... | collective-permute-start | bytes 147464 | tf_op jit(solution)/shard_map/ppermute | solution.py:27
  2.1 2.6 %collective-permute-start.1 = (f32[2,4,4,384]{3,2,1,0:T(4,128)}, f32[2,4,4,384]{3,2,1,0:T(4,128)S(1)}, u32[]{:S(2)}, u32[]{:S(2)}) collective-permute-start(f32[2,4,4,384]{3,2,1,0:T(4,128)} %refs_0_.1), channel_id=1, source_target_pairs={{0,4},{1,5},{2,6},{3,7},{4,0},{5,1},{6,2},{7,3},{8,12},{9,13},{10,... | collective-permute-start | bytes 147464 | tf_op jit(solution)/shard_map/ppermute | solution.py:27
  4.8 1.1 %collective-permute-start.2 = (f32[2,4,4,384]{3,2,1,0:T(4,128)}, f32[2,4,4,384]{3,2,1,0:T(4,128)S(1)}, u32[]{:S(2)}, u32[]{:S(2)}) collective-permute-start(f32[2,4,4,384]{3,2,1,0:T(4,128)} %refs_0_.1), channel_id=1, source_target_pairs={{0,6},{1,7},{2,0},{3,1},{4,2},{5,3},{6,4},{7,5},{8,14},{9,15},{10,... | collective-permute-start | bytes 147464 | tf_op jit(solution)/shard_map/ppermute | solution.py:27
  5.8 1.5 %collective-permute-start.3 = (f32[2,4,4,384]{3,2,1,0:T(4,128)}, f32[2,4,4,384]{3,2,1,0:T(4,128)S(1)}, u32[]{:S(2)}, u32[]{:S(2)}) collective-permute-start(f32[2,4,4,384]{3,2,1,0:T(4,128)} %refs_0_.1), channel_id=1, source_target_pairs={{0,1},{1,0},{2,3},{3,2},{4,5},{5,4},{6,7},{7,6},{8,9},{9,8},{10,11... | collective-permute-start | bytes 147464 | tf_op jit(solution)/shard_map/ppermute | solution.py:21
  7.3 0.7 stack.41
  8.0 0.7 stack.42
  8.7 0.7 stack.43
  9.7 0.5 collective-permute-start.5
  11.5 1.9 %shard_map.127 = (f32[48,384]{1,0:T(8,128)S(1)}, f32[48,384]{1,0:T(8,128)S(1)}, f32[384,256]{1,0:T(8,128)S(1)}, bf16[384,256]{1,0:T(8,128)(2,1)S(1)}, bf16[384,256]{1,0:T(8,128)(2,1)S(1)}) custom-call(s32[4]{0:T(128)S(1)} %pad_add_fusion.at, f32[2,4,4,384]{3,2,1,0:T(4,128)S(1)} %copy-done.1, f32[2,4,4,384]{3,2,1,0:T(4,128)S(1)} %collective-permute-done.refs_1_, ...), custom_call_target="tpu_custom_call" | custom-call | flops 1000000000 | bytes 2658816 | tf_op jit(solution)/shard_map/pallas_call | solution.py:49
  13.4 1.3 %collective-permute-start.7 = (f32[48,384]{1,0:T(8,128)S(1)}, f32[48,384]{1,0:T(8,128)S(1)}, u32[]{:S(2)}, u32[]{:S(2)}) collective-permute-start(f32[48,384]{1,0:T(8,128)S(1)} %get-tuple-element.27), channel_id=1, source_target_pairs={{0,64},{64,128},{128,192},{192,0},{1,65},{65,129},{129,193},{193,1... | collective-permute-start | bytes 221192 | tf_op jit(solution)/shard_map/ppermute | solution.py:39
  14.8 0.6 shard_map.128
  15.4 3.0 %collective-permute-done.7 = f32[48,384]{1,0:T(8,128)S(1)} collective-permute-done((f32[48,384]{1,0:T(8,128)S(1)}, f32[48,384]{1,0:T(8,128)S(1)}, u32[]{:S(2)}, u32[]{:S(2)}) %collective-permute-start.7) | collective-permute-done | bytes 73760 | tf_op jit(solution)/shard_map/ppermute | solution.py:39
  18.4 1.7 %collective-permute-start.8 = (f32[48,128]{1,0:T(8,128)S(1)}, f32[48,128]{1,0:T(8,128)S(1)}, u32[]{:S(2)}, u32[]{:S(2)}) collective-permute-start(f32[48,128]{1,0:T(8,128)S(1)} %get-tuple-element.54), channel_id=1, source_target_pairs={{0,8},{8,16},{16,24},{24,32},{32,40},{40,48},{48,56},{56,0},{1,9},... | collective-permute-start | bytes 73736 | tf_op jit(solution)/shard_map/ppermute | solution.py:39
  20.1 4.0 %collective-permute-start.9 = (f32[48,128]{1,0:T(8,128)S(1)}, f32[48,128]{1,0:T(8,128)S(1)}, u32[]{:S(2)}, u32[]{:S(2)}) collective-permute-start(f32[48,128]{1,0:T(8,128)S(1)} %get-tuple-element.55), channel_id=1, source_target_pairs={{0,56},{8,0},{16,8},{24,16},{32,24},{40,32},{48,40},{56,48},{1,57}... | collective-permute-start | bytes 73736 | tf_op jit(solution)/shard_map/ppermute | solution.py:39
  24.2 0.8 dynamic-slice.6
  25.9 2.3 %collective-permute-start.11 = (f32[48,384]{1,0:T(8,128)S(1)}, f32[48,384]{1,0:T(8,128)S(1)}, u32[]{:S(2)}, u32[]{:S(2)}) collective-permute-start(f32[48,384]{1,0:T(8,128)S(1)} %pad_maximum_fusion.refs_0_), channel_id=1, source_target_pairs={{0,4},{1,5},{2,6},{3,7},{4,0},{5,1},{6,2},{7,3},{8,12},{9,13},{10,... | collective-permute-start | bytes 221192 | tf_op jit(solution)/shard_map/ppermute | solution.py:27
  28.1 0.7 collective-permute-start.12
  28.8 2.6 %copy.20 = f32[3,3,48,3,384]{4,3,2,1,0:T(4,128)S(1)} copy(f32[3,3,48,3,384]{4,2,1,3,0:T(8,128)} %bitcast.28) | data formatting | bytes 3981312 | tf_op jit(solution)/shard_map/transpose | solution.py:278
  31.6 2.8 %collective-permute-start.13 = (f32[48,384]{1,0:T(8,128)S(1)}, f32[48,384]{1,0:T(8,128)S(1)}, u32[]{:S(2)}, u32[]{:S(2)}) collective-permute-start(f32[48,384]{1,0:T(8,128)S(1)} %pad_maximum_fusion.refs_0_), channel_id=1, source_target_pairs={{0,1},{1,0},{2,3},{3,2},{4,5},{5,4},{6,7},{7,6},{8,9},{9,8},{10,11... | collective-permute-start | bytes 221192 | tf_op jit(solution)/shard_map/ppermute | solution.py:21
  34.8 0.6 collective-permute-start.16
  35.7 0.6 collective-permute-done.16.refs_7_
  36.3 2.0 %shard_map.129 = (f32[48,128]{1,0:T(8,128)S(1)}, f32[48,128]{1,0:T(8,128)S(1)}, f32[48,128]{1,0:T(8,128)S(1)}, f32[48,128]{1,0:T(8,128)S(1)}) custom-call(s32[4]{0:T(128)S(1)} %pad_add_fusion.at, f32[48,384]{1,0:T(8,128)S(1)} %pad_maximum_fusion.refs_0_, f32[48,384]{1,0:T(8,128)S(1)} %collective-permute-done.10.refs_1_, ...), custom_call_target="tpu_custom_call" | custom-call | flops 1000000000 | bytes 2683392 | tf_op jit(solution)/shard_map/pallas_call | solution.py:49
  38.4 0.6 collective-permute-start.18
  39.0 1.1 %collective-permute-start.19 = (f32[48,128]{1,0:T(8,128)S(1)}, f32[48,128]{1,0:T(8,128)S(1)}, u32[]{:S(2)}, u32[]{:S(2)}) collective-permute-start(f32[48,128]{1,0:T(8,128)S(1)} %get-tuple-element.31), channel_id=1, source_target_pairs={{0,65},{1,64},{2,67},{3,66},{4,69},{5,68},{6,71},{7,70},{64,129},{... | collective-permute-start | bytes 73736 | tf_op jit(solution)/shard_map/ppermute | solution.py:359
  40.1 0.8 dynamic-slice.7
  40.9 1.4 %collective-permute-done.17 = f32[48,128]{1,0:T(8,128)S(1)} collective-permute-done((f32[48,128]{1,0:T(8,128)S(1)}, f32[48,128]{1,0:T(8,128)S(1)}, u32[]{:S(2)}, u32[]{:S(2)}) %collective-permute-start.17) | collective-permute-done | bytes 24608 | tf_op jit(solution)/shard_map/ppermute | solution.py:39
  42.3 1.2 %collective-permute-done.19 = f32[48,128]{1,0:T(8,128)S(1)} collective-permute-done((f32[48,128]{1,0:T(8,128)S(1)}, f32[48,128]{1,0:T(8,128)S(1)}, u32[]{:S(2)}, u32[]{:S(2)}) %collective-permute-start.19) | collective-permute-done | bytes 24608 | tf_op jit(solution)/shard_map/ppermute | solution.py:359
  43.6 1.0 %collective-permute-start.20 = (f32[96,128]{1,0:T(8,128)S(1)}, f32[96,128]{1,0:T(8,128)S(1)}, u32[]{:S(2)}, u32[]{:S(2)}) collective-permute-start(f32[96,128]{1,0:T(8,128)S(1)} %maximum_add_fusion.refs_0_), channel_id=1, source_target_pairs={{0,2},{1,3},{2,4},{3,5},{4,6},{5,7},{6,0},{7,1},{8,10},{9,11},{10,... | collective-permute-start | bytes 147464 | tf_op jit(solution)/shard_map/ppermute | solution.py:27
  44.6 1.8 %collective-permute-start.21 = (f32[96,128]{1,0:T(8,128)S(1)}, f32[96,128]{1,0:T(8,128)S(1)}, u32[]{:S(2)}, u32[]{:S(2)}) collective-permute-start(f32[96,128]{1,0:T(8,128)S(1)} %maximum_add_fusion.refs_0_), channel_id=1, source_target_pairs={{0,4},{1,5},{2,6},{3,7},{4,0},{5,1},{6,2},{7,3},{8,12},{9,13},{10,... | collective-permute-start | bytes 147464 | tf_op jit(solution)/shard_map/ppermute | solution.py:27
  46.4 0.8 %collective-permute-start.22 = (f32[96,128]{1,0:T(8,128)S(1)}, f32[96,128]{1,0:T(8,128)S(1)}, u32[]{:S(2)}, u32[]{:S(2)}) collective-permute-start(f32[96,128]{1,0:T(8,128)S(1)} %maximum_add_fusion.refs_0_), channel_id=1, source_target_pairs={{0,6},{1,7},{2,0},{3,1},{4,2},{5,3},{6,4},{7,5},{8,14},{9,15},{10,... | collective-permute-start | bytes 147464 | tf_op jit(solution)/shard_map/ppermute | solution.py:27
  47.2 0.7 collective-permute-done.20.refs_1_
  47.8 1.4 %collective-permute-done.21.refs_2_ = f32[96,128]{1,0:T(8,128)S(1)} collective-permute-done((f32[96,128]{1,0:T(8,128)S(1)}, f32[96,128]{1,0:T(8,128)S(1)}, u32[]{:S(2)}, u32[]{:S(2)}) %collective-permute-start.21) | collective-permute-done | bytes 49184 | tf_op jit(solution)/shard_map/ppermute | solution.py:27
  49.2 0.7 collective-permute-done.22.refs_3_
  49.9 0.8 shard_map.130
  50.7 4.4 %collective-permute-start.23 = (f32[384,128]{1,0:T(8,128)S(1)}, f32[384,128]{1,0:T(8,128)S(1)}, u32[]{:S(2)}, u32[]{:S(2)}) collective-permute-start(f32[384,128]{1,0:T(8,128)S(1)} %get-tuple-element.34.normed), channel_id=1, source_target_pairs={{32,0},{33,1},{42,2},{27,3},{52,4},{21,5},{30,6},{47,7},{40,8},{41... | collective-permute-start | bytes 589832 | tf_op jit(solution)/shard_map/ppermute | solution.py:387
  55.0 0.9 %collective-permute-start.24 = (f32[384,128]{1,0:T(8,128)S(1)}, f32[384,128]{1,0:T(8,128)S(1)}, u32[]{:S(2)}, u32[]{:S(2)}) collective-permute-start(f32[384,128]{1,0:T(8,128)S(1)} %get-tuple-element.34.normed), channel_id=1, source_target_pairs={{0,0},{1,1},{10,2},{59,3},{20,4},{53,5},{62,6},{15,7},{8,8},{9,9},... | collective-permute-start | bytes 589832 | tf_op jit(solution)/shard_map/ppermute | solution.py:387
  55.9 1.3 %convolution_multiply_fusion.w_score = f32[384,384]{1,0:T(8,128)S(1)} fusion(f32[384,384]{1,0:T(8,128)S(1)} %copy-done, f32[384,384]{1,0:T(8,128)S(1)} %copy-done.2), kind=kOutput, calls=%fused_computation.6 | convolution fusion | flops 679624704 | bytes 1769472 | tf_op jit(solution)/shard_map/dot_general | solution.py:307
  57.2 1.1 %shard_map.131 = (f32[128,384]{1,0:T(8,128)S(1)}, f32[32,384]{1,0:T(8,128)S(1)}) custom-call(s32[4]{0:T(128)S(1)} %pad_add_fusion.at, f32[384,128]{1,0:T(8,128)S(1)} %get-tuple-element.33.blocked, f32[384,128]{1,0:T(8,128)S(1)} %get-tuple-element.34.normed, f32[384,384]{1,0:T(8,128)S(1)} %convolution_multiply_fusion.w_score), custom_call_target="tpu_custom_call" | custom-call | flops 1000000 | bytes 1228800 | tf_op jit(solution)/shard_map/pallas_call | solution.py:49
  58.3 1.2 %collective-permute-done.23.keys_a = f32[384,128]{1,0:T(8,128)S(1)} collective-permute-done((f32[384,128]{1,0:T(8,128)S(1)}, f32[384,128]{1,0:T(8,128)S(1)}, u32[]{:S(2)}, u32[]{:S(2)}) %collective-permute-start.23) | collective-permute-done | bytes 196640 | tf_op jit(solution)/shard_map/ppermute | solution.py:387
  59.5 1.4 %shard_map.132 = (f32[32,512]{1,0:T(8,128)S(1)}, f32[32,512]{1,0:T(8,128)S(1)}, f32[32,512]{1,0:T(8,128)S(1)}, f32[32,512]{1,0:T(8,128)S(1)}) custom-call(s32[4]{0:T(128)S(1)} %pad_add_fusion.at, f32[128,384]{1,0:T(8,128)S(1)} %get-tuple-element.35.queries, f32[384,128]{1,0:T(8,128)S(1)} %collective-permute-done.23.keys_a, ...), custom_call_target="tpu_custom_call" | custom-call | flops 1000000 | bytes 851968 | tf_op jit(solution)/shard_map/pallas_call | solution.py:49
  61.0 6.2 %collective-permute-start.25 = (f32[32,512]{1,0:T(8,128)S(1)}, f32[32,512]{1,0:T(8,128)S(1)}, u32[]{:S(2)}, u32[]{:S(2)}) collective-permute-start(f32[32,512]{1,0:T(8,128)S(1)} %get-tuple-element.37), channel_id=1, source_target_pairs={{0,2},{1,3},{2,4},{3,5},{4,6},{5,7},{6,0},{7,1},{8,10},{9,11},{10,... | collective-permute-start | bytes 196616 | tf_op jit(solution)/shard_map/ppermute | solution.py:27
  67.2 4.0 %collective-permute-start.26 = (f32[32,512]{1,0:T(8,128)S(1)}, f32[32,512]{1,0:T(8,128)S(1)}, u32[]{:S(2)}, u32[]{:S(2)}) collective-permute-start(f32[32,512]{1,0:T(8,128)S(1)} %get-tuple-element.38), channel_id=1, source_target_pairs={{0,4},{1,5},{2,6},{3,7},{4,0},{5,1},{6,2},{7,3},{8,12},{9,13},{10,... | collective-permute-start | bytes 196616 | tf_op jit(solution)/shard_map/ppermute | solution.py:27
  71.2 1.3 %fusion.4.w_mixed = f32[384,384]{1,0:T(8,128)S(1)} fusion(f32[384,384]{1,0:T(8,128)S(1)} %copy-done.3, f32[384,384]{1,0:T(8,128)S(1)} %copy-done.4), kind=kOutput, calls=%fused_computation.29 | convolution fusion | flops 679477248 | bytes 1769472 | tf_op jit(solution)/shard_map/dot_general | solution.py:314
  72.5 2.5 %collective-permute-done.26.c = f32[32,512]{1,0:T(8,128)S(1)} collective-permute-done((f32[32,512]{1,0:T(8,128)S(1)}, f32[32,512]{1,0:T(8,128)S(1)}, u32[]{:S(2)}, u32[]{:S(2)}) %collective-permute-start.26) | collective-permute-done | bytes 65568 | tf_op jit(solution)/shard_map/ppermute | solution.py:27
  75.0 0.9 %shard_map.133 = (f32[4,4,384]{2,1,0:T(4,128)S(1)}, f32[4,4,384]{2,1,0:T(4,128)S(1)}) custom-call(s32[4]{0:T(128)S(1)} %pad_add_fusion.at, f32[32,512]{1,0:T(8,128)S(1)} %get-tuple-element.36.a, f32[32,512]{1,0:T(8,128)S(1)} %collective-permute-done.25.b, f32[32,512]{1,0:T(8,128)S(1)} %collective-permute-done.26.c, f32[32,512]{1,0:T(8,128)S(1)} %collective-permute-done.27.d, ...), custom_call_target="tpu_custom_call" | custom-call | flops 1000000 | bytes 951808 | tf_op jit(solution)/shard_map/pallas_call | solution.py:49
  76.0 0.8 collective-permute-start.28
  76.7 0.8 %collective-permute-done.28 = f32[4,4,384]{2,1,0:T(4,128)S(1)} collective-permute-done((f32[4,4,384]{2,1,0:T(4,128)S(1)}, f32[4,4,384]{2,1,0:T(4,128)S(1)}, u32[]{:S(2)}, u32[]{:S(2)}) %collective-permute-start.28) | collective-permute-done | bytes 24608 | tf_op jit(solution)/shard_map/ppermute | solution.py:21
  77.6 0.6 pad_maximum_fusion.1
  (58 shorter events, 3.8 us)
Async XLA Ops:
  0.0 55.9 %copy-start = (f32[384,384]{1,0:T(8,128)S(1)}, f32[384,384]{1,0:T(8,128)}, u32[]{:S(2)}) copy-start(f32[384,384]{1,0:T(8,128)} %param.21) | copy-start | bytes 1769476
  0.0 9.4 %slice-start = ((f32[48,3,3,3,384]{4,0,3,2,1:T(8,128)}), f32[48,2,3,3,384]{4,0,3,2,1:T(8,128)S(1)}, s32[]{:S(2)}) async-start(f32[48,3,3,3,384]{4,0,3,2,1:T(8,128)} %param.15), calls=%async_computation | async-start | bytes 2654208 | tf_op jit(solution)/shard_map/slice | solution.py:304
  0.0 9.6 %collective-permute-start = (f32[2,4,4,384]{3,2,1,0:T(4,128)}, f32[2,4,4,384]{3,2,1,0:T(4,128)S(1)}, u32[]{:S(2)}, u32[]{:S(2)}) collective-permute-start(f32[2,4,4,384]{3,2,1,0:T(4,128)} %refs_0_.1), channel_id=1, source_target_pairs={{0,2},{1,3},{2,4},{3,5},{4,6},{5,7},{6,0},{7,1},{8,10},{9,11},{10,... | collective-permute-start | bytes 147464 | tf_op jit(solution)/shard_map/ppermute | solution.py:27
  2.1 7.6 %collective-permute-start.1 = (f32[2,4,4,384]{3,2,1,0:T(4,128)}, f32[2,4,4,384]{3,2,1,0:T(4,128)S(1)}, u32[]{:S(2)}, u32[]{:S(2)}) collective-permute-start(f32[2,4,4,384]{3,2,1,0:T(4,128)} %refs_0_.1), channel_id=1, source_target_pairs={{0,4},{1,5},{2,6},{3,7},{4,0},{5,1},{6,2},{7,3},{8,12},{9,13},{10,... | collective-permute-start | bytes 147464 | tf_op jit(solution)/shard_map/ppermute | solution.py:27
  4.8 5.5 %collective-permute-start.2 = (f32[2,4,4,384]{3,2,1,0:T(4,128)}, f32[2,4,4,384]{3,2,1,0:T(4,128)S(1)}, u32[]{:S(2)}, u32[]{:S(2)}) collective-permute-start(f32[2,4,4,384]{3,2,1,0:T(4,128)} %refs_0_.1), channel_id=1, source_target_pairs={{0,6},{1,7},{2,0},{3,1},{4,2},{5,3},{6,4},{7,5},{8,14},{9,15},{10,... | collective-permute-start | bytes 147464 | tf_op jit(solution)/shard_map/ppermute | solution.py:27
  5.8 4.8 %collective-permute-start.3 = (f32[2,4,4,384]{3,2,1,0:T(4,128)}, f32[2,4,4,384]{3,2,1,0:T(4,128)S(1)}, u32[]{:S(2)}, u32[]{:S(2)}) collective-permute-start(f32[2,4,4,384]{3,2,1,0:T(4,128)} %refs_0_.1), channel_id=1, source_target_pairs={{0,1},{1,0},{2,3},{3,2},{4,5},{5,4},{6,7},{7,6},{8,9},{9,8},{10,11... | collective-permute-start | bytes 147464 | tf_op jit(solution)/shard_map/ppermute | solution.py:21
  9.4 2.1 %copy-start.1 = (f32[2,4,4,384]{3,2,1,0:T(4,128)S(1)}, f32[2,4,4,384]{3,2,1,0:T(4,128)}, u32[]{:S(2)}) copy-start(f32[2,4,4,384]{3,2,1,0:T(4,128)} %refs_0_.1) | copy-start | bytes 147460
  9.6 1.3 %collective-permute-start.4 = (f32[2,4,4,384]{3,2,1,0:T(4,128)S(1)}, f32[2,4,4,384]{3,2,1,0:T(4,128)S(1)}, u32[]{:S(2)}, u32[]{:S(2)}) collective-permute-start(f32[2,4,4,384]{3,2,1,0:T(4,128)S(1)} %collective-permute-done.refs_1_), channel_id=1, source_target_pairs={{0,1},{1,0},{2,3},{3,2},{4,5},{5,4},{6,7},{7,6},{8,9},{9,8},{10,11... | collective-permute-start | bytes 147464 | tf_op jit(solution)/shard_map/ppermute | solution.py:21
  9.7 1.4 %collective-permute-start.5 = (f32[2,4,4,384]{3,2,1,0:T(4,128)S(1)}, f32[2,4,4,384]{3,2,1,0:T(4,128)S(1)}, u32[]{:S(2)}, u32[]{:S(2)}) collective-permute-start(f32[2,4,4,384]{3,2,1,0:T(4,128)S(1)} %collective-permute-done.1.refs_2_), channel_id=1, source_target_pairs={{0,1},{1,0},{2,3},{3,2},{4,5},{5,4},{6,7},{7,6},{8,9},{9,8},{10,11... | collective-permute-start | bytes 147464 | tf_op jit(solution)/shard_map/ppermute | solution.py:21
  10.2 1.2 %collective-permute-start.6 = (f32[2,4,4,384]{3,2,1,0:T(4,128)S(1)}, f32[2,4,4,384]{3,2,1,0:T(4,128)S(1)}, u32[]{:S(2)}, u32[]{:S(2)}) collective-permute-start(f32[2,4,4,384]{3,2,1,0:T(4,128)S(1)} %collective-permute-done.2.refs_3_), channel_id=1, source_target_pairs={{0,1},{1,0},{2,3},{3,2},{4,5},{5,4},{6,7},{7,6},{8,9},{9,8},{10,11... | collective-permute-start | bytes 147464 | tf_op jit(solution)/shard_map/ppermute | solution.py:21
  10.6 4.1 %slice-start.1 = ((f32[48,3,3,3,384]{4,0,3,2,1:T(8,128)}), f32[48,1,3,3,384]{4,0,3,2,1:T(8,128)S(1)}, s32[]{:S(2)}) async-start(f32[48,3,3,3,384]{4,0,3,2,1:T(8,128)} %param.15), calls=%async_computation.1 | async-start | bytes 1327104 | tf_op jit(solution)/shard_map/slice | solution.py:305
  13.4 5.0 %collective-permute-start.7 = (f32[48,384]{1,0:T(8,128)S(1)}, f32[48,384]{1,0:T(8,128)S(1)}, u32[]{:S(2)}, u32[]{:S(2)}) collective-permute-start(f32[48,384]{1,0:T(8,128)S(1)} %get-tuple-element.27), channel_id=1, source_target_pairs={{0,64},{64,128},{128,192},{192,0},{1,65},{65,129},{129,193},{193,1... | collective-permute-start | bytes 221192 | tf_op jit(solution)/shard_map/ppermute | solution.py:39
  18.4 6.9 %collective-permute-start.8 = (f32[48,128]{1,0:T(8,128)S(1)}, f32[48,128]{1,0:T(8,128)S(1)}, u32[]{:S(2)}, u32[]{:S(2)}) collective-permute-start(f32[48,128]{1,0:T(8,128)S(1)} %get-tuple-element.54), channel_id=1, source_target_pairs={{0,8},{8,16},{16,24},{24,32},{32,40},{40,48},{48,56},{56,0},{1,9},... | collective-permute-start | bytes 73736 | tf_op jit(solution)/shard_map/ppermute | solution.py:39
  20.1 5.2 %collective-permute-start.9 = (f32[48,128]{1,0:T(8,128)S(1)}, f32[48,128]{1,0:T(8,128)S(1)}, u32[]{:S(2)}, u32[]{:S(2)}) collective-permute-start(f32[48,128]{1,0:T(8,128)S(1)} %get-tuple-element.55), channel_id=1, source_target_pairs={{0,56},{8,0},{16,8},{24,16},{32,24},{40,32},{48,40},{56,48},{1,57}... | collective-permute-start | bytes 73736 | tf_op jit(solution)/shard_map/ppermute | solution.py:39
  25.4 8.9 %collective-permute-start.10 = (f32[48,384]{1,0:T(8,128)S(1)}, f32[48,384]{1,0:T(8,128)S(1)}, u32[]{:S(2)}, u32[]{:S(2)}) collective-permute-start(f32[48,384]{1,0:T(8,128)S(1)} %pad_maximum_fusion.refs_0_), channel_id=1, source_target_pairs={{0,2},{1,3},{2,4},{3,5},{4,6},{5,7},{6,0},{7,1},{8,10},{9,11},{10,... | collective-permute-start | bytes 221192 | tf_op jit(solution)/shard_map/ppermute | solution.py:27
  25.9 8.6 %collective-permute-start.11 = (f32[48,384]{1,0:T(8,128)S(1)}, f32[48,384]{1,0:T(8,128)S(1)}, u32[]{:S(2)}, u32[]{:S(2)}) collective-permute-start(f32[48,384]{1,0:T(8,128)S(1)} %pad_maximum_fusion.refs_0_), channel_id=1, source_target_pairs={{0,4},{1,5},{2,6},{3,7},{4,0},{5,1},{6,2},{7,3},{8,12},{9,13},{10,... | collective-permute-start | bytes 221192 | tf_op jit(solution)/shard_map/ppermute | solution.py:27
  28.1 6.7 %collective-permute-start.12 = (f32[48,384]{1,0:T(8,128)S(1)}, f32[48,384]{1,0:T(8,128)S(1)}, u32[]{:S(2)}, u32[]{:S(2)}) collective-permute-start(f32[48,384]{1,0:T(8,128)S(1)} %pad_maximum_fusion.refs_0_), channel_id=1, source_target_pairs={{0,6},{1,7},{2,0},{3,1},{4,2},{5,3},{6,4},{7,5},{8,14},{9,15},{10,... | collective-permute-start | bytes 221192 | tf_op jit(solution)/shard_map/ppermute | solution.py:27
  31.6 4.1 %collective-permute-start.13 = (f32[48,384]{1,0:T(8,128)S(1)}, f32[48,384]{1,0:T(8,128)S(1)}, u32[]{:S(2)}, u32[]{:S(2)}) collective-permute-start(f32[48,384]{1,0:T(8,128)S(1)} %pad_maximum_fusion.refs_0_), channel_id=1, source_target_pairs={{0,1},{1,0},{2,3},{3,2},{4,5},{5,4},{6,7},{7,6},{8,9},{9,8},{10,11... | collective-permute-start | bytes 221192 | tf_op jit(solution)/shard_map/ppermute | solution.py:21
  34.3 1.4 %collective-permute-start.14 = (f32[48,384]{1,0:T(8,128)S(1)}, f32[48,384]{1,0:T(8,128)S(1)}, u32[]{:S(2)}, u32[]{:S(2)}) collective-permute-start(f32[48,384]{1,0:T(8,128)S(1)} %collective-permute-done.10.refs_1_), channel_id=1, source_target_pairs={{0,1},{1,0},{2,3},{3,2},{4,5},{5,4},{6,7},{7,6},{8,9},{9,8},{10,11... | collective-permute-start | bytes 221192 | tf_op jit(solution)/shard_map/ppermute | solution.py:21
  34.4 1.3 %collective-permute-start.15 = (f32[48,384]{1,0:T(8,128)S(1)}, f32[48,384]{1,0:T(8,128)S(1)}, u32[]{:S(2)}, u32[]{:S(2)}) collective-permute-start(f32[48,384]{1,0:T(8,128)S(1)} %collective-permute-done.11.refs_2_), channel_id=1, source_target_pairs={{0,1},{1,0},{2,3},{3,2},{4,5},{5,4},{6,7},{7,6},{8,9},{9,8},{10,11... | collective-permute-start | bytes 221192 | tf_op jit(solution)/shard_map/ppermute | solution.py:21
  34.8 1.5 %collective-permute-start.16 = (f32[48,384]{1,0:T(8,128)S(1)}, f32[48,384]{1,0:T(8,128)S(1)}, u32[]{:S(2)}, u32[]{:S(2)}) collective-permute-start(f32[48,384]{1,0:T(8,128)S(1)} %collective-permute-done.12.refs_3_), channel_id=1, source_target_pairs={{0,1},{1,0},{2,3},{3,2},{4,5},{5,4},{6,7},{7,6},{8,9},{9,8},{10,11... | collective-permute-start | bytes 221192 | tf_op jit(solution)/shard_map/ppermute | solution.py:21
  36.3 19.6 %copy-start.2 = (f32[384,384]{1,0:T(8,128)S(1)}, f32[384,384]{1,0:T(8,128)}, u32[]{:S(2)}) copy-start(f32[384,384]{1,0:T(8,128)} %param.22) | copy-start | bytes 1769476
  38.3 4.0 %collective-permute-start.17 = (f32[48,128]{1,0:T(8,128)S(1)}, f32[48,128]{1,0:T(8,128)S(1)}, u32[]{:S(2)}, u32[]{:S(2)}) collective-permute-start(f32[48,128]{1,0:T(8,128)S(1)} %get-tuple-element.29), channel_id=1, source_target_pairs={{0,64},{64,128},{128,192},{192,0},{1,65},{65,129},{129,193},{193,1... | collective-permute-start | bytes 73736 | tf_op jit(solution)/shard_map/ppermute | solution.py:39
  38.4 3.9 %collective-permute-start.18 = (f32[48,128]{1,0:T(8,128)S(1)}, f32[48,128]{1,0:T(8,128)S(1)}, u32[]{:S(2)}, u32[]{:S(2)}) collective-permute-start(f32[48,128]{1,0:T(8,128)S(1)} %get-tuple-element.30), channel_id=1, source_target_pairs={{0,1},{1,0},{2,3},{3,2},{4,5},{5,4},{6,7},{7,6},{8,9},{9,8},{10,11... | collective-permute-start | bytes 73736 | tf_op jit(solution)/shard_map/ppermute | solution.py:21
  39.0 4.5 %collective-permute-start.19 = (f32[48,128]{1,0:T(8,128)S(1)}, f32[48,128]{1,0:T(8,128)S(1)}, u32[]{:S(2)}, u32[]{:S(2)}) collective-permute-start(f32[48,128]{1,0:T(8,128)S(1)} %get-tuple-element.31), channel_id=1, source_target_pairs={{0,65},{1,64},{2,67},{3,66},{4,69},{5,68},{6,71},{7,70},{64,129},{... | collective-permute-start | bytes 73736 | tf_op jit(solution)/shard_map/ppermute | solution.py:359
  43.6 4.2 %collective-permute-start.20 = (f32[96,128]{1,0:T(8,128)S(1)}, f32[96,128]{1,0:T(8,128)S(1)}, u32[]{:S(2)}, u32[]{:S(2)}) collective-permute-start(f32[96,128]{1,0:T(8,128)S(1)} %maximum_add_fusion.refs_0_), channel_id=1, source_target_pairs={{0,2},{1,3},{2,4},{3,5},{4,6},{5,7},{6,0},{7,1},{8,10},{9,11},{10,... | collective-permute-start | bytes 147464 | tf_op jit(solution)/shard_map/ppermute | solution.py:27
  44.6 4.6 %collective-permute-start.21 = (f32[96,128]{1,0:T(8,128)S(1)}, f32[96,128]{1,0:T(8,128)S(1)}, u32[]{:S(2)}, u32[]{:S(2)}) collective-permute-start(f32[96,128]{1,0:T(8,128)S(1)} %maximum_add_fusion.refs_0_), channel_id=1, source_target_pairs={{0,4},{1,5},{2,6},{3,7},{4,0},{5,1},{6,2},{7,3},{8,12},{9,13},{10,... | collective-permute-start | bytes 147464 | tf_op jit(solution)/shard_map/ppermute | solution.py:27
  46.4 3.5 %collective-permute-start.22 = (f32[96,128]{1,0:T(8,128)S(1)}, f32[96,128]{1,0:T(8,128)S(1)}, u32[]{:S(2)}, u32[]{:S(2)}) collective-permute-start(f32[96,128]{1,0:T(8,128)S(1)} %maximum_add_fusion.refs_0_), channel_id=1, source_target_pairs={{0,6},{1,7},{2,0},{3,1},{4,2},{5,3},{6,4},{7,5},{8,14},{9,15},{10,... | collective-permute-start | bytes 147464 | tf_op jit(solution)/shard_map/ppermute | solution.py:27
  49.9 21.3 %copy-start.3 = (f32[384,384]{1,0:T(8,128)S(1)}, f32[384,384]{1,0:T(8,128)}, u32[]{:S(2)}) copy-start(f32[384,384]{1,0:T(8,128)} %param.23) | copy-start | bytes 1769476
  49.9 21.3 %copy-start.4 = (f32[384,384]{1,0:T(8,128)S(1)}, f32[384,384]{1,0:T(8,128)}, u32[]{:S(2)}) copy-start(f32[384,384]{1,0:T(8,128)} %param.24) | copy-start | bytes 1769476
  50.7 8.9 %collective-permute-start.23 = (f32[384,128]{1,0:T(8,128)S(1)}, f32[384,128]{1,0:T(8,128)S(1)}, u32[]{:S(2)}, u32[]{:S(2)}) collective-permute-start(f32[384,128]{1,0:T(8,128)S(1)} %get-tuple-element.34.normed), channel_id=1, source_target_pairs={{32,0},{33,1},{42,2},{27,3},{52,4},{21,5},{30,6},{47,7},{40,8},{41... | collective-permute-start | bytes 589832 | tf_op jit(solution)/shard_map/ppermute | solution.py:387
  55.0 4.5 %collective-permute-start.24 = (f32[384,128]{1,0:T(8,128)S(1)}, f32[384,128]{1,0:T(8,128)S(1)}, u32[]{:S(2)}, u32[]{:S(2)}) collective-permute-start(f32[384,128]{1,0:T(8,128)S(1)} %get-tuple-element.34.normed), channel_id=1, source_target_pairs={{0,0},{1,1},{10,2},{59,3},{20,4},{53,5},{62,6},{15,7},{8,8},{9,9},... | collective-permute-start | bytes 589832 | tf_op jit(solution)/shard_map/ppermute | solution.py:387
  57.2 15.3 %copy-start.5 = (f32[384]{0:T(512)S(1)}, f32[384]{0:T(512)}, u32[]{:S(2)}) copy-start(f32[384]{0:T(512)} %param.25) | copy-start | bytes 4612
  61.0 11.6 %collective-permute-start.25 = (f32[32,512]{1,0:T(8,128)S(1)}, f32[32,512]{1,0:T(8,128)S(1)}, u32[]{:S(2)}, u32[]{:S(2)}) collective-permute-start(f32[32,512]{1,0:T(8,128)S(1)} %get-tuple-element.37), channel_id=1, source_target_pairs={{0,2},{1,3},{2,4},{3,5},{4,6},{5,7},{6,0},{7,1},{8,10},{9,11},{10,... | collective-permute-start | bytes 196616 | tf_op jit(solution)/shard_map/ppermute | solution.py:27
  67.2 7.9 %collective-permute-start.26 = (f32[32,512]{1,0:T(8,128)S(1)}, f32[32,512]{1,0:T(8,128)S(1)}, u32[]{:S(2)}, u32[]{:S(2)}) collective-permute-start(f32[32,512]{1,0:T(8,128)S(1)} %get-tuple-element.38), channel_id=1, source_target_pairs={{0,4},{1,5},{2,6},{3,7},{4,0},{5,1},{6,2},{7,3},{8,12},{9,13},{10,... | collective-permute-start | bytes 196616 | tf_op jit(solution)/shard_map/ppermute | solution.py:27
  71.2 3.8 %collective-permute-start.27 = (f32[32,512]{1,0:T(8,128)S(1)}, f32[32,512]{1,0:T(8,128)S(1)}, u32[]{:S(2)}, u32[]{:S(2)}) collective-permute-start(f32[32,512]{1,0:T(8,128)S(1)} %get-tuple-element.39), channel_id=1, source_target_pairs={{0,6},{1,7},{2,0},{3,1},{4,2},{5,3},{6,4},{7,5},{8,14},{9,15},{10,... | collective-permute-start | bytes 196616 | tf_op jit(solution)/shard_map/ppermute | solution.py:27
  76.0 1.6 %collective-permute-start.28 = (f32[4,4,384]{2,1,0:T(4,128)S(1)}, f32[4,4,384]{2,1,0:T(4,128)S(1)}, u32[]{:S(2)}, u32[]{:S(2)}) collective-permute-start(f32[4,4,384]{2,1,0:T(4,128)S(1)} %get-tuple-element.42), channel_id=1, source_target_pairs={{0,1},{1,0},{2,3},{3,2},{4,5},{5,4},{6,7},{7,6},{8,9},{9,8},{10,11... | collective-permute-start | bytes 73736 | tf_op jit(solution)/shard_map/ppermute | solution.py:21

commit v4 on v3

--- a/solution.py
+++ b/solution.py
@@ -24,9 +24,13 @@
 def across_chips(xs):
     n = 2 * CHIPS
     return [
-        lax.ppermute(x, "wa", [(i, (i + 2 * k) % n) for i in range(n)])
+        lax.ppermute(x, "wa", [(i, (i + 2 * k * (1 - 2 * (i % 2))) % n) for i in range(n)])
         for k, x in enumerate(xs, 1)
     ]
+
+
+def chip_away(at, k):
+    return lax.rem(at[2] + (1 - 2 * at[3]) * k + CHIPS, CHIPS)
 
 
 def gathered(x):
@@ -138,20 +142,20 @@
 def first_conv_kernel(at, *refs):
     pieces, (gain, wh, wl) = refs[:8], refs[8:11]
     next_out, own_out, strip_out, xh_out, xl_out, cells, prod = refs[11:]
-    y, c = at[2], at[3]
+    c = at[3]
     for k in range(CHIPS):
-        mine, other = pieces[k][...], pieces[CHIPS + k][...]
+        mine, other = pieces[k][...], pieces[CHIPS + (CHIPS - k) % CHIPS][...]
         both = jnp.concatenate(
             [jnp.where(c == 0, mine, other), jnp.where(c == 0, other, mine)], axis=2
         )
-        chip = lax.rem(y - k + CHIPS, CHIPS)
+        chip = chip_away(at, -k)
         for f in range(2):
             for r in range(4):
                 base = (r // 2) * 128 + f * 64 + (r % 2) * 32
                 cells[pl.ds(pl.multiple_of(base + 8 * chip, 8), 8), :] = both[f, r]
     strip = cells[...].T
     strip_out[...] = strip
-    xh, xl = halves(activated(strip, gain[:, 0:1]))
+    xh, xl = halves(activated(strip, gain[...]))
     xh_out[...] = xh
     xl_out[...] = xl
     prod[...] = product(wh[...], wl[...], xh, xl)
@@ -172,13 +176,13 @@
 def second_conv_kernel(at, *refs):
     pieces, (gain, wh, wl) = refs[:8], refs[8:11]
     next_mine, next_other, own_mine, own_other, inner, prod = refs[11:]
-    y, c = at[2], at[3]
+    c = at[3]
     for k in range(CHIPS):
-        chip = lax.rem(y - k + CHIPS, CHIPS)
-        for core, piece in ((c, pieces[k]), (1 - c, pieces[CHIPS + k])):
+        chip = chip_away(at, -k)
+        for core, piece in ((c, pieces[k]), (1 - c, pieces[CHIPS + (CHIPS - k) % CHIPS])):
             start = pl.multiple_of((2 * chip + core) * OUT, 8)
             inner[pl.ds(start, OUT), :] = piece[...]
-    act = activated(inner[...], gain[:, 1:2])
+    act = activated(inner[...], gain[...])
     top, mid, bottom = act[:, :128], act[:, 128:256], act[:, 256:]
     second_row = (lane_of((C, 128)) & 63) >= 32
     level = jnp.concatenate(
@@ -213,13 +217,13 @@
     pieces, (strip, gain) = refs[:4], refs[4:6]
     blocked_out, normed_out, total = refs[6:]
     for k in range(CHIPS):
-        chip = lax.rem(at[2] - k + CHIPS, CHIPS)
+        chip = chip_away(at, -k)
         start = pl.multiple_of(chip * (2 * OUT), 8)
         total[pl.ds(start, 2 * OUT), :] = pieces[k][...]
     frame = total[...] + one_frame(strip[:, :128], strip[:, 128:], at[3] == 1)
     blocked_out[...] = frame
     mean = jnp.mean(frame * frame, axis=0, keepdims=True)
-    normed_out[...] = frame * lax.rsqrt(mean + 1e-6) * gain[:, 2:3]
+    normed_out[...] = frame * lax.rsqrt(mean + 1e-6) * gain[...]
 
 
 def query_kernel(at, blocked, normed, w_score, queries_out, rest_out, cells):
@@ -250,7 +254,7 @@
     )
     state[:, C:] = jnp.where(lane_of((128, 128)) < 64, top, denom)
     for k in range(CHIPS):
-        chip = lax.rem(at[2] + k, CHIPS)
+        chip = chip_away(at, k)
         for r in range(4):
             start = pl.multiple_of(32 * r + 8 * chip, 8)
             outs[k][8 * r : 8 * r + 8, :] = state[pl.ds(start, 8), :]
@@ -299,7 +303,6 @@
     wa = lax.axis_index("wa")
     at = jnp.stack([lax.axis_index("ta"), lax.axis_index("ha"), wa // 2, wa % 2]).astype(jnp.int32)
     column = lambda v: v.reshape(C, 1)
-    gains = jnp.stack([first_gain, second_gain, attn_gain], axis=1)
 
     first_w = split_weights(first_kernel[:, :2], (1, 2, 3, 0, 4))
     first_w_own = split_weights(first_kernel[:, 2:], (1, 2, 3, 0, 4))
@@ -318,7 +321,7 @@
         first_conv_kernel,
         [(OUT, 384), (OUT, 384), (C, 256), operand(C, 256), operand(C, 256)],
         *gathered(latents),
-        gains,
+        column(first_gain),
         *first_w,
         scratch=[pltpu.VMEM((256, C), F32), pltpu.VMEM((18 * OUT, 256), F32)],
         scalars=at,
@@ -348,7 +351,7 @@
         second_conv_kernel,
         [(OUT, 128)] * 4,
         *gathered(inner),
-        gains,
+        column(second_gain),
         *second_w,
         scratch=[pltpu.VMEM((C, 384), F32), pltpu.VMEM((9 * OUT, 256), F32)],
         scalars=at,
@@ -373,7 +376,7 @@
         change,
         *across_chips([change] * (CHIPS - 1)),
         strip,
-        gains,
+        column(attn_gain),
         scratch=[pltpu.VMEM((C, 128), F32)],
         scalars=at,
     )

time: 78.5 us -> 78.2 us (level)
  waiting for transfers between devices: 14.7 us -> 18.6 us
  starting transfers between devices: 44 us -> 41.3 us
  local copies, waits for them, and re-layouts: 6.46 us -> 5 us
    ppermute x12, starting transfers between devices: 23.1 us -> 16.6 us  [across_chips(): lax.ppermute(x, 'wa', [(i, (i + 2 * k * (1 - 2 * (i % 2))) % n) for i in...]
    ppermute x10, starting transfers between devices: 7.43 us -> 12 us  [sibling(): return lax.ppermute(x, 'wa', [(i, i ^ 1) for i in range(2 * CHIPS)])]
    ppermute x2, waiting for transfers between devices: 1.18 us -> 3.57 us  [per_device(): keys.append(lax.ppermute(normed, ('ha', 'wa'), pairs))]
    ppermute x12, waiting for transfers between devices: 5.23 us -> 7.56 us  [across_chips(): lax.ppermute(x, 'wa', [(i, (i + 2 * k * (1 - 2 * (i % 2))) % n) for i in...]
    another operation x6 -> x2, local copies, waits for them, and re-layouts: 3.69 us -> 1.51 us  [the longest x4 2.18 us: per_device(): gains = jnp.stack([first_gain, second_gain, attn_gain], axis=1)]
  transfers between devices with their start and end apart: 29 -> 29, of which waited for: 14 -> 16; matrix products, arithmetic and copies ran while one was open for 12% -> 10% of each run, Pallas kernels for 2% -> 2%
where the time goes in v4:
time: 78.2 us; the launch traced here: 78 us
  starting transfers between devices  41.3 us (53%)
  waiting for transfers between devices  18.6 us (24%)
  Pallas kernels  8.81 us (11%)
  local copies, waits for them, and re-layouts  5 us (6%)
  matrix products  2.53 us (3%)
  other arithmetic  1.45 us (2%)
    ppermute x12, starting transfers between devices, across_chips(): lax.ppermute(x, 'wa', [(i, (i + 2 * k * (1 - 2 * (i % 2))) % n) for i in...  16.6 us
    ppermute x10, starting transfers between devices, sibling(): return lax.ppermute(x, 'wa', [(i, i ^ 1) for i in range(2 * CHIPS)])  12 us
    pallas_call x7, Pallas kernels, call(): pl.pallas_call(kernel, out_shape=outs, in_specs=in_specs, out_specs=[pl.B...  8.81 us
    ppermute x12, waiting for transfers between devices, across_chips(): lax.ppermute(x, 'wa', [(i, (i + 2 * k * (1 - 2 * (i % 2))) % n) for i in...  7.56 us
    ppermute x4, starting transfers between devices, shifted(): return lax.ppermute(x, axis, [(i, (i + by) % n) for i in range(n)])  6.38 us
    ppermute x2, starting transfers between devices, per_device(): keys.append(lax.ppermute(normed, ('ha', 'wa'), pairs))  5.25 us
    ppermute x4, waiting for transfers between devices, shifted(): return lax.ppermute(x, axis, [(i, (i + by) % n) for i in range(n)])  4.61 us
    ppermute x2, waiting for transfers between devices, per_device(): keys.append(lax.ppermute(normed, ('ha', 'wa'), pairs))  3.57 us
  transfers between devices with their start and end apart: 29, of which 16 were waited for; matrix products, arithmetic and copies ran while one was open for 10% of the time, Pallas kernels for 2%

profile of v4, /device:TPU:1, one launch (start us, length us, event | category | flops | bytes accessed | tf_op | source)
XLA Modules:
  0.0 78.0 jit_solution(14443428510649064976)
XLA Ops:
  0.0 3.6 %collective-permute-start = (f32[2,4,4,384]{3,2,1,0:T(4,128)}, f32[2,4,4,384]{3,2,1,0:T(4,128)S(1)}, u32[]{:S(2)}, u32[]{:S(2)}) collective-permute-start(f32[2,4,4,384]{3,2,1,0:T(4,128)} %refs_0_.1), channel_id=1, source_target_pairs={{0,2},{1,7},{2,4},{3,1},{4,6},{5,3},{6,0},{7,5},{8,10},{9,15},{10,... | collective-permute-start | bytes 147464 | tf_op jit(solution)/shard_map/ppermute | solution.py:27
  3.6 0.3 collective-permute-start.1
  3.9 0.7 collective-permute-start.2
  4.6 2.7 %collective-permute-start.3 = (f32[2,4,4,384]{3,2,1,0:T(4,128)}, f32[2,4,4,384]{3,2,1,0:T(4,128)S(1)}, u32[]{:S(2)}, u32[]{:S(2)}) collective-permute-start(f32[2,4,4,384]{3,2,1,0:T(4,128)} %refs_0_.1), channel_id=1, source_target_pairs={{0,1},{1,0},{2,3},{3,2},{4,5},{5,4},{6,7},{7,6},{8,9},{9,8},{10,11... | collective-permute-start | bytes 147464 | tf_op jit(solution)/shard_map/ppermute | solution.py:21
  7.6 2.6 %collective-permute-start.4 = (f32[2,4,4,384]{3,2,1,0:T(4,128)S(1)}, f32[2,4,4,384]{3,2,1,0:T(4,128)S(1)}, u32[]{:S(2)}, u32[]{:S(2)}) collective-permute-start(f32[2,4,4,384]{3,2,1,0:T(4,128)S(1)} %collective-permute-done.refs_1_), channel_id=1, source_target_pairs={{0,1},{1,0},{2,3},{3,2},{4,5},{5,4},{6,7},{7,6},{8,9},{9,8},{10,11... | collective-permute-start | bytes 147464 | tf_op jit(solution)/shard_map/ppermute | solution.py:21
  10.1 0.5 collective-permute-start.6
  11.0 0.4 collective-permute-done.5.refs_6_
  11.5 1.9 %shard_map.127 = (f32[48,384]{1,0:T(8,128)S(1)}, f32[48,384]{1,0:T(8,128)S(1)}, f32[384,256]{1,0:T(8,128)S(1)}, bf16[384,256]{1,0:T(8,128)(2,1)S(1)}, bf16[384,256]{1,0:T(8,128)(2,1)S(1)}) custom-call(s32[4]{0:T(128)S(1)} %pad_add_fusion.at, f32[2,4,4,384]{3,2,1,0:T(4,128)S(1)} %copy-done.1, f32[2,4,4,384]{3,2,1,0:T(4,128)S(1)} %collective-permute-done.refs_1_, ...), custom_call_target="tpu_custom_call" | custom-call | flops 1000000000 | bytes 2655744 | tf_op jit(solution)/shard_map/pallas_call | solution.py:53
  13.5 0.9 %collective-permute-start.7 = (f32[48,384]{1,0:T(8,128)S(1)}, f32[48,384]{1,0:T(8,128)S(1)}, u32[]{:S(2)}, u32[]{:S(2)}) collective-permute-start(f32[48,384]{1,0:T(8,128)S(1)} %get-tuple-element.27), channel_id=1, source_target_pairs={{0,64},{64,128},{128,192},{192,0},{1,65},{65,129},{129,193},{193,1... | collective-permute-start | bytes 221192 | tf_op jit(solution)/shard_map/ppermute | solution.py:43
  14.5 0.6 shard_map.128
  15.1 2.8 %collective-permute-done.7 = f32[48,384]{1,0:T(8,128)S(1)} collective-permute-done((f32[48,384]{1,0:T(8,128)S(1)}, f32[48,384]{1,0:T(8,128)S(1)}, u32[]{:S(2)}, u32[]{:S(2)}) %collective-permute-start.7) | collective-permute-done | bytes 73760 | tf_op jit(solution)/shard_map/ppermute | solution.py:43
  18.0 1.3 %collective-permute-start.8 = (f32[48,128]{1,0:T(8,128)S(1)}, f32[48,128]{1,0:T(8,128)S(1)}, u32[]{:S(2)}, u32[]{:S(2)}) collective-permute-start(f32[48,128]{1,0:T(8,128)S(1)} %get-tuple-element.54), channel_id=1, source_target_pairs={{0,8},{8,16},{16,24},{24,32},{32,40},{40,48},{48,56},{56,0},{1,9},... | collective-permute-start | bytes 73736 | tf_op jit(solution)/shard_map/ppermute | solution.py:43
  19.3 4.0 %collective-permute-start.9 = (f32[48,128]{1,0:T(8,128)S(1)}, f32[48,128]{1,0:T(8,128)S(1)}, u32[]{:S(2)}, u32[]{:S(2)}) collective-permute-start(f32[48,128]{1,0:T(8,128)S(1)} %get-tuple-element.55), channel_id=1, source_target_pairs={{0,56},{8,0},{16,8},{24,16},{32,24},{40,32},{48,40},{56,48},{1,57}... | collective-permute-start | bytes 73736 | tf_op jit(solution)/shard_map/ppermute | solution.py:43
  23.4 0.8 dynamic-slice.6
  24.1 0.4 collective-permute-done.8
  24.6 2.4 %collective-permute-start.10 = (f32[48,384]{1,0:T(8,128)S(1)}, f32[48,384]{1,0:T(8,128)S(1)}, u32[]{:S(2)}, u32[]{:S(2)}) collective-permute-start(f32[48,384]{1,0:T(8,128)S(1)} %pad_maximum_fusion.refs_0_), channel_id=1, source_target_pairs={{0,2},{1,7},{2,4},{3,1},{4,6},{5,3},{6,0},{7,5},{8,10},{9,15},{10,... | collective-permute-start | bytes 221192 | tf_op jit(solution)/shard_map/ppermute | solution.py:27
  27.2 0.4 collective-permute-start.12
  27.6 2.6 %copy.16 = f32[3,3,48,3,384]{4,3,2,1,0:T(4,128)S(1)} copy(f32[3,3,48,3,384]{4,2,1,3,0:T(8,128)} %bitcast.28) | data formatting | bytes 3981312 | tf_op jit(solution)/shard_map/transpose | solution.py:282
  30.4 4.0 %collective-permute-start.13 = (f32[48,384]{1,0:T(8,128)S(1)}, f32[48,384]{1,0:T(8,128)S(1)}, u32[]{:S(2)}, u32[]{:S(2)}) collective-permute-start(f32[48,384]{1,0:T(8,128)S(1)} %pad_maximum_fusion.refs_0_), channel_id=1, source_target_pairs={{0,1},{1,0},{2,3},{3,2},{4,5},{5,4},{6,7},{7,6},{8,9},{9,8},{10,11... | collective-permute-start | bytes 221192 | tf_op jit(solution)/shard_map/ppermute | solution.py:21
  34.4 0.4 collective-permute-start.15
  34.8 0.6 collective-permute-start.16
  35.7 0.4 copy-done.6
  36.3 2.0 %shard_map.129 = (f32[48,128]{1,0:T(8,128)S(1)}, f32[48,128]{1,0:T(8,128)S(1)}, f32[48,128]{1,0:T(8,128)S(1)}, f32[48,128]{1,0:T(8,128)S(1)}) custom-call(s32[4]{0:T(128)S(1)} %pad_add_fusion.at, f32[48,384]{1,0:T(8,128)S(1)} %pad_maximum_fusion.refs_0_, f32[48,384]{1,0:T(8,128)S(1)} %collective-permute-done.10.refs_1_, ...), custom_call_target="tpu_custom_call" | custom-call | flops 1000000000 | bytes 2680320 | tf_op jit(solution)/shard_map/pallas_call | solution.py:53
  38.4 0.6 collective-permute-start.18
  39.1 1.1 %collective-permute-start.19 = (f32[48,128]{1,0:T(8,128)S(1)}, f32[48,128]{1,0:T(8,128)S(1)}, u32[]{:S(2)}, u32[]{:S(2)}) collective-permute-start(f32[48,128]{1,0:T(8,128)S(1)} %get-tuple-element.31), channel_id=1, source_target_pairs={{0,65},{1,64},{2,67},{3,66},{4,69},{5,68},{6,71},{7,70},{64,129},{... | collective-permute-start | bytes 73736 | tf_op jit(solution)/shard_map/ppermute | solution.py:362
  40.2 0.8 dynamic-slice.7
  40.9 1.4 %collective-permute-done.17 = f32[48,128]{1,0:T(8,128)S(1)} collective-permute-done((f32[48,128]{1,0:T(8,128)S(1)}, f32[48,128]{1,0:T(8,128)S(1)}, u32[]{:S(2)}, u32[]{:S(2)}) %collective-permute-start.17) | collective-permute-done | bytes 24608 | tf_op jit(solution)/shard_map/ppermute | solution.py:43
  42.3 1.2 %collective-permute-done.19 = f32[48,128]{1,0:T(8,128)S(1)} collective-permute-done((f32[48,128]{1,0:T(8,128)S(1)}, f32[48,128]{1,0:T(8,128)S(1)}, u32[]{:S(2)}, u32[]{:S(2)}) %collective-permute-start.19) | collective-permute-done | bytes 24608 | tf_op jit(solution)/shard_map/ppermute | solution.py:362
  43.6 1.5 %collective-permute-start.20 = (f32[96,128]{1,0:T(8,128)S(1)}, f32[96,128]{1,0:T(8,128)S(1)}, u32[]{:S(2)}, u32[]{:S(2)}) collective-permute-start(f32[96,128]{1,0:T(8,128)S(1)} %maximum_add_fusion.refs_0_), channel_id=1, source_target_pairs={{0,2},{1,7},{2,4},{3,1},{4,6},{5,3},{6,0},{7,5},{8,10},{9,15},{10,... | collective-permute-start | bytes 147464 | tf_op jit(solution)/shard_map/ppermute | solution.py:27
  45.1 1.3 %collective-permute-start.21 = (f32[96,128]{1,0:T(8,128)S(1)}, f32[96,128]{1,0:T(8,128)S(1)}, u32[]{:S(2)}, u32[]{:S(2)}) collective-permute-start(f32[96,128]{1,0:T(8,128)S(1)} %maximum_add_fusion.refs_0_), channel_id=1, source_target_pairs={{0,4},{1,5},{2,6},{3,7},{4,0},{5,1},{6,2},{7,3},{8,12},{9,13},{10,... | collective-permute-start | bytes 147464 | tf_op jit(solution)/shard_map/ppermute | solution.py:27
  46.6 2.9 %collective-permute-done.21.refs_2_ = f32[96,128]{1,0:T(8,128)S(1)} collective-permute-done((f32[96,128]{1,0:T(8,128)S(1)}, f32[96,128]{1,0:T(8,128)S(1)}, u32[]{:S(2)}, u32[]{:S(2)}) %collective-permute-start.21) | collective-permute-done | bytes 49184 | tf_op jit(solution)/shard_map/ppermute | solution.py:27
  49.5 1.5 %collective-permute-done.22.refs_3_ = f32[96,128]{1,0:T(8,128)S(1)} collective-permute-done((f32[96,128]{1,0:T(8,128)S(1)}, f32[96,128]{1,0:T(8,128)S(1)}, u32[]{:S(2)}, u32[]{:S(2)}) %collective-permute-start.22) | collective-permute-done | bytes 49184 | tf_op jit(solution)/shard_map/ppermute | solution.py:27
  51.0 0.8 shard_map.130
  51.8 4.4 %collective-permute-start.23 = (f32[384,128]{1,0:T(8,128)S(1)}, f32[384,128]{1,0:T(8,128)S(1)}, u32[]{:S(2)}, u32[]{:S(2)}) collective-permute-start(f32[384,128]{1,0:T(8,128)S(1)} %get-tuple-element.34.normed), channel_id=1, source_target_pairs={{32,0},{33,1},{42,2},{27,3},{52,4},{21,5},{30,6},{47,7},{40,8},{41... | collective-permute-start | bytes 589832 | tf_op jit(solution)/shard_map/ppermute | solution.py:390
  56.2 0.9 %collective-permute-start.24 = (f32[384,128]{1,0:T(8,128)S(1)}, f32[384,128]{1,0:T(8,128)S(1)}, u32[]{:S(2)}, u32[]{:S(2)}) collective-permute-start(f32[384,128]{1,0:T(8,128)S(1)} %get-tuple-element.34.normed), channel_id=1, source_target_pairs={{0,0},{1,1},{10,2},{59,3},{20,4},{53,5},{62,6},{15,7},{8,8},{9,9},... | collective-permute-start | bytes 589832 | tf_op jit(solution)/shard_map/ppermute | solution.py:390
  57.1 1.3 %convolution_multiply_fusion.w_score = f32[384,384]{1,0:T(8,128)S(1)} fusion(f32[384,384]{1,0:T(8,128)S(1)} %copy-done, f32[384,384]{1,0:T(8,128)S(1)} %copy-done.2), kind=kOutput, calls=%fused_computation.6 | convolution fusion | flops 679624704 | bytes 1769472 | tf_op jit(solution)/shard_map/dot_general | solution.py:310
  58.4 1.1 %shard_map.131 = (f32[128,384]{1,0:T(8,128)S(1)}, f32[32,384]{1,0:T(8,128)S(1)}) custom-call(s32[4]{0:T(128)S(1)} %pad_add_fusion.at, f32[384,128]{1,0:T(8,128)S(1)} %get-tuple-element.33.blocked, f32[384,128]{1,0:T(8,128)S(1)} %get-tuple-element.34.normed, f32[384,384]{1,0:T(8,128)S(1)} %convolution_multiply_fusion.w_score), custom_call_target="tpu_custom_call" | custom-call | flops 1000000 | bytes 1228800 | tf_op jit(solution)/shard_map/pallas_call | solution.py:53
  59.5 3.6 %collective-permute-done.23.keys_a = f32[384,128]{1,0:T(8,128)S(1)} collective-permute-done((f32[384,128]{1,0:T(8,128)S(1)}, f32[384,128]{1,0:T(8,128)S(1)}, u32[]{:S(2)}, u32[]{:S(2)}) %collective-permute-start.23) | collective-permute-done | bytes 196640 | tf_op jit(solution)/shard_map/ppermute | solution.py:390
  63.1 1.5 %shard_map.132 = (f32[32,512]{1,0:T(8,128)S(1)}, f32[32,512]{1,0:T(8,128)S(1)}, f32[32,512]{1,0:T(8,128)S(1)}, f32[32,512]{1,0:T(8,128)S(1)}) custom-call(s32[4]{0:T(128)S(1)} %pad_add_fusion.at, f32[128,384]{1,0:T(8,128)S(1)} %get-tuple-element.35.queries, f32[384,128]{1,0:T(8,128)S(1)} %collective-permute-done.23.keys_a, ...), custom_call_target="tpu_custom_call" | custom-call | flops 1000000 | bytes 851968 | tf_op jit(solution)/shard_map/pallas_call | solution.py:53
  64.5 5.5 %collective-permute-start.25 = (f32[32,512]{1,0:T(8,128)S(1)}, f32[32,512]{1,0:T(8,128)S(1)}, u32[]{:S(2)}, u32[]{:S(2)}) collective-permute-start(f32[32,512]{1,0:T(8,128)S(1)} %get-tuple-element.37), channel_id=1, source_target_pairs={{0,2},{1,7},{2,4},{3,1},{4,6},{5,3},{6,0},{7,5},{8,10},{9,15},{10,... | collective-permute-start | bytes 196616 | tf_op jit(solution)/shard_map/ppermute | solution.py:27
  70.1 0.7 collective-permute-start.27
  70.7 1.3 %fusion.4.w_mixed = f32[384,384]{1,0:T(8,128)S(1)} fusion(f32[384,384]{1,0:T(8,128)S(1)} %copy-done.3, f32[384,384]{1,0:T(8,128)S(1)} %copy-done.4), kind=kOutput, calls=%fused_computation.28 | convolution fusion | flops 679477248 | bytes 1769472 | tf_op jit(solution)/shard_map/dot_general | solution.py:317
  72.0 0.8 collective-permute-done.25.b
  72.8 2.0 %collective-permute-done.26.c = f32[32,512]{1,0:T(8,128)S(1)} collective-permute-done((f32[32,512]{1,0:T(8,128)S(1)}, f32[32,512]{1,0:T(8,128)S(1)}, u32[]{:S(2)}, u32[]{:S(2)}) %collective-permute-start.26) | collective-permute-done | bytes 65568 | tf_op jit(solution)/shard_map/ppermute | solution.py:27
  75.1 0.9 %shard_map.133 = (f32[4,4,384]{2,1,0:T(4,128)S(1)}, f32[4,4,384]{2,1,0:T(4,128)S(1)}) custom-call(s32[4]{0:T(128)S(1)} %pad_add_fusion.at, f32[32,512]{1,0:T(8,128)S(1)} %get-tuple-element.36.a, f32[32,512]{1,0:T(8,128)S(1)} %collective-permute-done.25.b, f32[32,512]{1,0:T(8,128)S(1)} %collective-permute-done.26.c, f32[32,512]{1,0:T(8,128)S(1)} %collective-permute-done.27.d, ...), custom_call_target="tpu_custom_call" | custom-call | flops 1000000 | bytes 951808 | tf_op jit(solution)/shard_map/pallas_call | solution.py:53
  76.0 0.5 collective-permute-start.28
  76.5 0.8 %collective-permute-done.28 = f32[4,4,384]{2,1,0:T(4,128)S(1)} collective-permute-done((f32[4,4,384]{2,1,0:T(4,128)S(1)}, f32[4,4,384]{2,1,0:T(4,128)S(1)}, u32[]{:S(2)}, u32[]{:S(2)}) %collective-permute-start.28) | collective-permute-done | bytes 24608 | tf_op jit(solution)/shard_map/ppermute | solution.py:21
  77.4 0.6 pad_maximum_fusion.1
  (62 shorter events, 2.6 us)
Async XLA Ops:
  0.0 57.1 %copy-start = (f32[384,384]{1,0:T(8,128)S(1)}, f32[384,384]{1,0:T(8,128)}, u32[]{:S(2)}) copy-start(f32[384,384]{1,0:T(8,128)} %param.21) | copy-start | bytes 1769476
  0.0 7.3 %slice-start = ((f32[48,3,3,3,384]{4,0,3,2,1:T(8,128)}), f32[48,2,3,3,384]{4,0,3,2,1:T(8,128)S(1)}, s32[]{:S(2)}) async-start(f32[48,3,3,3,384]{4,0,3,2,1:T(8,128)} %param.15), calls=%async_computation | async-start | bytes 2654208 | tf_op jit(solution)/shard_map/slice | solution.py:307
  0.0 7.5 %collective-permute-start = (f32[2,4,4,384]{3,2,1,0:T(4,128)}, f32[2,4,4,384]{3,2,1,0:T(4,128)S(1)}, u32[]{:S(2)}, u32[]{:S(2)}) collective-permute-start(f32[2,4,4,384]{3,2,1,0:T(4,128)} %refs_0_.1), channel_id=1, source_target_pairs={{0,2},{1,7},{2,4},{3,1},{4,6},{5,3},{6,0},{7,5},{8,10},{9,15},{10,... | collective-permute-start | bytes 147464 | tf_op jit(solution)/shard_map/ppermute | solution.py:27
  3.6 6.6 %collective-permute-start.1 = (f32[2,4,4,384]{3,2,1,0:T(4,128)}, f32[2,4,4,384]{3,2,1,0:T(4,128)S(1)}, u32[]{:S(2)}, u32[]{:S(2)}) collective-permute-start(f32[2,4,4,384]{3,2,1,0:T(4,128)} %refs_0_.1), channel_id=1, source_target_pairs={{0,4},{1,5},{2,6},{3,7},{4,0},{5,1},{6,2},{7,3},{8,12},{9,13},{10,... | collective-permute-start | bytes 147464 | tf_op jit(solution)/shard_map/ppermute | solution.py:27
  3.9 6.2 %collective-permute-start.2 = (f32[2,4,4,384]{3,2,1,0:T(4,128)}, f32[2,4,4,384]{3,2,1,0:T(4,128)S(1)}, u32[]{:S(2)}, u32[]{:S(2)}) collective-permute-start(f32[2,4,4,384]{3,2,1,0:T(4,128)} %refs_0_.1), channel_id=1, source_target_pairs={{0,6},{1,3},{2,0},{3,5},{4,2},{5,7},{6,4},{7,1},{8,14},{9,11},{10,... | collective-permute-start | bytes 147464 | tf_op jit(solution)/shard_map/ppermute | solution.py:27
  4.6 6.2 %collective-permute-start.3 = (f32[2,4,4,384]{3,2,1,0:T(4,128)}, f32[2,4,4,384]{3,2,1,0:T(4,128)S(1)}, u32[]{:S(2)}, u32[]{:S(2)}) collective-permute-start(f32[2,4,4,384]{3,2,1,0:T(4,128)} %refs_0_.1), channel_id=1, source_target_pairs={{0,1},{1,0},{2,3},{3,2},{4,5},{5,4},{6,7},{7,6},{8,9},{9,8},{10,11... | collective-permute-start | bytes 147464 | tf_op jit(solution)/shard_map/ppermute | solution.py:21
  7.3 3.4 %copy-start.5 = (f32[384]{0:T(512)S(1)}, f32[384]{0:T(512)}, u32[]{:S(2)}) copy-start(f32[384]{0:T(512)} %param.14) | copy-start | bytes 4612
  7.3 4.2 %copy-start.1 = (f32[2,4,4,384]{3,2,1,0:T(4,128)S(1)}, f32[2,4,4,384]{3,2,1,0:T(4,128)}, u32[]{:S(2)}) copy-start(f32[2,4,4,384]{3,2,1,0:T(4,128)} %refs_0_.1) | copy-start | bytes 147460
  7.6 3.5 %collective-permute-start.4 = (f32[2,4,4,384]{3,2,1,0:T(4,128)S(1)}, f32[2,4,4,384]{3,2,1,0:T(4,128)S(1)}, u32[]{:S(2)}, u32[]{:S(2)}) collective-permute-start(f32[2,4,4,384]{3,2,1,0:T(4,128)S(1)} %collective-permute-done.refs_1_), channel_id=1, source_target_pairs={{0,1},{1,0},{2,3},{3,2},{4,5},{5,4},{6,7},{7,6},{8,9},{9,8},{10,11... | collective-permute-start | bytes 147464 | tf_op jit(solution)/shard_map/ppermute | solution.py:21
  10.1 1.2 %collective-permute-start.5 = (f32[2,4,4,384]{3,2,1,0:T(4,128)S(1)}, f32[2,4,4,384]{3,2,1,0:T(4,128)S(1)}, u32[]{:S(2)}, u32[]{:S(2)}) collective-permute-start(f32[2,4,4,384]{3,2,1,0:T(4,128)S(1)} %collective-permute-done.1.refs_2_), channel_id=1, source_target_pairs={{0,1},{1,0},{2,3},{3,2},{4,5},{5,4},{6,7},{7,6},{8,9},{9,8},{10,11... | collective-permute-start | bytes 147464 | tf_op jit(solution)/shard_map/ppermute | solution.py:21
  10.1 1.4 %collective-permute-start.6 = (f32[2,4,4,384]{3,2,1,0:T(4,128)S(1)}, f32[2,4,4,384]{3,2,1,0:T(4,128)S(1)}, u32[]{:S(2)}, u32[]{:S(2)}) collective-permute-start(f32[2,4,4,384]{3,2,1,0:T(4,128)S(1)} %collective-permute-done.2.refs_3_), channel_id=1, source_target_pairs={{0,1},{1,0},{2,3},{3,2},{4,5},{5,4},{6,7},{7,6},{8,9},{9,8},{10,11... | collective-permute-start | bytes 147464 | tf_op jit(solution)/shard_map/ppermute | solution.py:21
  10.7 3.7 %slice-start.1 = ((f32[48,3,3,3,384]{4,0,3,2,1:T(8,128)}), f32[48,1,3,3,384]{4,0,3,2,1:T(8,128)S(1)}, s32[]{:S(2)}) async-start(f32[48,3,3,3,384]{4,0,3,2,1:T(8,128)} %param.15), calls=%async_computation.1 | async-start | bytes 1327104 | tf_op jit(solution)/shard_map/slice | solution.py:308
  13.5 4.5 %collective-permute-start.7 = (f32[48,384]{1,0:T(8,128)S(1)}, f32[48,384]{1,0:T(8,128)S(1)}, u32[]{:S(2)}, u32[]{:S(2)}) collective-permute-start(f32[48,384]{1,0:T(8,128)S(1)} %get-tuple-element.27), channel_id=1, source_target_pairs={{0,64},{64,128},{128,192},{192,0},{1,65},{65,129},{129,193},{193,1... | collective-permute-start | bytes 221192 | tf_op jit(solution)/shard_map/ppermute | solution.py:43
  18.0 6.5 %collective-permute-start.8 = (f32[48,128]{1,0:T(8,128)S(1)}, f32[48,128]{1,0:T(8,128)S(1)}, u32[]{:S(2)}, u32[]{:S(2)}) collective-permute-start(f32[48,128]{1,0:T(8,128)S(1)} %get-tuple-element.54), channel_id=1, source_target_pairs={{0,8},{8,16},{16,24},{24,32},{32,40},{40,48},{48,56},{56,0},{1,9},... | collective-permute-start | bytes 73736 | tf_op jit(solution)/shard_map/ppermute | solution.py:43
  19.3 5.2 %collective-permute-start.9 = (f32[48,128]{1,0:T(8,128)S(1)}, f32[48,128]{1,0:T(8,128)S(1)}, u32[]{:S(2)}, u32[]{:S(2)}) collective-permute-start(f32[48,128]{1,0:T(8,128)S(1)} %get-tuple-element.55), channel_id=1, source_target_pairs={{0,56},{8,0},{16,8},{24,16},{32,24},{40,32},{48,40},{56,48},{1,57}... | collective-permute-start | bytes 73736 | tf_op jit(solution)/shard_map/ppermute | solution.py:43
  24.6 9.7 %collective-permute-start.10 = (f32[48,384]{1,0:T(8,128)S(1)}, f32[48,384]{1,0:T(8,128)S(1)}, u32[]{:S(2)}, u32[]{:S(2)}) collective-permute-start(f32[48,384]{1,0:T(8,128)S(1)} %pad_maximum_fusion.refs_0_), channel_id=1, source_target_pairs={{0,2},{1,7},{2,4},{3,1},{4,6},{5,3},{6,0},{7,5},{8,10},{9,15},{10,... | collective-permute-start | bytes 221192 | tf_op jit(solution)/shard_map/ppermute | solution.py:27
  26.9 7.5 %collective-permute-start.11 = (f32[48,384]{1,0:T(8,128)S(1)}, f32[48,384]{1,0:T(8,128)S(1)}, u32[]{:S(2)}, u32[]{:S(2)}) collective-permute-start(f32[48,384]{1,0:T(8,128)S(1)} %pad_maximum_fusion.refs_0_), channel_id=1, source_target_pairs={{0,4},{1,5},{2,6},{3,7},{4,0},{5,1},{6,2},{7,3},{8,12},{9,13},{10,... | collective-permute-start | bytes 221192 | tf_op jit(solution)/shard_map/ppermute | solution.py:27
  27.2 7.6 %collective-permute-start.12 = (f32[48,384]{1,0:T(8,128)S(1)}, f32[48,384]{1,0:T(8,128)S(1)}, u32[]{:S(2)}, u32[]{:S(2)}) collective-permute-start(f32[48,384]{1,0:T(8,128)S(1)} %pad_maximum_fusion.refs_0_), channel_id=1, source_target_pairs={{0,6},{1,3},{2,0},{3,5},{4,2},{5,7},{6,4},{7,1},{8,14},{9,11},{10,... | collective-permute-start | bytes 221192 | tf_op jit(solution)/shard_map/ppermute | solution.py:27
  30.4 5.9 %collective-permute-start.13 = (f32[48,384]{1,0:T(8,128)S(1)}, f32[48,384]{1,0:T(8,128)S(1)}, u32[]{:S(2)}, u32[]{:S(2)}) collective-permute-start(f32[48,384]{1,0:T(8,128)S(1)} %pad_maximum_fusion.refs_0_), channel_id=1, source_target_pairs={{0,1},{1,0},{2,3},{3,2},{4,5},{5,4},{6,7},{7,6},{8,9},{9,8},{10,11... | collective-permute-start | bytes 221192 | tf_op jit(solution)/shard_map/ppermute | solution.py:21
  34.3 1.9 %collective-permute-start.14 = (f32[48,384]{1,0:T(8,128)S(1)}, f32[48,384]{1,0:T(8,128)S(1)}, u32[]{:S(2)}, u32[]{:S(2)}) collective-permute-start(f32[48,384]{1,0:T(8,128)S(1)} %collective-permute-done.10.refs_1_), channel_id=1, source_target_pairs={{0,1},{1,0},{2,3},{3,2},{4,5},{5,4},{6,7},{7,6},{8,9},{9,8},{10,11... | collective-permute-start | bytes 221192 | tf_op jit(solution)/shard_map/ppermute | solution.py:21
  34.4 1.8 %collective-permute-start.15 = (f32[48,384]{1,0:T(8,128)S(1)}, f32[48,384]{1,0:T(8,128)S(1)}, u32[]{:S(2)}, u32[]{:S(2)}) collective-permute-start(f32[48,384]{1,0:T(8,128)S(1)} %collective-permute-done.11.refs_2_), channel_id=1, source_target_pairs={{0,1},{1,0},{2,3},{3,2},{4,5},{5,4},{6,7},{7,6},{8,9},{9,8},{10,11... | collective-permute-start | bytes 221192 | tf_op jit(solution)/shard_map/ppermute | solution.py:21
  34.8 1.5 %collective-permute-start.16 = (f32[48,384]{1,0:T(8,128)S(1)}, f32[48,384]{1,0:T(8,128)S(1)}, u32[]{:S(2)}, u32[]{:S(2)}) collective-permute-start(f32[48,384]{1,0:T(8,128)S(1)} %collective-permute-done.12.refs_3_), channel_id=1, source_target_pairs={{0,1},{1,0},{2,3},{3,2},{4,5},{5,4},{6,7},{7,6},{8,9},{9,8},{10,11... | collective-permute-start | bytes 221192 | tf_op jit(solution)/shard_map/ppermute | solution.py:21
  35.4 0.7 copy-start.6
  36.2 10.2 %copy-start.7 = (f32[384]{0:T(512)S(1)}, f32[384]{0:T(512)}, u32[]{:S(2)}) copy-start(f32[384]{0:T(512)} %param.20) | copy-start | bytes 4612
  36.3 20.8 %copy-start.2 = (f32[384,384]{1,0:T(8,128)S(1)}, f32[384,384]{1,0:T(8,128)}, u32[]{:S(2)}) copy-start(f32[384,384]{1,0:T(8,128)} %param.22) | copy-start | bytes 1769476
  38.3 4.0 %collective-permute-start.17 = (f32[48,128]{1,0:T(8,128)S(1)}, f32[48,128]{1,0:T(8,128)S(1)}, u32[]{:S(2)}, u32[]{:S(2)}) collective-permute-start(f32[48,128]{1,0:T(8,128)S(1)} %get-tuple-element.29), channel_id=1, source_target_pairs={{0,64},{64,128},{128,192},{192,0},{1,65},{65,129},{129,193},{193,1... | collective-permute-start | bytes 73736 | tf_op jit(solution)/shard_map/ppermute | solution.py:43
  38.4 3.9 %collective-permute-start.18 = (f32[48,128]{1,0:T(8,128)S(1)}, f32[48,128]{1,0:T(8,128)S(1)}, u32[]{:S(2)}, u32[]{:S(2)}) collective-permute-start(f32[48,128]{1,0:T(8,128)S(1)} %get-tuple-element.30), channel_id=1, source_target_pairs={{0,1},{1,0},{2,3},{3,2},{4,5},{5,4},{6,7},{7,6},{8,9},{9,8},{10,11... | collective-permute-start | bytes 73736 | tf_op jit(solution)/shard_map/ppermute | solution.py:21
  39.1 4.5 %collective-permute-start.19 = (f32[48,128]{1,0:T(8,128)S(1)}, f32[48,128]{1,0:T(8,128)S(1)}, u32[]{:S(2)}, u32[]{:S(2)}) collective-permute-start(f32[48,128]{1,0:T(8,128)S(1)} %get-tuple-element.31), channel_id=1, source_target_pairs={{0,65},{1,64},{2,67},{3,66},{4,69},{5,68},{6,71},{7,70},{64,129},{... | collective-permute-start | bytes 73736 | tf_op jit(solution)/shard_map/ppermute | solution.py:362
  43.6 3.0 %collective-permute-start.20 = (f32[96,128]{1,0:T(8,128)S(1)}, f32[96,128]{1,0:T(8,128)S(1)}, u32[]{:S(2)}, u32[]{:S(2)}) collective-permute-start(f32[96,128]{1,0:T(8,128)S(1)} %maximum_add_fusion.refs_0_), channel_id=1, source_target_pairs={{0,2},{1,7},{2,4},{3,1},{4,6},{5,3},{6,0},{7,5},{8,10},{9,15},{10,... | collective-permute-start | bytes 147464 | tf_op jit(solution)/shard_map/ppermute | solution.py:27
  45.1 4.4 %collective-permute-start.21 = (f32[96,128]{1,0:T(8,128)S(1)}, f32[96,128]{1,0:T(8,128)S(1)}, u32[]{:S(2)}, u32[]{:S(2)}) collective-permute-start(f32[96,128]{1,0:T(8,128)S(1)} %maximum_add_fusion.refs_0_), channel_id=1, source_target_pairs={{0,4},{1,5},{2,6},{3,7},{4,0},{5,1},{6,2},{7,3},{8,12},{9,13},{10,... | collective-permute-start | bytes 147464 | tf_op jit(solution)/shard_map/ppermute | solution.py:27
  46.4 4.6 %collective-permute-start.22 = (f32[96,128]{1,0:T(8,128)S(1)}, f32[96,128]{1,0:T(8,128)S(1)}, u32[]{:S(2)}, u32[]{:S(2)}) collective-permute-start(f32[96,128]{1,0:T(8,128)S(1)} %maximum_add_fusion.refs_0_), channel_id=1, source_target_pairs={{0,6},{1,3},{2,0},{3,5},{4,2},{5,7},{6,4},{7,1},{8,14},{9,11},{10,... | collective-permute-start | bytes 147464 | tf_op jit(solution)/shard_map/ppermute | solution.py:27
  51.0 19.7 %copy-start.3 = (f32[384,384]{1,0:T(8,128)S(1)}, f32[384,384]{1,0:T(8,128)}, u32[]{:S(2)}) copy-start(f32[384,384]{1,0:T(8,128)} %param.23) | copy-start | bytes 1769476
  51.0 19.7 %copy-start.4 = (f32[384,384]{1,0:T(8,128)S(1)}, f32[384,384]{1,0:T(8,128)}, u32[]{:S(2)}) copy-start(f32[384,384]{1,0:T(8,128)} %param.24) | copy-start | bytes 1769476
  51.8 11.3 %collective-permute-start.23 = (f32[384,128]{1,0:T(8,128)S(1)}, f32[384,128]{1,0:T(8,128)S(1)}, u32[]{:S(2)}, u32[]{:S(2)}) collective-permute-start(f32[384,128]{1,0:T(8,128)S(1)} %get-tuple-element.34.normed), channel_id=1, source_target_pairs={{32,0},{33,1},{42,2},{27,3},{52,4},{21,5},{30,6},{47,7},{40,8},{41... | collective-permute-start | bytes 589832 | tf_op jit(solution)/shard_map/ppermute | solution.py:390
  56.2 6.9 %collective-permute-start.24 = (f32[384,128]{1,0:T(8,128)S(1)}, f32[384,128]{1,0:T(8,128)S(1)}, u32[]{:S(2)}, u32[]{:S(2)}) collective-permute-start(f32[384,128]{1,0:T(8,128)S(1)} %get-tuple-element.34.normed), channel_id=1, source_target_pairs={{0,0},{1,1},{10,2},{59,3},{20,4},{53,5},{62,6},{15,7},{8,8},{9,9},... | collective-permute-start | bytes 589832 | tf_op jit(solution)/shard_map/ppermute | solution.py:390
  58.3 13.7 %copy-start.8 = (f32[384]{0:T(512)S(1)}, f32[384]{0:T(512)}, u32[]{:S(2)}) copy-start(f32[384]{0:T(512)} %param.25) | copy-start | bytes 4612
  64.5 8.3 %collective-permute-start.25 = (f32[32,512]{1,0:T(8,128)S(1)}, f32[32,512]{1,0:T(8,128)S(1)}, u32[]{:S(2)}, u32[]{:S(2)}) collective-permute-start(f32[32,512]{1,0:T(8,128)S(1)} %get-tuple-element.37), channel_id=1, source_target_pairs={{0,2},{1,7},{2,4},{3,1},{4,6},{5,3},{6,0},{7,5},{8,10},{9,15},{10,... | collective-permute-start | bytes 196616 | tf_op jit(solution)/shard_map/ppermute | solution.py:27
  70.1 4.7 %collective-permute-start.26 = (f32[32,512]{1,0:T(8,128)S(1)}, f32[32,512]{1,0:T(8,128)S(1)}, u32[]{:S(2)}, u32[]{:S(2)}) collective-permute-start(f32[32,512]{1,0:T(8,128)S(1)} %get-tuple-element.38), channel_id=1, source_target_pairs={{0,4},{1,5},{2,6},{3,7},{4,0},{5,1},{6,2},{7,3},{8,12},{9,13},{10,... | collective-permute-start | bytes 196616 | tf_op jit(solution)/shard_map/ppermute | solution.py:27
  70.1 5.0 %collective-permute-start.27 = (f32[32,512]{1,0:T(8,128)S(1)}, f32[32,512]{1,0:T(8,128)S(1)}, u32[]{:S(2)}, u32[]{:S(2)}) collective-permute-start(f32[32,512]{1,0:T(8,128)S(1)} %get-tuple-element.39), channel_id=1, source_target_pairs={{0,6},{1,3},{2,0},{3,5},{4,2},{5,7},{6,4},{7,1},{8,14},{9,11},{10,... | collective-permute-start | bytes 196616 | tf_op jit(solution)/shard_map/ppermute | solution.py:27
  76.0 1.3 %collective-permute-start.28 = (f32[4,4,384]{2,1,0:T(4,128)S(1)}, f32[4,4,384]{2,1,0:T(4,128)S(1)}, u32[]{:S(2)}, u32[]{:S(2)}) collective-permute-start(f32[4,4,384]{2,1,0:T(4,128)S(1)} %get-tuple-element.42), channel_id=1, source_target_pairs={{0,1},{1,0},{2,3},{3,2},{4,5},{5,4},{6,7},{7,6},{8,9},{9,8},{10,11... | collective-permute-start | bytes 73736 | tf_op jit(solution)/shard_map/ppermute | solution.py:21

commit v5 on v4

--- a/solution.py
+++ b/solution.py
@@ -166,7 +166,8 @@
         next_out[:, n * 128 : n * 128 + 128] = first[n] + following
 
 
-def first_conv_own_kernel(xh, xl, wh, wl, earlier, own_out, prod):
+def first_conv_own_kernel(at, xh, xl, wh, wl, earlier, strip, own_out, frame_out, prod):
+    frame_out[...] = one_frame(strip[:, :128], strip[:, 128:], at[3] == 1)
     prod[...] = product(wh[...], wl[...], xh[...], xl[...])
     for n, tile in enumerate(rows_joined(prod, 0)):
         lanes = slice(n * 128, n * 128 + 128)
@@ -220,7 +221,7 @@
         chip = chip_away(at, -k)
         start = pl.multiple_of(chip * (2 * OUT), 8)
         total[pl.ds(start, 2 * OUT), :] = pieces[k][...]
-    frame = total[...] + one_frame(strip[:, :128], strip[:, 128:], at[3] == 1)
+    frame = total[...] + strip[...]
     blocked_out[...] = frame
     mean = jnp.mean(frame * frame, axis=0, keepdims=True)
     normed_out[...] = frame * lax.rsqrt(mean + 1e-6) * gain[...]
@@ -328,13 +329,15 @@
         flops=1_000_000_000,
     )
     arrived = shifted(following, "ta", 1)
-    (own,) = call(
+    own, strip = call(
         first_conv_own_kernel,
-        [(OUT, 384)],
+        [(OUT, 384), (C, 128)],
         *x,
         *first_w_own,
         earlier,
+        strip,
         scratch=[pltpu.VMEM((9 * OUT, 256), F32)],
+        scalars=at,
         flops=500_000_000,
     )
     own = own + jnp.where(at[0] > 0, arrived, 0.0)

time: 78.2 us -> 78.1 us (level)
  transfers between devices with their start and end apart: 29 -> 29, of which waited for: 16 -> 16; matrix products, arithmetic and copies ran while one was open for 10% -> 10% of each run, Pallas kernels for 2% -> 3%
where the time goes in v5:
time: 78.1 us; the launch traced here: 77.9 us
  starting transfers between devices  41.3 us (53%)
  waiting for transfers between devices  18 us (23%)
  Pallas kernels  9.26 us (12%)
  local copies, waits for them, and re-layouts  5 us (6%)
  matrix products  2.54 us (3%)
  other arithmetic  1.45 us (2%)
    ppermute x12, starting transfers between devices, across_chips(): lax.ppermute(x, 'wa', [(i, (i + 2 * k * (1 - 2 * (i % 2))) % n) for i in...  16.7 us
    ppermute x10, starting transfers between devices, sibling(): return lax.ppermute(x, 'wa', [(i, i ^ 1) for i in range(2 * CHIPS)])  12 us
    pallas_call x7, Pallas kernels, call(): pl.pallas_call(kernel, out_shape=outs, in_specs=in_specs, out_specs=[pl.B...  9.26 us
    ppermute x12, waiting for transfers between devices, across_chips(): lax.ppermute(x, 'wa', [(i, (i + 2 * k * (1 - 2 * (i % 2))) % n) for i in...  7.54 us
    ppermute x4, starting transfers between devices, shifted(): return lax.ppermute(x, axis, [(i, (i + by) % n) for i in range(n)])  6.39 us
    ppermute x2, starting transfers between devices, per_device(): keys.append(lax.ppermute(normed, ('ha', 'wa'), pairs))  5.24 us
    ppermute x4, waiting for transfers between devices, shifted(): return lax.ppermute(x, axis, [(i, (i + by) % n) for i in range(n)])  4.06 us
    ppermute x2, waiting for transfers between devices, per_device(): keys.append(lax.ppermute(normed, ('ha', 'wa'), pairs))  3.56 us
  transfers between devices with their start and end apart: 29, of which 16 were waited for; matrix products, arithmetic and copies ran while one was open for 10% of the time, Pallas kernels for 3%

profile of v5, /device:TPU:1, one launch (start us, length us, event | category | flops | bytes accessed | tf_op | source)
XLA Modules:
  0.0 77.9 jit_solution(13077248856510326347)
XLA Ops:
  0.0 3.6 %collective-permute-start = (f32[2,4,4,384]{3,2,1,0:T(4,128)}, f32[2,4,4,384]{3,2,1,0:T(4,128)S(1)}, u32[]{:S(2)}, u32[]{:S(2)}) collective-permute-start(f32[2,4,4,384]{3,2,1,0:T(4,128)} %refs_0_.1), channel_id=1, source_target_pairs={{0,2},{1,7},{2,4},{3,1},{4,6},{5,3},{6,0},{7,5},{8,10},{9,15},{10,... | collective-permute-start | bytes 147464 | tf_op jit(solution)/shard_map/ppermute | solution.py:27
  3.6 0.3 collective-permute-start.1
  3.9 0.7 collective-permute-start.2
  4.6 2.7 %collective-permute-start.3 = (f32[2,4,4,384]{3,2,1,0:T(4,128)}, f32[2,4,4,384]{3,2,1,0:T(4,128)S(1)}, u32[]{:S(2)}, u32[]{:S(2)}) collective-permute-start(f32[2,4,4,384]{3,2,1,0:T(4,128)} %refs_0_.1), channel_id=1, source_target_pairs={{0,1},{1,0},{2,3},{3,2},{4,5},{5,4},{6,7},{7,6},{8,9},{9,8},{10,11... | collective-permute-start | bytes 147464 | tf_op jit(solution)/shard_map/ppermute | solution.py:21
  7.6 2.6 %collective-permute-start.4 = (f32[2,4,4,384]{3,2,1,0:T(4,128)S(1)}, f32[2,4,4,384]{3,2,1,0:T(4,128)S(1)}, u32[]{:S(2)}, u32[]{:S(2)}) collective-permute-start(f32[2,4,4,384]{3,2,1,0:T(4,128)S(1)} %collective-permute-done.refs_1_), channel_id=1, source_target_pairs={{0,1},{1,0},{2,3},{3,2},{4,5},{5,4},{6,7},{7,6},{8,9},{9,8},{10,11... | collective-permute-start | bytes 147464 | tf_op jit(solution)/shard_map/ppermute | solution.py:21
  10.1 0.5 collective-permute-start.6
  11.0 0.4 collective-permute-done.5.refs_6_
  11.5 1.9 %shard_map.127 = (f32[48,384]{1,0:T(8,128)S(1)}, f32[48,384]{1,0:T(8,128)S(1)}, f32[384,256]{1,0:T(8,128)S(1)}, bf16[384,256]{1,0:T(8,128)(2,1)S(1)}, bf16[384,256]{1,0:T(8,128)(2,1)S(1)}) custom-call(s32[4]{0:T(128)S(1)} %pad_add_fusion.at, f32[2,4,4,384]{3,2,1,0:T(4,128)S(1)} %copy-done.1, f32[2,4,4,384]{3,2,1,0:T(4,128)S(1)} %collective-permute-done.refs_1_, ...), custom_call_target="tpu_custom_call" | custom-call | flops 1000000000 | bytes 2655744 | tf_op jit(solution)/shard_map/pallas_call | solution.py:53
  13.5 0.9 %collective-permute-start.7 = (f32[48,384]{1,0:T(8,128)S(1)}, f32[48,384]{1,0:T(8,128)S(1)}, u32[]{:S(2)}, u32[]{:S(2)}) collective-permute-start(f32[48,384]{1,0:T(8,128)S(1)} %get-tuple-element.31), channel_id=1, source_target_pairs={{0,64},{64,128},{128,192},{192,0},{1,65},{65,129},{129,193},{193,1... | collective-permute-start | bytes 221192 | tf_op jit(solution)/shard_map/ppermute | solution.py:43
  14.5 1.2 %shard_map.128 = (f32[48,384]{1,0:T(8,128)S(1)}, f32[384,128]{1,0:T(8,128)S(1)}) custom-call(s32[4]{0:T(128)S(1)} %pad_add_fusion.at, bf16[384,256]{1,0:T(8,128)(2,1)S(1)} %get-tuple-element.26.xh, bf16[384,256]{1,0:T(8,128)(2,1)S(1)} %get-tuple-element.27.xl, bf16[432,384]{1,0:T(8,128)(2,1)S(1)} %get-tuple-element.52.wh, ...), custom_call_target="tpu_custom_call" | custom-call | flops 500000000 | bytes 1794048 | tf_op jit(solution)/shard_map/pallas_call | solution.py:53
  15.7 2.3 %collective-permute-done.7 = f32[48,384]{1,0:T(8,128)S(1)} collective-permute-done((f32[48,384]{1,0:T(8,128)S(1)}, f32[48,384]{1,0:T(8,128)S(1)}, u32[]{:S(2)}, u32[]{:S(2)}) %collective-permute-start.7) | collective-permute-done | bytes 73760 | tf_op jit(solution)/shard_map/ppermute | solution.py:43
  18.0 1.4 %collective-permute-start.8 = (f32[48,128]{1,0:T(8,128)S(1)}, f32[48,128]{1,0:T(8,128)S(1)}, u32[]{:S(2)}, u32[]{:S(2)}) collective-permute-start(f32[48,128]{1,0:T(8,128)S(1)} %get-tuple-element.58), channel_id=1, source_target_pairs={{0,8},{8,16},{16,24},{24,32},{32,40},{40,48},{48,56},{56,0},{1,9},... | collective-permute-start | bytes 73736 | tf_op jit(solution)/shard_map/ppermute | solution.py:43
  19.3 4.0 %collective-permute-start.9 = (f32[48,128]{1,0:T(8,128)S(1)}, f32[48,128]{1,0:T(8,128)S(1)}, u32[]{:S(2)}, u32[]{:S(2)}) collective-permute-start(f32[48,128]{1,0:T(8,128)S(1)} %get-tuple-element.59), channel_id=1, source_target_pairs={{0,56},{8,0},{16,8},{24,16},{32,24},{40,32},{48,40},{56,48},{1,57}... | collective-permute-start | bytes 73736 | tf_op jit(solution)/shard_map/ppermute | solution.py:43
  23.4 0.8 dynamic-slice.6
  24.1 0.4 collective-permute-done.8
  24.6 2.4 %collective-permute-start.10 = (f32[48,384]{1,0:T(8,128)S(1)}, f32[48,384]{1,0:T(8,128)S(1)}, u32[]{:S(2)}, u32[]{:S(2)}) collective-permute-start(f32[48,384]{1,0:T(8,128)S(1)} %pad_maximum_fusion.refs_0_), channel_id=1, source_target_pairs={{0,2},{1,7},{2,4},{3,1},{4,6},{5,3},{6,0},{7,5},{8,10},{9,15},{10,... | collective-permute-start | bytes 221192 | tf_op jit(solution)/shard_map/ppermute | solution.py:27
  27.2 0.4 collective-permute-start.12
  27.6 2.6 %copy.16 = f32[3,3,48,3,384]{4,3,2,1,0:T(4,128)S(1)} copy(f32[3,3,48,3,384]{4,2,1,3,0:T(8,128)} %bitcast.28) | data formatting | bytes 3981312 | tf_op jit(solution)/shard_map/transpose | solution.py:283
  30.4 4.0 %collective-permute-start.13 = (f32[48,384]{1,0:T(8,128)S(1)}, f32[48,384]{1,0:T(8,128)S(1)}, u32[]{:S(2)}, u32[]{:S(2)}) collective-permute-start(f32[48,384]{1,0:T(8,128)S(1)} %pad_maximum_fusion.refs_0_), channel_id=1, source_target_pairs={{0,1},{1,0},{2,3},{3,2},{4,5},{5,4},{6,7},{7,6},{8,9},{9,8},{10,11... | collective-permute-start | bytes 221192 | tf_op jit(solution)/shard_map/ppermute | solution.py:21
  34.4 0.4 collective-permute-start.15
  34.8 0.6 collective-permute-start.16
  35.7 0.4 copy-done.6
  36.3 2.0 %shard_map.129 = (f32[48,128]{1,0:T(8,128)S(1)}, f32[48,128]{1,0:T(8,128)S(1)}, f32[48,128]{1,0:T(8,128)S(1)}, f32[48,128]{1,0:T(8,128)S(1)}) custom-call(s32[4]{0:T(128)S(1)} %pad_add_fusion.at, f32[48,384]{1,0:T(8,128)S(1)} %pad_maximum_fusion.refs_0_, f32[48,384]{1,0:T(8,128)S(1)} %collective-permute-done.10.refs_1_, ...), custom_call_target="tpu_custom_call" | custom-call | flops 1000000000 | bytes 2680320 | tf_op jit(solution)/shard_map/pallas_call | solution.py:53
  38.4 0.6 collective-permute-start.18
  39.1 1.1 %collective-permute-start.19 = (f32[48,128]{1,0:T(8,128)S(1)}, f32[48,128]{1,0:T(8,128)S(1)}, u32[]{:S(2)}, u32[]{:S(2)}) collective-permute-start(f32[48,128]{1,0:T(8,128)S(1)} %get-tuple-element.35), channel_id=1, source_target_pairs={{0,65},{1,64},{2,67},{3,66},{4,69},{5,68},{6,71},{7,70},{64,129},{... | collective-permute-start | bytes 73736 | tf_op jit(solution)/shard_map/ppermute | solution.py:365
  40.2 0.8 dynamic-slice.7
  40.9 1.4 %collective-permute-done.17 = f32[48,128]{1,0:T(8,128)S(1)} collective-permute-done((f32[48,128]{1,0:T(8,128)S(1)}, f32[48,128]{1,0:T(8,128)S(1)}, u32[]{:S(2)}, u32[]{:S(2)}) %collective-permute-start.17) | collective-permute-done | bytes 24608 | tf_op jit(solution)/shard_map/ppermute | solution.py:43
  42.3 1.2 %collective-permute-done.19 = f32[48,128]{1,0:T(8,128)S(1)} collective-permute-done((f32[48,128]{1,0:T(8,128)S(1)}, f32[48,128]{1,0:T(8,128)S(1)}, u32[]{:S(2)}, u32[]{:S(2)}) %collective-permute-start.19) | collective-permute-done | bytes 24608 | tf_op jit(solution)/shard_map/ppermute | solution.py:365
  43.6 1.5 %collective-permute-start.20 = (f32[96,128]{1,0:T(8,128)S(1)}, f32[96,128]{1,0:T(8,128)S(1)}, u32[]{:S(2)}, u32[]{:S(2)}) collective-permute-start(f32[96,128]{1,0:T(8,128)S(1)} %maximum_add_fusion.refs_0_), channel_id=1, source_target_pairs={{0,2},{1,7},{2,4},{3,1},{4,6},{5,3},{6,0},{7,5},{8,10},{9,15},{10,... | collective-permute-start | bytes 147464 | tf_op jit(solution)/shard_map/ppermute | solution.py:27
  45.1 1.3 %collective-permute-start.21 = (f32[96,128]{1,0:T(8,128)S(1)}, f32[96,128]{1,0:T(8,128)S(1)}, u32[]{:S(2)}, u32[]{:S(2)}) collective-permute-start(f32[96,128]{1,0:T(8,128)S(1)} %maximum_add_fusion.refs_0_), channel_id=1, source_target_pairs={{0,4},{1,5},{2,6},{3,7},{4,0},{5,1},{6,2},{7,3},{8,12},{9,13},{10,... | collective-permute-start | bytes 147464 | tf_op jit(solution)/shard_map/ppermute | solution.py:27
  46.6 2.9 %collective-permute-done.21.refs_2_ = f32[96,128]{1,0:T(8,128)S(1)} collective-permute-done((f32[96,128]{1,0:T(8,128)S(1)}, f32[96,128]{1,0:T(8,128)S(1)}, u32[]{:S(2)}, u32[]{:S(2)}) %collective-permute-start.21) | collective-permute-done | bytes 49184 | tf_op jit(solution)/shard_map/ppermute | solution.py:27
  49.5 1.5 %collective-permute-done.22.refs_3_ = f32[96,128]{1,0:T(8,128)S(1)} collective-permute-done((f32[96,128]{1,0:T(8,128)S(1)}, f32[96,128]{1,0:T(8,128)S(1)}, u32[]{:S(2)}, u32[]{:S(2)}) %collective-permute-start.22) | collective-permute-done | bytes 49184 | tf_op jit(solution)/shard_map/ppermute | solution.py:27
  51.0 0.7 shard_map.130
  51.7 4.4 %collective-permute-start.23 = (f32[384,128]{1,0:T(8,128)S(1)}, f32[384,128]{1,0:T(8,128)S(1)}, u32[]{:S(2)}, u32[]{:S(2)}) collective-permute-start(f32[384,128]{1,0:T(8,128)S(1)} %get-tuple-element.38.normed), channel_id=1, source_target_pairs={{32,0},{33,1},{42,2},{27,3},{52,4},{21,5},{30,6},{47,7},{40,8},{41... | collective-permute-start | bytes 589832 | tf_op jit(solution)/shard_map/ppermute | solution.py:393
  56.0 0.9 %collective-permute-start.24 = (f32[384,128]{1,0:T(8,128)S(1)}, f32[384,128]{1,0:T(8,128)S(1)}, u32[]{:S(2)}, u32[]{:S(2)}) collective-permute-start(f32[384,128]{1,0:T(8,128)S(1)} %get-tuple-element.38.normed), channel_id=1, source_target_pairs={{0,0},{1,1},{10,2},{59,3},{20,4},{53,5},{62,6},{15,7},{8,8},{9,9},... | collective-permute-start | bytes 589832 | tf_op jit(solution)/shard_map/ppermute | solution.py:393
  57.0 1.3 %convolution_multiply_fusion.w_score = f32[384,384]{1,0:T(8,128)S(1)} fusion(f32[384,384]{1,0:T(8,128)S(1)} %copy-done, f32[384,384]{1,0:T(8,128)S(1)} %copy-done.2), kind=kOutput, calls=%fused_computation.6 | convolution fusion | flops 679624704 | bytes 1769472 | tf_op jit(solution)/shard_map/dot_general | solution.py:311
  58.2 1.1 %shard_map.131 = (f32[128,384]{1,0:T(8,128)S(1)}, f32[32,384]{1,0:T(8,128)S(1)}) custom-call(s32[4]{0:T(128)S(1)} %pad_add_fusion.at, f32[384,128]{1,0:T(8,128)S(1)} %get-tuple-element.37.blocked, f32[384,128]{1,0:T(8,128)S(1)} %get-tuple-element.38.normed, f32[384,384]{1,0:T(8,128)S(1)} %convolution_multiply_fusion.w_score), custom_call_target="tpu_custom_call" | custom-call | flops 1000000 | bytes 1228800 | tf_op jit(solution)/shard_map/pallas_call | solution.py:53
  59.4 3.6 %collective-permute-done.23.keys_a = f32[384,128]{1,0:T(8,128)S(1)} collective-permute-done((f32[384,128]{1,0:T(8,128)S(1)}, f32[384,128]{1,0:T(8,128)S(1)}, u32[]{:S(2)}, u32[]{:S(2)}) %collective-permute-start.23) | collective-permute-done | bytes 196640 | tf_op jit(solution)/shard_map/ppermute | solution.py:393
  62.9 1.5 %shard_map.132 = (f32[32,512]{1,0:T(8,128)S(1)}, f32[32,512]{1,0:T(8,128)S(1)}, f32[32,512]{1,0:T(8,128)S(1)}, f32[32,512]{1,0:T(8,128)S(1)}) custom-call(s32[4]{0:T(128)S(1)} %pad_add_fusion.at, f32[128,384]{1,0:T(8,128)S(1)} %get-tuple-element.39.queries, f32[384,128]{1,0:T(8,128)S(1)} %collective-permute-done.23.keys_a, ...), custom_call_target="tpu_custom_call" | custom-call | flops 1000000 | bytes 851968 | tf_op jit(solution)/shard_map/pallas_call | solution.py:53
  64.4 5.5 %collective-permute-start.25 = (f32[32,512]{1,0:T(8,128)S(1)}, f32[32,512]{1,0:T(8,128)S(1)}, u32[]{:S(2)}, u32[]{:S(2)}) collective-permute-start(f32[32,512]{1,0:T(8,128)S(1)} %get-tuple-element.41), channel_id=1, source_target_pairs={{0,2},{1,7},{2,4},{3,1},{4,6},{5,3},{6,0},{7,5},{8,10},{9,15},{10,... | collective-permute-start | bytes 196616 | tf_op jit(solution)/shard_map/ppermute | solution.py:27
  69.9 0.7 collective-permute-start.27
  70.6 1.3 %fusion.4.w_mixed = f32[384,384]{1,0:T(8,128)S(1)} fusion(f32[384,384]{1,0:T(8,128)S(1)} %copy-done.3, f32[384,384]{1,0:T(8,128)S(1)} %copy-done.4), kind=kOutput, calls=%fused_computation.28 | convolution fusion | flops 679477248 | bytes 1769472 | tf_op jit(solution)/shard_map/dot_general | solution.py:318
  71.9 0.8 collective-permute-done.25.b
  72.7 2.0 %collective-permute-done.26.c = f32[32,512]{1,0:T(8,128)S(1)} collective-permute-done((f32[32,512]{1,0:T(8,128)S(1)}, f32[32,512]{1,0:T(8,128)S(1)}, u32[]{:S(2)}, u32[]{:S(2)}) %collective-permute-start.26) | collective-permute-done | bytes 65568 | tf_op jit(solution)/shard_map/ppermute | solution.py:27
  75.0 0.9 %shard_map.133 = (f32[4,4,384]{2,1,0:T(4,128)S(1)}, f32[4,4,384]{2,1,0:T(4,128)S(1)}) custom-call(s32[4]{0:T(128)S(1)} %pad_add_fusion.at, f32[32,512]{1,0:T(8,128)S(1)} %get-tuple-element.40.a, f32[32,512]{1,0:T(8,128)S(1)} %collective-permute-done.25.b, f32[32,512]{1,0:T(8,128)S(1)} %collective-permute-done.26.c, f32[32,512]{1,0:T(8,128)S(1)} %collective-permute-done.27.d, ...), custom_call_target="tpu_custom_call" | custom-call | flops 1000000 | bytes 951808 | tf_op jit(solution)/shard_map/pallas_call | solution.py:53
  75.9 0.5 collective-permute-start.28
  76.4 0.8 %collective-permute-done.28 = f32[4,4,384]{2,1,0:T(4,128)S(1)} collective-permute-done((f32[4,4,384]{2,1,0:T(4,128)S(1)}, f32[4,4,384]{2,1,0:T(4,128)S(1)}, u32[]{:S(2)}, u32[]{:S(2)}) %collective-permute-start.28) | collective-permute-done | bytes 24608 | tf_op jit(solution)/shard_map/ppermute | solution.py:21
  77.2 0.6 pad_maximum_fusion.1
  (62 shorter events, 2.6 us)
Async XLA Ops:
  0.0 56.9 %copy-start = (f32[384,384]{1,0:T(8,128)S(1)}, f32[384,384]{1,0:T(8,128)}, u32[]{:S(2)}) copy-start(f32[384,384]{1,0:T(8,128)} %param.21) | copy-start | bytes 1769476
  0.0 7.3 %slice-start = ((f32[48,3,3,3,384]{4,0,3,2,1:T(8,128)}), f32[48,2,3,3,384]{4,0,3,2,1:T(8,128)S(1)}, s32[]{:S(2)}) async-start(f32[48,3,3,3,384]{4,0,3,2,1:T(8,128)} %param.15), calls=%async_computation | async-start | bytes 2654208 | tf_op jit(solution)/shard_map/slice | solution.py:308
  0.0 7.5 %collective-permute-start = (f32[2,4,4,384]{3,2,1,0:T(4,128)}, f32[2,4,4,384]{3,2,1,0:T(4,128)S(1)}, u32[]{:S(2)}, u32[]{:S(2)}) collective-permute-start(f32[2,4,4,384]{3,2,1,0:T(4,128)} %refs_0_.1), channel_id=1, source_target_pairs={{0,2},{1,7},{2,4},{3,1},{4,6},{5,3},{6,0},{7,5},{8,10},{9,15},{10,... | collective-permute-start | bytes 147464 | tf_op jit(solution)/shard_map/ppermute | solution.py:27
  3.6 6.6 %collective-permute-start.1 = (f32[2,4,4,384]{3,2,1,0:T(4,128)}, f32[2,4,4,384]{3,2,1,0:T(4,128)S(1)}, u32[]{:S(2)}, u32[]{:S(2)}) collective-permute-start(f32[2,4,4,384]{3,2,1,0:T(4,128)} %refs_0_.1), channel_id=1, source_target_pairs={{0,4},{1,5},{2,6},{3,7},{4,0},{5,1},{6,2},{7,3},{8,12},{9,13},{10,... | collective-permute-start | bytes 147464 | tf_op jit(solution)/shard_map/ppermute | solution.py:27
  3.9 6.2 %collective-permute-start.2 = (f32[2,4,4,384]{3,2,1,0:T(4,128)}, f32[2,4,4,384]{3,2,1,0:T(4,128)S(1)}, u32[]{:S(2)}, u32[]{:S(2)}) collective-permute-start(f32[2,4,4,384]{3,2,1,0:T(4,128)} %refs_0_.1), channel_id=1, source_target_pairs={{0,6},{1,3},{2,0},{3,5},{4,2},{5,7},{6,4},{7,1},{8,14},{9,11},{10,... | collective-permute-start | bytes 147464 | tf_op jit(solution)/shard_map/ppermute | solution.py:27
  4.6 6.2 %collective-permute-start.3 = (f32[2,4,4,384]{3,2,1,0:T(4,128)}, f32[2,4,4,384]{3,2,1,0:T(4,128)S(1)}, u32[]{:S(2)}, u32[]{:S(2)}) collective-permute-start(f32[2,4,4,384]{3,2,1,0:T(4,128)} %refs_0_.1), channel_id=1, source_target_pairs={{0,1},{1,0},{2,3},{3,2},{4,5},{5,4},{6,7},{7,6},{8,9},{9,8},{10,11... | collective-permute-start | bytes 147464 | tf_op jit(solution)/shard_map/ppermute | solution.py:21
  7.3 3.4 %copy-start.5 = (f32[384]{0:T(512)S(1)}, f32[384]{0:T(512)}, u32[]{:S(2)}) copy-start(f32[384]{0:T(512)} %param.14) | copy-start | bytes 4612
  7.3 4.2 %copy-start.1 = (f32[2,4,4,384]{3,2,1,0:T(4,128)S(1)}, f32[2,4,4,384]{3,2,1,0:T(4,128)}, u32[]{:S(2)}) copy-start(f32[2,4,4,384]{3,2,1,0:T(4,128)} %refs_0_.1) | copy-start | bytes 147460
  7.6 3.5 %collective-permute-start.4 = (f32[2,4,4,384]{3,2,1,0:T(4,128)S(1)}, f32[2,4,4,384]{3,2,1,0:T(4,128)S(1)}, u32[]{:S(2)}, u32[]{:S(2)}) collective-permute-start(f32[2,4,4,384]{3,2,1,0:T(4,128)S(1)} %collective-permute-done.refs_1_), channel_id=1, source_target_pairs={{0,1},{1,0},{2,3},{3,2},{4,5},{5,4},{6,7},{7,6},{8,9},{9,8},{10,11... | collective-permute-start | bytes 147464 | tf_op jit(solution)/shard_map/ppermute | solution.py:21
  10.1 1.2 %collective-permute-start.5 = (f32[2,4,4,384]{3,2,1,0:T(4,128)S(1)}, f32[2,4,4,384]{3,2,1,0:T(4,128)S(1)}, u32[]{:S(2)}, u32[]{:S(2)}) collective-permute-start(f32[2,4,4,384]{3,2,1,0:T(4,128)S(1)} %collective-permute-done.1.refs_2_), channel_id=1, source_target_pairs={{0,1},{1,0},{2,3},{3,2},{4,5},{5,4},{6,7},{7,6},{8,9},{9,8},{10,11... | collective-permute-start | bytes 147464 | tf_op jit(solution)/shard_map/ppermute | solution.py:21
  10.1 1.4 %collective-permute-start.6 = (f32[2,4,4,384]{3,2,1,0:T(4,128)S(1)}, f32[2,4,4,384]{3,2,1,0:T(4,128)S(1)}, u32[]{:S(2)}, u32[]{:S(2)}) collective-permute-start(f32[2,4,4,384]{3,2,1,0:T(4,128)S(1)} %collective-permute-done.2.refs_3_), channel_id=1, source_target_pairs={{0,1},{1,0},{2,3},{3,2},{4,5},{5,4},{6,7},{7,6},{8,9},{9,8},{10,11... | collective-permute-start | bytes 147464 | tf_op jit(solution)/shard_map/ppermute | solution.py:21
  10.7 3.7 %slice-start.1 = ((f32[48,3,3,3,384]{4,0,3,2,1:T(8,128)}), f32[48,1,3,3,384]{4,0,3,2,1:T(8,128)S(1)}, s32[]{:S(2)}) async-start(f32[48,3,3,3,384]{4,0,3,2,1:T(8,128)} %param.15), calls=%async_computation.1 | async-start | bytes 1327104 | tf_op jit(solution)/shard_map/slice | solution.py:309
  13.5 4.5 %collective-permute-start.7 = (f32[48,384]{1,0:T(8,128)S(1)}, f32[48,384]{1,0:T(8,128)S(1)}, u32[]{:S(2)}, u32[]{:S(2)}) collective-permute-start(f32[48,384]{1,0:T(8,128)S(1)} %get-tuple-element.31), channel_id=1, source_target_pairs={{0,64},{64,128},{128,192},{192,0},{1,65},{65,129},{129,193},{193,1... | collective-permute-start | bytes 221192 | tf_op jit(solution)/shard_map/ppermute | solution.py:43
  18.0 6.5 %collective-permute-start.8 = (f32[48,128]{1,0:T(8,128)S(1)}, f32[48,128]{1,0:T(8,128)S(1)}, u32[]{:S(2)}, u32[]{:S(2)}) collective-permute-start(f32[48,128]{1,0:T(8,128)S(1)} %get-tuple-element.58), channel_id=1, source_target_pairs={{0,8},{8,16},{16,24},{24,32},{32,40},{40,48},{48,56},{56,0},{1,9},... | collective-permute-start | bytes 73736 | tf_op jit(solution)/shard_map/ppermute | solution.py:43
  19.3 5.2 %collective-permute-start.9 = (f32[48,128]{1,0:T(8,128)S(1)}, f32[48,128]{1,0:T(8,128)S(1)}, u32[]{:S(2)}, u32[]{:S(2)}) collective-permute-start(f32[48,128]{1,0:T(8,128)S(1)} %get-tuple-element.59), channel_id=1, source_target_pairs={{0,56},{8,0},{16,8},{24,16},{32,24},{40,32},{48,40},{56,48},{1,57}... | collective-permute-start | bytes 73736 | tf_op jit(solution)/shard_map/ppermute | solution.py:43
  24.6 9.7 %collective-permute-start.10 = (f32[48,384]{1,0:T(8,128)S(1)}, f32[48,384]{1,0:T(8,128)S(1)}, u32[]{:S(2)}, u32[]{:S(2)}) collective-permute-start(f32[48,384]{1,0:T(8,128)S(1)} %pad_maximum_fusion.refs_0_), channel_id=1, source_target_pairs={{0,2},{1,7},{2,4},{3,1},{4,6},{5,3},{6,0},{7,5},{8,10},{9,15},{10,... | collective-permute-start | bytes 221192 | tf_op jit(solution)/shard_map/ppermute | solution.py:27
  26.9 7.5 %collective-permute-start.11 = (f32[48,384]{1,0:T(8,128)S(1)}, f32[48,384]{1,0:T(8,128)S(1)}, u32[]{:S(2)}, u32[]{:S(2)}) collective-permute-start(f32[48,384]{1,0:T(8,128)S(1)} %pad_maximum_fusion.refs_0_), channel_id=1, source_target_pairs={{0,4},{1,5},{2,6},{3,7},{4,0},{5,1},{6,2},{7,3},{8,12},{9,13},{10,... | collective-permute-start | bytes 221192 | tf_op jit(solution)/shard_map/ppermute | solution.py:27
  27.2 7.6 %collective-permute-start.12 = (f32[48,384]{1,0:T(8,128)S(1)}, f32[48,384]{1,0:T(8,128)S(1)}, u32[]{:S(2)}, u32[]{:S(2)}) collective-permute-start(f32[48,384]{1,0:T(8,128)S(1)} %pad_maximum_fusion.refs_0_), channel_id=1, source_target_pairs={{0,6},{1,3},{2,0},{3,5},{4,2},{5,7},{6,4},{7,1},{8,14},{9,11},{10,... | collective-permute-start | bytes 221192 | tf_op jit(solution)/shard_map/ppermute | solution.py:27
  30.4 5.9 %collective-permute-start.13 = (f32[48,384]{1,0:T(8,128)S(1)}, f32[48,384]{1,0:T(8,128)S(1)}, u32[]{:S(2)}, u32[]{:S(2)}) collective-permute-start(f32[48,384]{1,0:T(8,128)S(1)} %pad_maximum_fusion.refs_0_), channel_id=1, source_target_pairs={{0,1},{1,0},{2,3},{3,2},{4,5},{5,4},{6,7},{7,6},{8,9},{9,8},{10,11... | collective-permute-start | bytes 221192 | tf_op jit(solution)/shard_map/ppermute | solution.py:21
  34.3 1.9 %collective-permute-start.14 = (f32[48,384]{1,0:T(8,128)S(1)}, f32[48,384]{1,0:T(8,128)S(1)}, u32[]{:S(2)}, u32[]{:S(2)}) collective-permute-start(f32[48,384]{1,0:T(8,128)S(1)} %collective-permute-done.10.refs_1_), channel_id=1, source_target_pairs={{0,1},{1,0},{2,3},{3,2},{4,5},{5,4},{6,7},{7,6},{8,9},{9,8},{10,11... | collective-permute-start | bytes 221192 | tf_op jit(solution)/shard_map/ppermute | solution.py:21
  34.4 1.8 %collective-permute-start.15 = (f32[48,384]{1,0:T(8,128)S(1)}, f32[48,384]{1,0:T(8,128)S(1)}, u32[]{:S(2)}, u32[]{:S(2)}) collective-permute-start(f32[48,384]{1,0:T(8,128)S(1)} %collective-permute-done.11.refs_2_), channel_id=1, source_target_pairs={{0,1},{1,0},{2,3},{3,2},{4,5},{5,4},{6,7},{7,6},{8,9},{9,8},{10,11... | collective-permute-start | bytes 221192 | tf_op jit(solution)/shard_map/ppermute | solution.py:21
  34.8 1.5 %collective-permute-start.16 = (f32[48,384]{1,0:T(8,128)S(1)}, f32[48,384]{1,0:T(8,128)S(1)}, u32[]{:S(2)}, u32[]{:S(2)}) collective-permute-start(f32[48,384]{1,0:T(8,128)S(1)} %collective-permute-done.12.refs_3_), channel_id=1, source_target_pairs={{0,1},{1,0},{2,3},{3,2},{4,5},{5,4},{6,7},{7,6},{8,9},{9,8},{10,11... | collective-permute-start | bytes 221192 | tf_op jit(solution)/shard_map/ppermute | solution.py:21
  35.4 0.7 copy-start.6
  36.2 10.2 %copy-start.7 = (f32[384]{0:T(512)S(1)}, f32[384]{0:T(512)}, u32[]{:S(2)}) copy-start(f32[384]{0:T(512)} %param.20) | copy-start | bytes 4612
  36.3 20.6 %copy-start.2 = (f32[384,384]{1,0:T(8,128)S(1)}, f32[384,384]{1,0:T(8,128)}, u32[]{:S(2)}) copy-start(f32[384,384]{1,0:T(8,128)} %param.22) | copy-start | bytes 1769476
  38.3 4.0 %collective-permute-start.17 = (f32[48,128]{1,0:T(8,128)S(1)}, f32[48,128]{1,0:T(8,128)S(1)}, u32[]{:S(2)}, u32[]{:S(2)}) collective-permute-start(f32[48,128]{1,0:T(8,128)S(1)} %get-tuple-element.33), channel_id=1, source_target_pairs={{0,64},{64,128},{128,192},{192,0},{1,65},{65,129},{129,193},{193,1... | collective-permute-start | bytes 73736 | tf_op jit(solution)/shard_map/ppermute | solution.py:43
  38.4 3.9 %collective-permute-start.18 = (f32[48,128]{1,0:T(8,128)S(1)}, f32[48,128]{1,0:T(8,128)S(1)}, u32[]{:S(2)}, u32[]{:S(2)}) collective-permute-start(f32[48,128]{1,0:T(8,128)S(1)} %get-tuple-element.34), channel_id=1, source_target_pairs={{0,1},{1,0},{2,3},{3,2},{4,5},{5,4},{6,7},{7,6},{8,9},{9,8},{10,11... | collective-permute-start | bytes 73736 | tf_op jit(solution)/shard_map/ppermute | solution.py:21
  39.1 4.5 %collective-permute-start.19 = (f32[48,128]{1,0:T(8,128)S(1)}, f32[48,128]{1,0:T(8,128)S(1)}, u32[]{:S(2)}, u32[]{:S(2)}) collective-permute-start(f32[48,128]{1,0:T(8,128)S(1)} %get-tuple-element.35), channel_id=1, source_target_pairs={{0,65},{1,64},{2,67},{3,66},{4,69},{5,68},{6,71},{7,70},{64,129},{... | collective-permute-start | bytes 73736 | tf_op jit(solution)/shard_map/ppermute | solution.py:365
  43.6 3.0 %collective-permute-start.20 = (f32[96,128]{1,0:T(8,128)S(1)}, f32[96,128]{1,0:T(8,128)S(1)}, u32[]{:S(2)}, u32[]{:S(2)}) collective-permute-start(f32[96,128]{1,0:T(8,128)S(1)} %maximum_add_fusion.refs_0_), channel_id=1, source_target_pairs={{0,2},{1,7},{2,4},{3,1},{4,6},{5,3},{6,0},{7,5},{8,10},{9,15},{10,... | collective-permute-start | bytes 147464 | tf_op jit(solution)/shard_map/ppermute | solution.py:27
  45.1 4.4 %collective-permute-start.21 = (f32[96,128]{1,0:T(8,128)S(1)}, f32[96,128]{1,0:T(8,128)S(1)}, u32[]{:S(2)}, u32[]{:S(2)}) collective-permute-start(f32[96,128]{1,0:T(8,128)S(1)} %maximum_add_fusion.refs_0_), channel_id=1, source_target_pairs={{0,4},{1,5},{2,6},{3,7},{4,0},{5,1},{6,2},{7,3},{8,12},{9,13},{10,... | collective-permute-start | bytes 147464 | tf_op jit(solution)/shard_map/ppermute | solution.py:27
  46.4 4.6 %collective-permute-start.22 = (f32[96,128]{1,0:T(8,128)S(1)}, f32[96,128]{1,0:T(8,128)S(1)}, u32[]{:S(2)}, u32[]{:S(2)}) collective-permute-start(f32[96,128]{1,0:T(8,128)S(1)} %maximum_add_fusion.refs_0_), channel_id=1, source_target_pairs={{0,6},{1,3},{2,0},{3,5},{4,2},{5,7},{6,4},{7,1},{8,14},{9,11},{10,... | collective-permute-start | bytes 147464 | tf_op jit(solution)/shard_map/ppermute | solution.py:27
  46.5 24.1 %copy-start.3 = (f32[384,384]{1,0:T(8,128)S(1)}, f32[384,384]{1,0:T(8,128)}, u32[]{:S(2)}) copy-start(f32[384,384]{1,0:T(8,128)} %param.23) | copy-start | bytes 1769476
  46.5 24.1 %copy-start.4 = (f32[384,384]{1,0:T(8,128)S(1)}, f32[384,384]{1,0:T(8,128)}, u32[]{:S(2)}) copy-start(f32[384,384]{1,0:T(8,128)} %param.24) | copy-start | bytes 1769476
  51.7 11.2 %collective-permute-start.23 = (f32[384,128]{1,0:T(8,128)S(1)}, f32[384,128]{1,0:T(8,128)S(1)}, u32[]{:S(2)}, u32[]{:S(2)}) collective-permute-start(f32[384,128]{1,0:T(8,128)S(1)} %get-tuple-element.38.normed), channel_id=1, source_target_pairs={{32,0},{33,1},{42,2},{27,3},{52,4},{21,5},{30,6},{47,7},{40,8},{41... | collective-permute-start | bytes 589832 | tf_op jit(solution)/shard_map/ppermute | solution.py:393
  56.0 6.9 %collective-permute-start.24 = (f32[384,128]{1,0:T(8,128)S(1)}, f32[384,128]{1,0:T(8,128)S(1)}, u32[]{:S(2)}, u32[]{:S(2)}) collective-permute-start(f32[384,128]{1,0:T(8,128)S(1)} %get-tuple-element.38.normed), channel_id=1, source_target_pairs={{0,0},{1,1},{10,2},{59,3},{20,4},{53,5},{62,6},{15,7},{8,8},{9,9},... | collective-permute-start | bytes 589832 | tf_op jit(solution)/shard_map/ppermute | solution.py:393
  58.2 13.7 %copy-start.8 = (f32[384]{0:T(512)S(1)}, f32[384]{0:T(512)}, u32[]{:S(2)}) copy-start(f32[384]{0:T(512)} %param.25) | copy-start | bytes 4612
  64.4 8.3 %collective-permute-start.25 = (f32[32,512]{1,0:T(8,128)S(1)}, f32[32,512]{1,0:T(8,128)S(1)}, u32[]{:S(2)}, u32[]{:S(2)}) collective-permute-start(f32[32,512]{1,0:T(8,128)S(1)} %get-tuple-element.41), channel_id=1, source_target_pairs={{0,2},{1,7},{2,4},{3,1},{4,6},{5,3},{6,0},{7,5},{8,10},{9,15},{10,... | collective-permute-start | bytes 196616 | tf_op jit(solution)/shard_map/ppermute | solution.py:27
  69.9 4.7 %collective-permute-start.26 = (f32[32,512]{1,0:T(8,128)S(1)}, f32[32,512]{1,0:T(8,128)S(1)}, u32[]{:S(2)}, u32[]{:S(2)}) collective-permute-start(f32[32,512]{1,0:T(8,128)S(1)} %get-tuple-element.42), channel_id=1, source_target_pairs={{0,4},{1,5},{2,6},{3,7},{4,0},{5,1},{6,2},{7,3},{8,12},{9,13},{10,... | collective-permute-start | bytes 196616 | tf_op jit(solution)/shard_map/ppermute | solution.py:27
  69.9 5.0 %collective-permute-start.27 = (f32[32,512]{1,0:T(8,128)S(1)}, f32[32,512]{1,0:T(8,128)S(1)}, u32[]{:S(2)}, u32[]{:S(2)}) collective-permute-start(f32[32,512]{1,0:T(8,128)S(1)} %get-tuple-element.43), channel_id=1, source_target_pairs={{0,6},{1,3},{2,0},{3,5},{4,2},{5,7},{6,4},{7,1},{8,14},{9,11},{10,... | collective-permute-start | bytes 196616 | tf_op jit(solution)/shard_map/ppermute | solution.py:27
  75.9 1.3 %collective-permute-start.28 = (f32[4,4,384]{2,1,0:T(4,128)S(1)}, f32[4,4,384]{2,1,0:T(4,128)S(1)}, u32[]{:S(2)}, u32[]{:S(2)}) collective-permute-start(f32[4,4,384]{2,1,0:T(4,128)S(1)} %get-tuple-element.46), channel_id=1, source_target_pairs={{0,1},{1,0},{2,3},{3,2},{4,5},{5,4},{6,7},{7,6},{8,9},{9,8},{10,11... | collective-permute-start | bytes 73736 | tf_op jit(solution)/shard_map/ppermute | solution.py:21
